TPU v7x, 32 devices: a whole 2x2x4 slice. The times are simulated.
32 devices in a mesh: shard: 4 (over x, core), ctx: 4 (over z), tp: 2 (over y).
Axes of the slice: x: 2, y: 2, z: 4, core: 2. Of those that a mesh axis runs over, the one named last changes fastest.
Arguments:
- tokens: bfloat16 [18432, 768], P(('shard', 'ctx')), may hold values from -6 to 6
- cotangent: bfloat16 [18432, 768], P(('shard', 'ctx')), may hold values from -6 to 6
- seq_lengths: int32 [4, 12], P('shard'), may hold values from 1 to 512, 4608 in all within a row
- dealing: int32 [4, 4608], P('shard'), may hold values from 0 to 4607, each once within a row
- query_weight: bfloat16 [768, 768], P('shard', 'tp'), may hold values from -0.21875 to 0.21875
- query_bias: bfloat16 [768], P('tp'), may hold values from -1.5 to 1.5
- key_weight: bfloat16 [768, 768], P('shard', 'tp'), may hold values from -0.21875 to 0.21875
- value_weight: bfloat16 [768, 768], P('shard', 'tp'), may hold values from -0.21875 to 0.21875
- value_bias: bfloat16 [768], P('tp'), may hold values from -0.14941406 to 0.14941406
- output_weight: bfloat16 [768, 768], P('tp', 'shard'), may hold values from -3.5 to 3.5
- output_bias: bfloat16 [768], replicated, may hold values from -2.5 to 2.5
- first_gain: bfloat16 [768], replicated, may hold values from 0.25 to 1.75
- first_shift: bfloat16 [768], replicated, may hold values from -1.5 to 1.5
- up_weight: bfloat16 [768, 3072], P('shard', 'tp'), may hold values from -0.21875 to 0.21875
- up_bias: bfloat16 [3072], P('tp'), may hold values from -2.5 to 2.5
- down_weight: bfloat16 [3072, 768], P('tp', 'shard'), may hold values from -0.109375 to 0.109375
- down_bias: bfloat16 [768], replicated, may hold values from -1.5 to 1.5
- second_gain: bfloat16 [768], replicated, may hold values from 0.25 to 1.75
- second_shift: bfloat16 [768], replicated, may hold values from -1.5 to 1.5
Outputs:
- layer_out: bfloat16 [18432, 768], P(('shard', 'ctx'))
- tokens_grad: bfloat16 [18432, 768], P(('shard', 'ctx'))
- query_weight_grad: float32 [768, 768], P('shard', 'tp')
- query_bias_grad: float32 [768], P('tp')
- key_weight_grad: float32 [768, 768], P('shard', 'tp')
- value_weight_grad: float32 [768, 768], P('shard', 'tp')
- value_bias_grad: float32 [768], P('tp')
- output_weight_grad: float32 [768, 768], P('tp', 'shard')
- output_bias_grad: float32 [768], replicated
- first_gain_grad: float32 [768], replicated
- first_shift_grad: float32 [768], replicated
- up_weight_grad: float32 [768, 3072], P('shard', 'tp')
- up_bias_grad: float32 [3072], P('tp')
- down_weight_grad: float32 [3072, 768], P('tp', 'shard')
- down_bias_grad: float32 [768], replicated
- second_gain_grad: float32 [768], replicated
- second_shift_grad: float32 [768], replicated
Inputs may be any that keep to these rules, and one draw needn't show every extreme that they name: `seq_lengths`: each row holds 12 lengths that sum to 4608; the longest is exactly 512. `dealing`: each row is a permutation of the 4608 positions of its group.
All inputs are finite; a program needn't handle non-finite values.
Results may differ from a plain program's by a relative error of at most 0.02.
Values may be sent and summed in bfloat16 or wider, within the bound.
A program may use at most 128 MiB of HBM per device.

v0:
```python
import jax
import jax.numpy as jnp
from jax import lax
from jax.sharding import PartitionSpec as P

HEAD = 64


HALF_ROOT = 0.7071067811865476
DENSITY = 0.3989422804014327
NEG_FILL = -1000000000.0


def matmul(former, latter):
    return jnp.dot(former, latter, preferred_element_type=jnp.float32)


def matmul_first(former, latter):
    return lax.dot_general(
        former, latter, (((0,), (0,)), ((), ())), preferred_element_type=jnp.float32
    )


def matmul_second(former, latter):
    return lax.dot_general(
        former, latter, (((1,), (1,)), ((), ())), preferred_element_type=jnp.float32
    )


def norm_forward(values, norm_gain, norm_shift):
    centre = values - jnp.mean(values, axis=1, keepdims=True)
    spread = jnp.mean(centre * centre, axis=1, keepdims=True)
    inverse = lax.rsqrt(spread + 1e-06)
    normed = centre * inverse
    return (norm_gain * normed + norm_shift, normed, inverse)


def norm_backward(gradient, normed, inverse, norm_gain):
    scaled = gradient * norm_gain
    bracket = (
        scaled
        - jnp.mean(scaled, axis=1, keepdims=True)
        - normed * jnp.mean(scaled * normed, axis=1, keepdims=True)
    )
    return inverse * bracket


def masked_scores(query_block, key_head, seg_block, key_seg):
    scores = 0.125 * matmul_second(query_block, key_head)
    return jnp.where(seg_block[:, None] == key_seg[None, :], scores, NEG_FILL)


def split_heads(matrix):
    return matrix.reshape(matrix.shape[0], -1, HEAD).transpose(1, 0, 2)


def merge_heads(stacked):
    return stacked.transpose(1, 0, 2).reshape(stacked.shape[1], -1)


def head_forward(query_head, key_head, value_head, query_seg, key_seg, block_rows):
    block_count = query_head.shape[0] // block_rows

    def one_block(packed):
        query_block, seg_block = packed
        scores = masked_scores(query_block, key_head, seg_block, key_seg)
        row_max = jnp.max(scores, axis=1, keepdims=True)
        raised = jnp.exp(scores - row_max)
        row_sum = jnp.sum(raised, axis=1, keepdims=True)
        weights = (raised / row_sum).astype(jnp.bfloat16)
        return (matmul(weights, value_head), (row_max + jnp.log(row_sum))[:, 0])

    blocks = (
        query_head.reshape(block_count, block_rows, -1),
        query_seg.reshape(block_count, block_rows),
    )
    outputs, logsum = lax.map(one_block, blocks)
    return (outputs.reshape(query_head.shape[0], -1), logsum.reshape(-1))


def head_backward(
    query_head, key_head, value_head, grad_head, logsum, query_seg, key_seg, block_rows
):
    block_count = query_head.shape[0] // block_rows

    def one_block(running, packed):
        query_block, grad_block, logsum_block, seg_block = packed
        scores = masked_scores(query_block, key_head, seg_block, key_seg)
        probs = jnp.exp(scores - logsum_block[:, None])
        grad_probs = matmul_second(grad_block, value_head)
        grad_scores = (
            probs * (grad_probs - jnp.sum(grad_probs * probs, axis=1, keepdims=True))
        ).astype(jnp.bfloat16)
        key_acc = running[0] + 0.125 * matmul_first(grad_scores, query_block)
        value_acc = running[1] + matmul_first(probs.astype(jnp.bfloat16), grad_block)
        return ((key_acc, value_acc), 0.125 * matmul(grad_scores, key_head))

    initial = (jnp.zeros(key_head.shape, jnp.float32), jnp.zeros(value_head.shape, jnp.float32))
    blocks = (
        query_head.reshape(block_count, block_rows, -1),
        grad_head.reshape(block_count, block_rows, -1),
        logsum.reshape(block_count, block_rows),
        query_seg.reshape(block_count, block_rows),
    )
    sums, query_grad = lax.scan(one_block, initial, blocks)
    return (query_grad.reshape(query_head.shape[0], -1), sums[0], sums[1])


def per_device(
    tokens,
    cotangent,
    seq_lengths,
    dealing,
    query_weight,
    query_bias,
    key_weight,
    value_weight,
    value_bias,
    output_weight,
    output_bias,
    first_gain,
    first_shift,
    up_weight,
    up_bias,
    down_weight,
    down_bias,
    second_gain,
    second_shift,
):
    rows_mine = tokens.shape[0]
    group_rows = rows_mine * lax.axis_size("ctx")
    ctx_place = lax.axis_index("ctx")
    query_bias = query_bias.astype(jnp.float32)
    value_bias = value_bias.astype(jnp.float32)
    output_bias = output_bias.astype(jnp.float32)
    first_gain = first_gain.astype(jnp.float32)
    first_shift = first_shift.astype(jnp.float32)
    up_bias = up_bias.astype(jnp.float32)
    down_bias = down_bias.astype(jnp.float32)
    second_gain = second_gain.astype(jnp.float32)
    second_shift = second_shift.astype(jnp.float32)
    all_tokens = lax.all_gather(tokens, "ctx", axis=0, tiled=True)
    dealt_order = dealing[0]
    own_slots = lax.dynamic_slice_in_dim(dealt_order, ctx_place * rows_mine, rows_mine)
    inputs = jnp.take(all_tokens, own_slots, axis=0)
    positions = jnp.arange(group_rows, dtype=jnp.int32)
    seq_ends = jnp.cumsum(seq_lengths[0])
    segment = jnp.sum((positions[:, None] >= seq_ends[None, :-1]).astype(jnp.int32), axis=1)
    key_seg = jnp.take(segment, dealt_order)
    query_seg = lax.dynamic_slice_in_dim(key_seg, ctx_place * rows_mine, rows_mine)
    wide_query, wide_key, wide_value, wide_up = (
        lax.all_gather(query_weight, "shard", axis=0, tiled=True),
        lax.all_gather(key_weight, "shard", axis=0, tiled=True),
        lax.all_gather(value_weight, "shard", axis=0, tiled=True),
        lax.all_gather(up_weight, "shard", axis=0, tiled=True),
    )
    wide_output, wide_down = (
        lax.all_gather(output_weight, "shard", axis=1, tiled=True),
        lax.all_gather(down_weight, "shard", axis=1, tiled=True),
    )
    queries = (matmul(inputs, wide_query) + query_bias).astype(jnp.bfloat16)
    key_rows = matmul(inputs, wide_key).astype(jnp.bfloat16)
    value_rows = (matmul(inputs, wide_value) + value_bias).astype(jnp.bfloat16)
    all_keys, all_values = (
        lax.all_gather(key_rows, "ctx", axis=0, tiled=True),
        lax.all_gather(value_rows, "ctx", axis=0, tiled=True),
    )
    block_rows = rows_mine
    for halving in range(8):
        if block_rows > 768 and block_rows % 2 == 0:
            block_rows = block_rows // 2
    query_heads = split_heads(queries)
    key_heads = split_heads(all_keys)
    value_heads = split_heads(all_values)

    def forward_head(packed):
        return head_forward(packed[0], packed[1], packed[2], query_seg, key_seg, block_rows)

    head_out, logsum = lax.map(forward_head, (query_heads, key_heads, value_heads))
    attended = merge_heads(head_out).astype(jnp.bfloat16)
    attn_total = lax.psum(matmul(attended, wide_output), "tp")
    hidden_one, normed_one, inverse_one = norm_forward(
        inputs.astype(jnp.float32) + attn_total + output_bias, first_gain, first_shift
    )
    hidden_low = hidden_one.astype(jnp.bfloat16)
    pre_act = matmul(hidden_low, wide_up) + up_bias
    erf_part = 0.5 * (1.0 + jax.scipy.special.erf(pre_act * HALF_ROOT))
    act_low = (pre_act * erf_part).astype(jnp.bfloat16)
    ffn_total = lax.psum(matmul(act_low, wide_down).astype(jnp.bfloat16), "tp").astype(jnp.float32)
    layer_value, normed_two, inverse_two = norm_forward(
        hidden_one + ffn_total + down_bias, second_gain, second_shift
    )
    layer_out = layer_value.astype(jnp.bfloat16)
    grad_out = cotangent.astype(jnp.float32)
    second_shift_grad = jnp.sum(grad_out, axis=0)
    second_gain_grad = jnp.sum(grad_out * normed_two, axis=0)
    grad_second = norm_backward(grad_out, normed_two, inverse_two, second_gain)
    down_bias_grad = jnp.sum(grad_second, axis=0)
    second_low = grad_second.astype(jnp.bfloat16)
    down_grad_turned = matmul_first(second_low, act_low)
    grad_act = matmul_second(second_low, wide_down)
    slope = erf_part + pre_act * DENSITY * jnp.exp(-0.5 * pre_act * pre_act)
    grad_pre = grad_act * slope
    up_bias_grad = jnp.sum(grad_pre, axis=0)
    pre_low = grad_pre.astype(jnp.bfloat16)
    up_grad_full = matmul_first(hidden_low, pre_low)
    back_hidden = lax.psum(matmul_second(pre_low, wide_up), "tp")
    grad_hidden = grad_second + back_hidden
    first_shift_grad = jnp.sum(grad_hidden, axis=0)
    first_gain_grad = jnp.sum(grad_hidden * normed_one, axis=0)
    grad_first = norm_backward(grad_hidden, normed_one, inverse_one, first_gain)
    output_bias_grad = jnp.sum(grad_first, axis=0)
    first_low = grad_first.astype(jnp.bfloat16)
    output_grad_turned = matmul_first(first_low, attended)
    attended_grad = matmul_second(first_low, wide_output).astype(jnp.bfloat16)

    def backward_head(packed):
        return head_backward(
            packed[0], packed[1], packed[2], packed[3], packed[4], query_seg, key_seg, block_rows
        )

    query_parts, key_parts, value_parts = lax.map(
        backward_head, (query_heads, key_heads, value_heads, split_heads(attended_grad), logsum)
    )
    query_grad = merge_heads(query_parts)
    key_sum, value_sum = (
        lax.psum_scatter(
            merge_heads(key_parts).astype(jnp.bfloat16), "ctx", scatter_dimension=0, tiled=True
        ).astype(jnp.float32),
        lax.psum_scatter(
            merge_heads(value_parts).astype(jnp.bfloat16), "ctx", scatter_dimension=0, tiled=True
        ).astype(jnp.float32),
    )
    query_bias_grad = jnp.sum(query_grad, axis=0)
    value_bias_grad = jnp.sum(value_sum, axis=0)
    query_low = query_grad.astype(jnp.bfloat16)
    key_low = key_sum.astype(jnp.bfloat16)
    value_low = value_sum.astype(jnp.bfloat16)
    input_part = (
        matmul_second(query_low, wide_query)
        + matmul_second(key_low, wide_key)
        + matmul_second(value_low, wide_value)
    )
    input_total = lax.psum(input_part.astype(jnp.bfloat16), "tp").astype(jnp.float32)
    tokens_grad = (grad_first + input_total).astype(jnp.bfloat16)
    query_grad_full = matmul_first(inputs, query_low)
    key_grad_full = matmul_first(inputs, key_low)
    value_grad_full = matmul_first(inputs, value_low)
    small = lax.psum(
        (
            query_bias_grad,
            value_bias_grad,
            output_bias_grad,
            first_gain_grad,
            first_shift_grad,
            up_bias_grad,
            down_bias_grad,
            second_gain_grad,
            second_shift_grad,
        ),
        ("shard", "ctx"),
    )
    shard_parts = (
        lax.psum_scatter(
            query_grad_full.astype(jnp.bfloat16), "shard", scatter_dimension=0, tiled=True
        ).astype(jnp.float32),
        lax.psum_scatter(
            key_grad_full.astype(jnp.bfloat16), "shard", scatter_dimension=0, tiled=True
        ).astype(jnp.float32),
        lax.psum_scatter(
            value_grad_full.astype(jnp.bfloat16), "shard", scatter_dimension=0, tiled=True
        ).astype(jnp.float32),
        lax.psum_scatter(
            output_grad_turned.astype(jnp.bfloat16), "shard", scatter_dimension=0, tiled=True
        ).astype(jnp.float32),
        lax.psum_scatter(
            up_grad_full.astype(jnp.bfloat16), "shard", scatter_dimension=0, tiled=True
        ).astype(jnp.float32),
        lax.psum_scatter(
            down_grad_turned.astype(jnp.bfloat16), "shard", scatter_dimension=0, tiled=True
        ).astype(jnp.float32),
    )
    owned = (
        lax.psum(shard_parts[0].astype(jnp.bfloat16), "ctx").astype(jnp.float32),
        lax.psum(shard_parts[1].astype(jnp.bfloat16), "ctx").astype(jnp.float32),
        lax.psum(shard_parts[2].astype(jnp.bfloat16), "ctx").astype(jnp.float32),
        lax.psum(shard_parts[3].astype(jnp.bfloat16), "ctx").astype(jnp.float32),
        lax.psum(shard_parts[4].astype(jnp.bfloat16), "ctx").astype(jnp.float32),
        lax.psum(shard_parts[5].astype(jnp.bfloat16), "ctx").astype(jnp.float32),
    )
    return (
        layer_out,
        tokens_grad,
        owned[0],
        small[0],
        owned[1],
        owned[2],
        small[1],
        owned[3].T,
        small[2],
        small[3],
        small[4],
        owned[4],
        small[5],
        owned[5].T,
        small[6],
        small[7],
        small[8],
    )


def solution(mesh):
    return jax.shard_map(
        per_device,
        mesh=mesh,
        in_specs=(
            P(("shard", "ctx"), None),
            P(("shard", "ctx"), None),
            P("shard", None),
            P("shard", None),
            P("shard", "tp"),
            P("tp"),
            P("shard", "tp"),
            P("shard", "tp"),
            P("tp"),
            P("tp", "shard"),
            P(),
            P(),
            P(),
            P("shard", "tp"),
            P("tp"),
            P("tp", "shard"),
            P(),
            P(),
            P(),
        ),
        out_specs=(
            P(("shard", "ctx"), None),
            P(("shard", "ctx"), None),
            P("shard", "tp"),
            P("tp"),
            P("shard", "tp"),
            P("shard", "tp"),
            P("tp"),
            P("tp", "shard"),
            P(),
            P(),
            P(),
            P("shard", "tp"),
            P("tp"),
            P("tp", "shard"),
            P(),
            P(),
            P(),
        ),
        check_vma=False,
    )
```

profile of v0, /device:TPU:0, one launch (start us, length us, event | category | flops | bytes accessed | tf_op | source)
XLA Modules:
  0.0 1389.6 jit_solution(315508970438273504)
XLA Ops:
  19.5 121.9 %all-gather.6.cloned.1.call-done = bf16[4608,768]{1,0:T(8,128)(2,1)} async-done(((bf16[1152,768]{1,0:T(8,128)(2,1)}), bf16[4608,768]{1,0:T(8,128)(2,1)}) %all-gather.6.cloned.1.call-update) | async-done | bytes 7077904 | tf_op jit(solution)/shard_map/all_gather | solution.py:142
  164.0 24.1 %gather_fusion.1 = s32[4608]{0:T(1024)S(1)} fusion(s32[4608]{0:T(1024)S(1)} %convert_reduce_fusion.2, s32[5120]{0:T(1024)S(1)} %pad_clamp_fusion), kind=kCustom, calls=%fused_computation.1 | custom fusion | bytes 55296 | tf_op jit(solution)/shard_map/jit(_take)/gather | solution.py:149
  231.1 61.0 %all-gather.10.cloned.1.call-done = bf16[4608,384]{1,0:T(8,128)(2,1)} async-done(((bf16[1152,384]{1,0:T(8,128)(2,1)}), bf16[4608,384]{1,0:T(8,128)(2,1)}) %all-gather.10.cloned.1.call-update) | async-done | bytes 3538960 | tf_op jit(solution)/shard_map/all_gather | solution.py:166
  302.0 102.7 %while.64 = (s32[]{:T(128)}, bf16[6,1152,64]{1,2,0:T(8,128)(2,1)}, f32[6,1152]{1,0:T(8,128)}, bf16[6,1152,64]{2,1,0:T(8,128)(2,1)}, s32[1152]{0:T(1024)}, /*inde...) while((s32[]{:T(128)}, bf16[6,1152,64]{1,2,0:T(8,128)(2,1)}, ...), condition=%wide.wide.region_7.8_spmd.clone, body=%wide.wide.region_2.0_spmd.sunk.clone | while | flops 703364544 | bytes 38196596 | solution.py:179
  412.0 89.9 %all-reduce.8.cloned.1.call-done = f32[1152,768]{1,0:T(8,128)} async-done(((f32[1152,768]{1,0:T(8,128)}), f32[1152,768]{1,0:T(8,128)}) %all-reduce.8.cloned.1.call-update) | async-done | bytes 3538960 | tf_op jit(solution)/shard_map/psum | solution.py:181
  525.2 52.0 %all-reduce.10.cloned.1.call-done = bf16[1152,768]{1,0:T(8,128)(2,1)} async-done(((bf16[1152,768]{1,0:T(8,128)(2,1)}), bf16[1152,768]{1,0:T(8,128)(2,1)}) %all-reduce.10.cloned.1.call-update) | async-done | bytes 1769488 | tf_op jit(solution)/shard_map/psum | solution.py:189
  600.2 93.7 %all-reduce.12.cloned.1.call-done = f32[1152,768]{1,0:T(8,128)} async-done(((f32[1152,768]{1,0:T(8,128)}), f32[1152,768]{1,0:T(8,128)}) %all-reduce.12.cloned.1.call-update) | async-done | bytes 3538960 | tf_op jit(solution)/shard_map/psum | solution.py:207
  705.6 215.5 %while.66 = (s32[]{:T(128)}, f32[6,1152,64]{1,2,0:T(8,128)}, bf16[6,4608,64]{1,2,0:T(8,128)(2,1)}, bf16[6,4608,64]{1,2,0:T(8,128)(2,1)}, bf16[6,1152,64]{2,1,0:T...) while((s32[]{:T(128)}, f32[6,1152,64]{1,2,0:T(8,128)}, ...), condition=%wide.wide.region_23.24_spmd.clone, body=%wide.wide.region_19.23_spmd.sunk.clone | while | flops 1726746112 | bytes 104030792 | solution.py:222
  713.6 24.6 %while.65 = (s32[]{:T(128)}, f32[4608,64]{0,1:T(8,128)S(1)}, f32[4608,64]{0,1:T(8,128)S(1)}, f32[2,576,64]{1,2,0:T(8,128)}, s32[2,576]{1,0:T(2,128)S(1)}, /*inde...) while((s32[]{:T(128)}, f32[4608,64]{0,1:T(8,128)S(1)}, ...), condition=%wide.region_22.22_spmd.clone, body=%wide.region_20.21_spmd.clone.sunk | while | flops 1726746112 | bytes 94574904 | solution.py:105
  749.5 24.6 %while.65 = (s32[]{:T(128)}, f32[4608,64]{0,1:T(8,128)S(1)}, f32[4608,64]{0,1:T(8,128)S(1)}, f32[2,576,64]{1,2,0:T(8,128)}, s32[2,576]{1,0:T(2,128)S(1)}, /*inde...) while((s32[]{:T(128)}, f32[4608,64]{0,1:T(8,128)S(1)}, ...), condition=%wide.region_22.22_spmd.clone, body=%wide.region_20.21_spmd.clone.sunk | while | flops 1726746112 | bytes 94574904 | solution.py:105
  785.4 24.6 %while.65 = (s32[]{:T(128)}, f32[4608,64]{0,1:T(8,128)S(1)}, f32[4608,64]{0,1:T(8,128)S(1)}, f32[2,576,64]{1,2,0:T(8,128)}, s32[2,576]{1,0:T(2,128)S(1)}, /*inde...) while((s32[]{:T(128)}, f32[4608,64]{0,1:T(8,128)S(1)}, ...), condition=%wide.region_22.22_spmd.clone, body=%wide.region_20.21_spmd.clone.sunk | while | flops 1726746112 | bytes 94574904 | solution.py:105
  821.3 24.6 %while.65 = (s32[]{:T(128)}, f32[4608,64]{0,1:T(8,128)S(1)}, f32[4608,64]{0,1:T(8,128)S(1)}, f32[2,576,64]{1,2,0:T(8,128)}, s32[2,576]{1,0:T(2,128)S(1)}, /*inde...) while((s32[]{:T(128)}, f32[4608,64]{0,1:T(8,128)S(1)}, ...), condition=%wide.region_22.22_spmd.clone, body=%wide.region_20.21_spmd.clone.sunk | while | flops 1726746112 | bytes 94574904 | solution.py:105
  857.2 24.6 %while.65 = (s32[]{:T(128)}, f32[4608,64]{0,1:T(8,128)S(1)}, f32[4608,64]{0,1:T(8,128)S(1)}, f32[2,576,64]{1,2,0:T(8,128)}, s32[2,576]{1,0:T(2,128)S(1)}, /*inde...) while((s32[]{:T(128)}, f32[4608,64]{0,1:T(8,128)S(1)}, ...), condition=%wide.region_22.22_spmd.clone, body=%wide.region_20.21_spmd.clone.sunk | while | flops 1726746112 | bytes 94574904 | solution.py:105
  893.2 24.6 %while.65 = (s32[]{:T(128)}, f32[4608,64]{0,1:T(8,128)S(1)}, f32[4608,64]{0,1:T(8,128)S(1)}, f32[2,576,64]{1,2,0:T(8,128)}, s32[2,576]{1,0:T(2,128)S(1)}, /*inde...) while((s32[]{:T(128)}, f32[4608,64]{0,1:T(8,128)S(1)}, ...), condition=%wide.region_22.22_spmd.clone, body=%wide.region_20.21_spmd.clone.sunk | while | flops 1726746112 | bytes 94574904 | solution.py:105
  956.3 37.0 %reduce-scatter.25.cloned.1.call-done = bf16[1152,384]{1,0:T(8,128)(2,1)} async-done(((bf16[4608,384]{1,0:T(8,128)(2,1)}), bf16[1152,384]{1,0:T(8,128)(2,1)}) %reduce-scatter.25.cloned.1.call-update) | async-done | bytes 884752
  996.7 65.7 %reduce-scatter.27.cloned.1.call-done = bf16[1152,384]{1,0:T(8,128)(2,1)} async-done(((bf16[4608,384]{1,0:T(8,128)(2,1)}), bf16[1152,384]{1,0:T(8,128)(2,1)}) %reduce-scatter.27.cloned.1.call-update) | async-done | bytes 884752
  1071.0 27.6 %reduce-scatter.23.cloned.1.call-done = bf16[192,1536]{1,0:T(8,128)(2,1)} async-done(((bf16[768,1536]{1,0:T(8,128)(2,1)}), bf16[192,1536]{1,0:T(8,128)(2,1)}) %reduce-scatter.23.cloned.1.call-update) | async-done | bytes 589840 | tf_op jit(solution)/shard_map/reduce_scatter | solution.py:279
  1098.5 35.5 %reduce-scatter.21.cloned.1.call-done = bf16[192,1536]{1,0:T(8,128)(2,1)} async-done(((bf16[768,1536]{1,0:T(8,128)(2,1)}), bf16[192,1536]{1,0:T(8,128)(2,1)}) %reduce-scatter.21.cloned.1.call-update) | async-done | bytes 589840 | tf_op jit(solution)/shard_map/reduce_scatter | solution.py:276
  1134.0 24.8 %reduce-scatter.19.cloned.1.call-done = bf16[192,384]{1,0:T(8,128)(2,1)} async-done(((bf16[768,384]{1,0:T(8,128)(2,1)}), bf16[192,384]{1,0:T(8,128)(2,1)}) %reduce-scatter.19.cloned.1.call-update) | async-done | bytes 147472 | tf_op jit(solution)/shard_map/reduce_scatter | solution.py:273
  1158.8 25.2 %reduce-scatter.13.cloned.1.call-done = bf16[192,384]{1,0:T(8,128)(2,1)} async-done(((bf16[768,384]{1,0:T(8,128)(2,1)}), bf16[192,384]{1,0:T(8,128)(2,1)}) %reduce-scatter.13.cloned.1.call-update) | async-done | bytes 147472 | tf_op jit(solution)/shard_map/reduce_scatter | solution.py:264
  1184.0 24.8 %reduce-scatter.15.cloned.1.call-done = bf16[192,384]{1,0:T(8,128)(2,1)} async-done(((bf16[768,384]{1,0:T(8,128)(2,1)}), bf16[192,384]{1,0:T(8,128)(2,1)}) %reduce-scatter.15.cloned.1.call-update) | async-done | bytes 147472 | tf_op jit(solution)/shard_map/reduce_scatter | solution.py:267
  1208.8 24.6 %reduce-scatter.17.cloned.1.call-done = bf16[192,384]{1,0:T(8,128)(2,1)} async-done(((bf16[768,384]{1,0:T(8,128)(2,1)}), bf16[192,384]{1,0:T(8,128)(2,1)}) %reduce-scatter.17.cloned.1.call-update) | async-done | bytes 147472 | tf_op jit(solution)/shard_map/reduce_scatter | solution.py:270
  1241.1 61.2 %all-reduce = (f32[384]{0:T(512)}, f32[384]{0:T(512)}, f32[768]{0:T(1024)}, f32[768]{0:T(1024)}, f32[768]{0:T(1024)}, /*index=5*/f32[1536]{0:T(1024)}, f32[768]{0:T(1024)}, f32[768]{0:T(1024)}, f32[768]{0:T(1024)}) all-reduce(f32[384]{0:T(512)} %reduce_sum.192, ...), channel_id=1, replica_groups=mesh['shard'=4,'ctx'=4,'tp'=2] {'shard','ctx'}, use_global_device_ids=true, to_apply=%region_30.31 | all-reduce | flops 6912 | bytes 55296 | tf_op jit(solution)/shard_map/psum | solution.py:249
  1305.4 66.8 %all-reduce.16.cloned.1.call-done = (bf16[192,384]{1,0:T(8,128)(2,1)}, bf16[192,384]{1,0:T(8,128)(2,1)}, bf16[192,384]{1,0:T(8,128)(2,1)}, bf16[384,192]{0,1:T(8...) async-done(((bf16[192,384]{1,0:T(8,128)(2,1)}, bf16[192,384]{1,0:T(8,128)(2,1)}, bf16[192,384]{1,0:T(8,128)(2,1)}, bf16[384,192]{0,1:T(8,128)(2,1)}, ...) | async-done | bytes 1769488 | tf_op jit(solution)/shard_map/psum | solution.py:284
  (689 shorter events, 605.6 us)
Async XLA Ops:
  8.0 133.3 %all-gather.6.cloned.1.call-start = ((), (), s32[]{:S(2)}) async-start(), calls=%async_computation.8 | async-start | bytes 8847360 | tf_op jit(solution)/shard_map/all_gather | solution.py:142
  8.8 212.5 %all-gather.8.cloned.1.call-start = ((), (), s32[]{:S(2)}) async-start(), calls=%async_computation.9 | async-start | bytes 4423680 | tf_op jit(solution)/shard_map/all_gather | solution.py:165
  19.4 186.1 %copy-start.47 = (pred[1152]{0:T(1024)(128)(4,1)}, pred[1152]{0:T(1024)(128)(4,1)S(1)}, u32[]{:S(2)}) copy-start(pred[1152]{0:T(1024)(128)(4,1)S(1)} %compare_and_fusion) | copy-start | bytes 3460
  152.9 139.1 %all-gather.10.cloned.1.call-start = ((), (), s32[]{:S(2)}) async-start(), calls=%async_computation.10 | async-start | bytes 4423680 | tf_op jit(solution)/shard_map/all_gather | solution.py:166
  163.4 338.5 %all-reduce.8.cloned.1.call-start = ((), (), s32[]{:S(2)}) async-start(), calls=%async_computation.11 | async-start | bytes 7077888 | tf_op jit(solution)/shard_map/psum | solution.py:181
  408.8 97.0 %all-gather.12.cloned.1.call-start = ((), (), s32[]{:S(2)}) async-start(), calls=%async_computation.12 | async-start | bytes 2949120 | tf_op jit(solution)/shard_map/all_gather | solution.py:155
  409.4 105.1 %all-gather.14.cloned.1.call-start = ((), (), s32[]{:S(2)}) async-start(), calls=%async_computation.13 | async-start | bytes 2949120 | tf_op jit(solution)/shard_map/all_gather | solution.py:159
  410.0 167.3 %all-reduce.10.cloned.1.call-start = ((), (), s32[]{:S(2)}) async-start(), calls=%async_computation.14 | async-start | bytes 3538944 | tf_op jit(solution)/shard_map/psum | solution.py:189
  505.2 193.9 %copy-start.3 = (f32[1152,768]{1,0:T(8,128)}, f32[1152,768]{1,0:T(8,128)S(1)}, u32[]{:S(2)}) copy-start(f32[1152,768]{1,0:T(8,128)S(1)} %get-tuple-element.426) | copy-start | bytes 10616836
  505.2 193.9 %copy-start.28 = (f32[1152]{0:T(1024)}, f32[1152]{0:T(1024)S(1)}, u32[]{:S(2)}) copy-start(f32[1152]{0:T(1024)S(1)} %broadcast_multiply_fusion.5) | copy-start | bytes 13828
  521.3 172.5 %all-reduce.12.cloned.1.call-start = ((), (), s32[]{:S(2)}) async-start(), calls=%async_computation.15 | async-start | bytes 7077888 | tf_op jit(solution)/shard_map/psum | solution.py:207
  599.3 394.0 %reduce-scatter.25.cloned.1.call-start = ((), (), s32[]{:S(2)}) async-start(), calls=%async_computation.23 | async-start | bytes 4423680
  926.8 135.6 %reduce-scatter.27.cloned.1.call-start = ((), (), s32[]{:S(2)}) async-start(), calls=%async_computation.24 | async-start | bytes 4423680
  932.5 166.1 %reduce-scatter.23.cloned.1.call-start = ((), (), s32[]{:S(2)}) async-start(), calls=%async_computation.22 | async-start | bytes 2949120 | tf_op jit(solution)/shard_map/reduce_scatter | solution.py:279
  941.4 192.6 %reduce-scatter.21.cloned.1.call-start = ((), (), s32[]{:S(2)}) async-start(), calls=%async_computation.21 | async-start | bytes 2949120 | tf_op jit(solution)/shard_map/reduce_scatter | solution.py:276
  948.4 210.4 %reduce-scatter.19.cloned.1.call-start = ((), (), s32[]{:S(2)}) async-start(), calls=%async_computation.20 | async-start | bytes 737280 | tf_op jit(solution)/shard_map/reduce_scatter | solution.py:273
  952.9 231.1 %reduce-scatter.13.cloned.1.call-start = ((), (), s32[]{:S(2)}) async-start(), calls=%async_computation.17 | async-start | bytes 737280 | tf_op jit(solution)/shard_map/reduce_scatter | solution.py:264
  956.3 252.5 %reduce-scatter.15.cloned.1.call-start = ((), (), s32[]{:S(2)}) async-start(), calls=%async_computation.18 | async-start | bytes 737280 | tf_op jit(solution)/shard_map/reduce_scatter | solution.py:267
  996.7 236.7 %reduce-scatter.17.cloned.1.call-start = ((), (), s32[]{:S(2)}) async-start(), calls=%async_computation.19 | async-start | bytes 737280 | tf_op jit(solution)/shard_map/reduce_scatter | solution.py:270
  1065.8 236.6 %all-reduce.14.cloned.1.call-start = ((), (), s32[]{:S(2)}) async-start(), calls=%async_computation.16 | async-start | bytes 3538944 | tf_op jit(solution)/shard_map/psum | solution.py:244
  1070.8 170.3 %copy-start.42 = (f32[768]{0:T(1024)S(1)}, f32[768]{0:T(1024)}, u32[]{:S(2)}) copy-start(f32[768]{0:T(1024)} %get-tuple-element.321) | copy-start | bytes 9220
  1070.9 170.3 %copy-start.43 = (f32[768]{0:T(1024)S(1)}, f32[768]{0:T(1024)}, u32[]{:S(2)}) copy-start(f32[768]{0:T(1024)} %get-tuple-element.326) | copy-start | bytes 9220
  1070.9 231.5 %copy-start.6 = (f32[1152,768]{1,0:T(8,128)S(1)}, f32[1152,768]{1,0:T(8,128)}, u32[]{:S(2)}) copy-start(f32[1152,768]{1,0:T(8,128)} %copy-done.5) | copy-start | bytes 10616836
  1070.9 301.4 %all-reduce.16.cloned.1.call-start = ((), (), s32[]{:S(2)}) async-start(), calls=%async_computation.25 | async-start | bytes 3538944 | tf_op jit(solution)/shard_map/psum | solution.py:284
  (116 other events, 1314.9 us)
Sparse Core Ops, SparseCore 0:
  10.4 130.8 all-gather.5
  153.0 68.2 all-gather.7
  223.4 68.5 all-gather.9
  408.9 92.9 all-reduce.7
  521.5 55.7 all-reduce.9
  599.4 94.3 all-reduce.11
  926.9 66.3 reduce-scatter.24
  995.8 66.6 reduce-scatter.26
  1065.2 33.3 reduce-scatter.22
  1100.9 33.0 reduce-scatter.20
  1136.7 22.0 reduce-scatter.18
  1161.9 22.0 reduce-scatter.12
  1186.7 22.0 reduce-scatter.14
  1211.3 22.0 reduce-scatter.16
  1236.2 55.8 all-reduce.13
  1294.8 77.4 all-reduce.15
Sparse Core Ops, SparseCore 1:
  410.9 22.5 all-gather.11
  434.9 23.9 all-gather.13
where the time goes:
time: 1400 us; the launch traced here: 1390 us
  waiting for transfers between devices  765 us (55%)
  matrix products  240 us (17%)
  local copies, waits for them, and re-layouts  181 us (13%)
  blocking collectives  94.2 us (7%)
  other arithmetic  88.9 us (6%)
  between operations  16.3 us (1%)
    all_gather x1, waiting for transfers between devices, per_device(): all_tokens = lax.all_gather(tokens, 'ctx', axis=0, tiled=True)  122 us
    dot_general x42, matrix products, matmul_second(): lax.dot_general(former, latter, (((1,), (1,)), ((), ())), preferred_eleme...  106 us
    unnamed x20, waiting for transfers between devices  105 us
    psum x1, waiting for transfers between devices, per_device(): back_hidden = lax.psum(matmul_second(pre_low, wide_up), 'tp')  93.7 us
    psum x1, waiting for transfers between devices, per_device(): attn_total = lax.psum(matmul(attended, wide_output), 'tp')  89.9 us
    dot_general x30, matrix products, matmul(): return jnp.dot(former, latter, preferred_element_type=jnp.float32)  72.2 us
    psum x1, waiting for transfers between devices, per_device(): lax.psum(shard_parts[0].astype(jnp.bfloat16), 'ctx').astype(jnp.float32)  66.8 us
    dot_general x30, matrix products, matmul_first(): lax.dot_general(former, latter, (((0,), (0,)), ((), ())), preferred_eleme...  62.3 us
  transfers between devices with their start and end apart: 18, of which 15 were waited for; matrix products, arithmetic and copies ran while one was open for 8% of the time, Pallas kernels for 0%

commit v1 on v0

v1 whole, which is shorter than its diff:
```python
import functools

import jax
import jax.numpy as jnp
from jax import lax
from jax.experimental import pallas as pl
from jax.experimental.pallas import tpu as pltpu
from jax.sharding import PartitionSpec as P

HEAD = 64
HALO = 512
HALF_ROOT = 0.7071067811865476
DENSITY = 0.3989422804014327
NEG_FILL = -1000000000.0
BF = jnp.bfloat16
F32 = jnp.float32
BLOCK = 256
VMEM_LIMIT = 56 * 1024 * 1024


def matmul(former, latter):
    return jnp.dot(former, latter, preferred_element_type=F32)


def matmul_first(former, latter):
    return lax.dot_general(former, latter, (((0,), (0,)), ((), ())), preferred_element_type=F32)


def matmul_second(former, latter):
    return lax.dot_general(former, latter, (((1,), (1,)), ((), ())), preferred_element_type=F32)


def norm_forward(values, norm_gain, norm_shift):
    centre = values - jnp.mean(values, axis=1, keepdims=True)
    spread = jnp.mean(centre * centre, axis=1, keepdims=True)
    inverse = lax.rsqrt(spread + 1e-06)
    normed = centre * inverse
    return (norm_gain * normed + norm_shift, normed, inverse)


def norm_backward(gradient, normed, inverse, norm_gain):
    scaled = gradient * norm_gain
    bracket = (
        scaled
        - jnp.mean(scaled, axis=1, keepdims=True)
        - normed * jnp.mean(scaled * normed, axis=1, keepdims=True)
    )
    return inverse * bracket


def low_lanes(rows):
    return lax.broadcasted_iota(jnp.int32, (rows, 128), 1) < HEAD


def stacked(pair):
    low = low_lanes(pair.shape[0])
    zero = jnp.zeros_like(pair)
    return jnp.concatenate([jnp.where(low, pair, zero), jnp.where(low, zero, pair)], axis=0)


def unstacked(both):
    rows = both.shape[0] // 2
    return jnp.where(low_lanes(rows), both[:rows], both[rows:])


def columns(ref_value, head, rows):
    return jnp.concatenate([ref_value[:, 2 * head : 2 * head + 1], ref_value[:, 2 * head + 1 : 2 * head + 2]], axis=0)


def bias_of(own_seg, other_seg):
    return jnp.where(own_seg == other_seg, 0.0, NEG_FILL)


def forward_kernel(dim, tile, bounds, qkv, seg_col, seg_row, out, logsum, query_st, bias_ref, acc, top, total):
    pairs = dim // 128
    own = out.shape[0]

    def one_tile(i, carry):
        first = pl.multiple_of(i * tile, tile)
        rows = pl.ds(pl.multiple_of(HALO + first, 64), tile)
        seg_here = seg_col[rows, :]
        for p in range(pairs):
            query_st[p] = stacked(qkv[rows, p * 128 : p * 128 + 128])
        acc[...] = jnp.zeros_like(acc)
        total[...] = jnp.zeros_like(total)
        top[...] = jnp.full_like(top, 2 * NEG_FILL)

        def one_block(j, inner):
            start = pl.multiple_of(j * BLOCK, BLOCK)
            bias = bias_of(seg_here, seg_row[:, pl.ds(start, BLOCK)])
            bias_ref[...] = jnp.concatenate([bias, bias], axis=0)
            for p in range(pairs):
                key = qkv[pl.ds(start, BLOCK), dim + p * 128 : dim + p * 128 + 128]
                value = qkv[pl.ds(start, BLOCK), 2 * dim + p * 128 : 2 * dim + p * 128 + 128]
                scores = matmul_second(query_st[p], key) + bias_ref[...]
                old = top[p]
                new = jnp.maximum(old, jnp.max(scores, axis=1, keepdims=True))
                keep = jnp.exp(old - new)
                raised = jnp.exp(scores - new[:, :1])
                total[p] = keep * total[p] + jnp.sum(raised, axis=1, keepdims=True)
                acc[p] = keep * acc[p] + matmul(raised.astype(BF), value)
                top[p] = new
            return inner

        lax.fori_loop(bounds[i, 0], bounds[i, 1], one_block, 0)
        lane = lax.broadcasted_iota(jnp.int32, (tile, 128), 1)
        sums = jnp.zeros((tile, 128), F32)
        for p in range(pairs):
            whole = total[p]
            out[pl.ds(first, tile), p * 128 : p * 128 + 128] = unstacked(acc[p] / whole).astype(BF)
            lse = top[p] + jnp.log(whole)
            sums = jnp.where(lane == 2 * p, lse[:tile], sums)
            sums = jnp.where(lane == 2 * p + 1, lse[tile:], sums)
        logsum[pl.ds(first, tile), :] = sums
        return carry

    lax.fori_loop(0, own // tile, one_tile, 0)


def query_kernel(dim, tile, bounds, qkv, seg_col, seg_row, grad, logsum, delta, out, query_st, grad_st, bias_ref, acc):
    pairs = dim // 128
    own = out.shape[0]

    def one_tile(i, carry):
        first = pl.multiple_of(i * tile, tile)
        own_rows = pl.ds(first, tile)
        rows = pl.ds(pl.multiple_of(HALO + first, 64), tile)
        seg_here = seg_col[rows, :]
        for p in range(pairs):
            query_st[p] = stacked(qkv[rows, p * 128 : p * 128 + 128])
            grad_st[p] = stacked(grad[own_rows, p * 128 : p * 128 + 128])
        acc[...] = jnp.zeros_like(acc)

        def one_block(j, inner):
            start = pl.multiple_of(j * BLOCK, BLOCK)
            bias = bias_of(seg_here, seg_row[:, pl.ds(start, BLOCK)])
            bias_ref[...] = jnp.concatenate([bias, bias], axis=0)
            for p in range(pairs):
                key = qkv[pl.ds(start, BLOCK), dim + p * 128 : dim + p * 128 + 128]
                value = qkv[pl.ds(start, BLOCK), 2 * dim + p * 128 : 2 * dim + p * 128 + 128]
                scores = matmul_second(query_st[p], key) + bias_ref[...]
                probs = jnp.exp(scores - columns(logsum[own_rows, :], p, tile))
                grad_probs = matmul_second(grad_st[p], value)
                grad_scores = (probs * (grad_probs - columns(delta[own_rows, :], p, tile))).astype(BF)
                acc[p] += matmul(grad_scores, key)
            return inner

        lax.fori_loop(bounds[i, 0], bounds[i, 1], one_block, 0)
        for p in range(pairs):
            out[own_rows, p * 128 : p * 128 + 128] = 0.125 * unstacked(acc[p])
        return carry

    lax.fori_loop(0, own // tile, one_tile, 0)


def key_kernel(dim, tile, bounds, qkv, seg_col, seg_row, grad, logsum, delta, out, key_st, value_st, bias_ref, key_acc, value_acc):
    pairs = dim // 128
    own = out.shape[0]

    def one_tile(i, carry):
        first = pl.multiple_of(i * tile, tile)
        own_rows = pl.ds(first, tile)
        rows = pl.ds(pl.multiple_of(HALO + first, 64), tile)
        seg_here = seg_col[rows, :]
        for p in range(pairs):
            key_st[p] = stacked(qkv[rows, dim + p * 128 : dim + p * 128 + 128])
            value_st[p] = stacked(qkv[rows, 2 * dim + p * 128 : 2 * dim + p * 128 + 128])
        key_acc[...] = jnp.zeros_like(key_acc)
        value_acc[...] = jnp.zeros_like(value_acc)

        def one_block(j, inner):
            start = pl.multiple_of(j * BLOCK, BLOCK)
            there = pl.ds(start, BLOCK)
            bias_ref[...] = bias_of(seg_here, seg_row[:, there])
            for p in range(pairs):
                query = qkv[there, p * 128 : p * 128 + 128]
                grad_pair = grad[there, p * 128 : p * 128 + 128]
                scores = matmul_second(key_st[p], query)
                grad_probs = matmul_second(value_st[p], grad_pair)
                probs_all, grads_all = [], []
                for half in range(2):
                    head = 2 * p + half
                    lines = slice(half * tile, half * tile + tile)
                    probs = jnp.exp(scores[lines] + bias_ref[...] - logsum[head : head + 1, there])
                    grads_all.append((probs * (grad_probs[lines] - delta[head : head + 1, there])).astype(BF))
                    probs_all.append(probs.astype(BF))
                key_acc[p] += matmul(jnp.concatenate(grads_all, axis=0), query)
                value_acc[p] += matmul(jnp.concatenate(probs_all, axis=0), grad_pair)
            return inner

        lax.fori_loop(bounds[i, 0], bounds[i, 1], one_block, 0)
        for p in range(pairs):
            out[own_rows, p * 128 : p * 128 + 128] = unstacked(key_acc[p])
            out[own_rows, dim + p * 128 : dim + p * 128 + 128] = unstacked(value_acc[p])
        return carry

    lax.fori_loop(0, own // tile, one_tile, 0)


def vmem_call(kernel, arrays, bounds, outs, scratch, flops):
    spec = pl.BlockSpec(memory_space=pltpu.VMEM)
    return pl.pallas_call(
        kernel,
        out_shape=outs,
        in_specs=[pl.BlockSpec(memory_space=pltpu.SMEM)] + [spec] * len(arrays),
        out_specs=jax.tree.map(lambda leaf: spec, outs),
        scratch_shapes=scratch,
        compiler_params=pltpu.CompilerParams(vmem_limit_bytes=VMEM_LIMIT),
        cost_estimate=pl.CostEstimate(flops=flops, bytes_accessed=12000000, transcendentals=6000000),
    )(bounds, *arrays)


def attention_tile(own):
    for tile in (192, 128, 64, 32, 16):
        if own % tile == 0:
            return tile
    raise ValueError("rows")


def attention_forward(qkv, seg_col, seg_row, bounds, own, dim):
    tile = attention_tile(own)
    pairs = dim // 128
    return vmem_call(
        functools.partial(forward_kernel, dim, tile),
        (qkv, seg_col, seg_row),
        bounds,
        (jax.ShapeDtypeStruct((own, dim), BF), jax.ShapeDtypeStruct((own, 128), F32)),
        [
            pltpu.VMEM((pairs, 2 * tile, 128), BF),
            pltpu.VMEM((2 * tile, BLOCK), F32),
            pltpu.VMEM((pairs, 2 * tile, 128), F32),
            pltpu.VMEM((pairs, 2 * tile, 128), F32),
            pltpu.VMEM((pairs, 2 * tile, 128), F32),
        ],
        10_000_000_000,
    )


def attention_query(qkv, seg_col, seg_row, bounds, grad, logsum, delta, dim):
    own = grad.shape[0]
    tile = attention_tile(own)
    pairs = dim // 128
    return vmem_call(
        functools.partial(query_kernel, dim, tile),
        (qkv, seg_col, seg_row, grad, logsum, delta),
        bounds,
        jax.ShapeDtypeStruct((own, dim), F32),
        [
            pltpu.VMEM((pairs, 2 * tile, 128), BF),
            pltpu.VMEM((pairs, 2 * tile, 128), BF),
            pltpu.VMEM((2 * tile, BLOCK), F32),
            pltpu.VMEM((pairs, 2 * tile, 128), F32),
        ],
        15_000_000_000,
    )


def attention_key(qkv, seg_col, seg_row, bounds, grad_win, logsum_rows, delta_rows, own, dim):
    tile = attention_tile(own)
    pairs = dim // 128
    return vmem_call(
        functools.partial(key_kernel, dim, tile),
        (qkv, seg_col, seg_row, grad_win, logsum_rows, delta_rows),
        bounds,
        jax.ShapeDtypeStruct((own, 2 * dim), F32),
        [
            pltpu.VMEM((pairs, 2 * tile, 128), BF),
            pltpu.VMEM((pairs, 2 * tile, 128), BF),
            pltpu.VMEM((tile, BLOCK), F32),
            pltpu.VMEM((pairs, 2 * tile, 128), F32),
            pltpu.VMEM((pairs, 2 * tile, 128), F32),
        ],
        20_000_000_000,
    )


def rows_to_slots(values, dealt, place_z, place_y):
    own, dim = values.shape
    half = dim // 2
    keep = lax.dynamic_slice_in_dim(values, place_y * half, half, axis=1)
    send = lax.dynamic_slice_in_dim(values, (1 - place_y) * half, half, axis=1)
    other = lax.ppermute(send, "tp", [(0, 1), (1, 0)])
    first = jnp.where(place_y == 0, keep, other)
    second = jnp.where(place_y == 0, other, keep)
    block = jnp.concatenate([first, second], axis=0)
    everything = lax.all_gather(block, "ctx", axis=0, tiled=True)
    slots = 2 * own
    mine = lax.dynamic_slice_in_dim(dealt, place_z * slots, slots)
    picked = jnp.take(everything, mine, axis=0, mode="clip")
    other_columns = lax.ppermute(picked, "tp", [(0, 1), (1, 0)])
    return jnp.concatenate(
        [jnp.where(place_y == 0, picked, other_columns), jnp.where(place_y == 0, other_columns, picked)], axis=1
    )


def slots_to_rows(values, dealt, place_z, place_y):
    slots, dim = values.shape
    half, own = dim // 2, slots // 2
    block = lax.dynamic_slice_in_dim(values, place_y * half, half, axis=1)
    everything = lax.all_gather(block, "ctx", axis=0, tiled=True)
    wanted = place_z * slots + lax.broadcasted_iota(jnp.int32, (slots, 1), 0)
    chosen = (wanted == dealt[None, :]).astype(BF)
    picked = matmul(chosen, everything).astype(BF)
    keep = lax.dynamic_slice_in_dim(picked, place_y * own, own, axis=0)
    send = lax.dynamic_slice_in_dim(picked, (1 - place_y) * own, own, axis=0)
    other = lax.ppermute(send, "tp", [(0, 1), (1, 0)])
    return jnp.concatenate([jnp.where(place_y == 0, keep, other), jnp.where(place_y == 0, other, keep)], axis=1)


def per_device(
    tokens,
    cotangent,
    seq_lengths,
    dealing,
    query_weight,
    query_bias,
    key_weight,
    value_weight,
    value_bias,
    output_weight,
    output_bias,
    first_gain,
    first_shift,
    up_weight,
    up_bias,
    down_weight,
    down_bias,
    second_gain,
    second_shift,
):
    rows, dim = tokens.shape
    ctx_size, tp_size = lax.axis_size("ctx"), lax.axis_size("tp")
    group_rows = rows * ctx_size
    own = rows // tp_size
    place_z, place_y = lax.axis_index("ctx"), lax.axis_index("tp")
    window = HALO + own + HALO
    padded = -(-window // BLOCK) * BLOCK
    heads = dim // HEAD
    dealt = dealing[0]

    lengths = seq_lengths[0]
    number = lengths.shape[0]
    upto = jnp.arange(number)[:, None] >= jnp.arange(number)[None, :]
    ends = jnp.sum(jnp.where(upto, lengths[None, :], 0), axis=1)
    starts = ends - lengths
    first_row = place_z * rows + place_y * own
    index = jnp.arange(padded, dtype=jnp.int32)
    position = first_row - HALO + index
    valid = (position >= 0) & (position < group_rows) & (index < window)
    segment = jnp.sum((position[:, None] >= ends[None, :-1]).astype(jnp.int32), axis=1)
    segment = jnp.where(valid, segment, -1)
    seg_row, seg_col = segment[None, :], segment[:, None]
    tile = attention_tile(own)
    tile_first = first_row + tile * jnp.arange(own // tile, dtype=jnp.int32)
    tile_last = tile_first + tile - 1
    begin = jnp.max(jnp.where(starts[None, :] <= tile_first[:, None], starts[None, :], 0), axis=1)
    finish = jnp.min(jnp.where(ends[None, :] > tile_last[:, None], ends[None, :], group_rows), axis=1)
    shift = HALO - first_row
    bounds = jnp.stack([(begin + shift) // BLOCK, (finish + shift + BLOCK - 1) // BLOCK], axis=1).astype(jnp.int32)

    def whole(weight, shard_axis):
        once = lax.all_gather(weight, "shard", axis=shard_axis, tiled=True)
        return lax.all_gather(once, "tp", axis=1 - shard_axis, tiled=True)

    edge = jnp.where(place_y == 0, tokens[rows - HALO :], tokens[:HALO])
    hops = [(2 * z, 2 * z + 2) for z in range(ctx_size - 1)] + [(2 * z + 1, 2 * z - 1) for z in range(1, ctx_size)]
    arrived = lax.ppermute(edge, ("ctx", "tp"), hops)
    x_window = jnp.where(
        place_y == 0,
        jnp.concatenate([arrived, tokens[: own + HALO]], axis=0),
        jnp.concatenate([tokens[own - HALO :], arrived], axis=0),
    )
    x_window = jnp.pad(x_window, ((0, padded - window), (0, 0)))
    inputs = lax.dynamic_slice_in_dim(tokens, place_y * own, own, axis=0)

    wide_qkv = jnp.concatenate([whole(query_weight, 0), whole(key_weight, 0), whole(value_weight, 0)], axis=1)
    wide_output = whole(output_weight, 1)
    wide_up = whole(up_weight, 0)
    wide_down = whole(down_weight, 1)
    whole_bias = lax.all_gather(jnp.stack([query_bias, value_bias]), "tp", axis=1, tiled=True).astype(F32)
    whole_up_bias = lax.all_gather(up_bias, "tp", axis=0, tiled=True).astype(F32)
    output_bias = output_bias.astype(F32)
    first_gain = first_gain.astype(F32)
    first_shift = first_shift.astype(F32)
    down_bias = down_bias.astype(F32)
    second_gain = second_gain.astype(F32)
    second_shift = second_shift.astype(F32)

    raw = matmul(x_window, wide_qkv)
    qkv = jnp.concatenate(
        [
            ((raw[:, :dim] + whole_bias[0]).astype(BF) * BF(0.125)),
            raw[:, dim : 2 * dim].astype(BF),
            (raw[:, 2 * dim :] + whole_bias[1]).astype(BF),
        ],
        axis=1,
    )
    attended, logsum = attention_forward(qkv, seg_col, seg_row, bounds, own, dim)
    grad_out = slots_to_rows(cotangent, dealt, place_z, place_y).astype(F32)
    hidden_one, normed_one, inverse_one = norm_forward(
        inputs.astype(F32) + matmul(attended, wide_output) + output_bias, first_gain, first_shift
    )
    hidden_low = hidden_one.astype(BF)
    pre_act = matmul(hidden_low, wide_up) + whole_up_bias
    erf_part = 0.5 * (1.0 + jax.scipy.special.erf(pre_act * HALF_ROOT))
    act_low = (pre_act * erf_part).astype(BF)
    layer_value, normed_two, inverse_two = norm_forward(
        hidden_one + matmul(act_low, wide_down) + down_bias, second_gain, second_shift
    )
    layer_out = rows_to_slots(layer_value.astype(BF), dealt, place_z, place_y)

    second_shift_grad = jnp.sum(grad_out, axis=0)
    second_gain_grad = jnp.sum(grad_out * normed_two, axis=0)
    grad_second = norm_backward(grad_out, normed_two, inverse_two, second_gain)
    down_bias_grad = jnp.sum(grad_second, axis=0)
    second_low = grad_second.astype(BF)
    slope = erf_part + pre_act * DENSITY * jnp.exp(-0.5 * pre_act * pre_act)
    grad_pre = matmul_second(second_low, wide_down) * slope
    up_bias_grad = jnp.sum(grad_pre, axis=0)
    pre_low = grad_pre.astype(BF)
    grad_hidden = grad_second + matmul_second(pre_low, wide_up)
    first_shift_grad = jnp.sum(grad_hidden, axis=0)
    first_gain_grad = jnp.sum(grad_hidden * normed_one, axis=0)
    grad_first = norm_backward(grad_hidden, normed_one, inverse_one, first_gain)
    output_bias_grad = jnp.sum(grad_first, axis=0)
    first_low = grad_first.astype(BF)
    attended_grad = matmul_second(first_low, wide_output).astype(BF)
    delta = jnp.sum(
        (attended_grad.astype(F32) * attended.astype(F32)).reshape(own, heads, HEAD), axis=2
    )
    delta = jnp.pad(delta, ((0, 0), (0, 128 - heads)))
    up_hops = [(i, i + 1) for i in range(ctx_size * tp_size - 1)]
    down_hops = [(i + 1, i) for i in range(ctx_size * tp_size - 1)]
    both = ("ctx", "tp")
    stats = jnp.concatenate([logsum[:, :16], delta[:, :16]], axis=1).T
    grad_win = jnp.concatenate(
        [
            lax.ppermute(attended_grad[own - HALO :], both, up_hops),
            attended_grad,
            lax.ppermute(attended_grad[:HALO], both, down_hops),
            jnp.zeros((padded - window, dim), BF),
        ],
        axis=0,
    )
    stats_win = jnp.concatenate(
        [
            lax.ppermute(stats[:, own - HALO :], both, up_hops),
            stats,
            lax.ppermute(stats[:, :HALO], both, down_hops),
            jnp.zeros((stats.shape[0], padded - window), F32),
        ],
        axis=1,
    )
    query_grad = attention_query(qkv, seg_col, seg_row, bounds, attended_grad, logsum, delta, dim)
    pair_grad = attention_key(
        qkv, seg_col, seg_row, bounds, grad_win, stats_win[:16], stats_win[16:], own, dim
    )
    query_bias_grad = jnp.sum(query_grad, axis=0)
    value_bias_grad = jnp.sum(pair_grad[:, dim:], axis=0)
    qkv_low = jnp.concatenate([query_grad.astype(BF), pair_grad.astype(BF)], axis=1)
    tokens_grad = (grad_first + matmul_second(qkv_low, wide_qkv)).astype(BF)
    tokens_grad = rows_to_slots(tokens_grad, dealt, place_z, place_y)

    def owned(full, shard_axis):
        part = lax.psum_scatter(full.astype(BF), "tp", scatter_dimension=1 - shard_axis, tiled=True)
        part = lax.psum_scatter(part, "shard", scatter_dimension=shard_axis, tiled=True)
        return lax.psum(part, "ctx").astype(F32)

    down_full = matmul_first(act_low, second_low)
    up_full = matmul_first(hidden_low, pre_low)
    output_full = matmul_first(attended, first_low)
    qkv_full = matmul_first(inputs, qkv_low)
    small = lax.psum(
        jnp.concatenate(
            [
                query_bias_grad,
                value_bias_grad,
                up_bias_grad,
                output_bias_grad,
                first_gain_grad,
                first_shift_grad,
                down_bias_grad,
                second_gain_grad,
                second_shift_grad,
            ]
        ),
        ("shard", "ctx", "tp"),
    )
    hidden = up_bias_grad.shape[0]
    sizes = [dim, dim, hidden] + [dim] * 6
    offsets = [sum(sizes[:i]) for i in range(len(sizes))]
    parts = [small[o : o + s] for o, s in zip(offsets, sizes)]

    def by_tp(vector):
        part = vector.shape[0] // tp_size
        return lax.dynamic_slice_in_dim(vector, place_y * part, part)

    return (
        layer_out,
        tokens_grad,
        owned(qkv_full[:, :dim], 0),
        by_tp(parts[0]),
        owned(qkv_full[:, dim : 2 * dim], 0),
        owned(qkv_full[:, 2 * dim :], 0),
        by_tp(parts[1]),
        owned(output_full, 1),
        parts[3],
        parts[4],
        parts[5],
        owned(up_full, 0),
        by_tp(parts[2]),
        owned(down_full, 1),
        parts[6],
        parts[7],
        parts[8],
    )


def solution(mesh):
    return jax.shard_map(
        per_device,
        mesh=mesh,
        in_specs=(
            P(("shard", "ctx"), None),
            P(("shard", "ctx"), None),
            P("shard", None),
            P("shard", None),
            P("shard", "tp"),
            P("tp"),
            P("shard", "tp"),
            P("shard", "tp"),
            P("tp"),
            P("tp", "shard"),
            P(),
            P(),
            P(),
            P("shard", "tp"),
            P("tp"),
            P("tp", "shard"),
            P(),
            P(),
            P(),
        ),
        out_specs=(
            P(("shard", "ctx"), None),
            P(("shard", "ctx"), None),
            P("shard", "tp"),
            P("tp"),
            P("shard", "tp"),
            P("shard", "tp"),
            P("tp"),
            P("tp", "shard"),
            P(),
            P(),
            P(),
            P("shard", "tp"),
            P("tp"),
            P("tp", "shard"),
            P(),
            P(),
            P(),
        ),
        check_vma=False,
    )
```

time: 1400 us -> 1100 us (0.79)
  matrix products: 240 us -> 75.6 us
  local copies, waits for them, and re-layouts: 181 us -> 68.9 us
  waiting for transfers between devices: 765 us -> 660 us
  Pallas kernels: 0 us -> 73.1 us
  other arithmetic: 88.9 us -> 56.2 us
  starting transfers between devices: 1.5 us -> 32.4 us
    psum x5 -> x1, waiting for transfers between devices: 302 us -> 86.8 us  [owned(): return lax.psum(part, 'ctx').astype(F32)]
    dot_general x42 -> x4, matrix products: 106 us -> 19 us  [matmul_second(): lax.dot_general(former, latter, (((1,), (1,)), ((), ())), preferred_eleme...]
    all_gather x5 -> x11, waiting for transfers between devices: 196 us -> 279 us  [the longest x6 130 us: whole(): return lax.all_gather(once, 'tp', axis=1 - shard_axis, tiled=True)]
    ppermute x0 -> x10, waiting for transfers between devices: none -> 74.2 us  [the longest x2 38.1 us: rows_to_slots(): other = lax.ppermute(send, 'tp', [(0, 1), (1, 0)])]
    pallas_call x0 -> x3, Pallas kernels: none -> 73.1 us  [vmem_call(): pl.pallas_call(kernel, out_shape=outs, in_specs=[pl.BlockSpec(memory_spac...]
    unnamed x20 -> x29, waiting for transfers between devices: 105 us -> 50.9 us
    dot_general x30 -> x4, matrix products: 62.3 us -> 21.3 us  [matmul_first(): lax.dot_general(former, latter, (((0,), (0,)), ((), ())), preferred_eleme...]
    dot_general x30 -> x5, matrix products: 72.2 us -> 35.3 us  [matmul(): return jnp.dot(former, latter, preferred_element_type=F32)]
  transfers between devices with their start and end apart: 18 -> 34, of which waited for: 15 -> 20; matrix products, arithmetic and copies ran while one was open for 8% -> 15% of each run, Pallas kernels for 0% -> 7%
where the time goes in v1:
time: 1100 us; the launch traced here: 1090 us
  waiting for transfers between devices  660 us (60%)
  blocking collectives  106 us (10%)
  matrix products  75.6 us (7%)
  Pallas kernels  73.1 us (7%)
  local copies, waits for them, and re-layouts  68.9 us (6%)
  other arithmetic  56.2 us (5%)
  starting transfers between devices  32.4 us (3%)
  between operations  15.8 us (1%)
    all_gather x6, waiting for transfers between devices, whole(): return lax.all_gather(once, 'tp', axis=1 - shard_axis, tiled=True)  130 us
    reduce_scatter x4, waiting for transfers between devices, owned(): lax.psum_scatter(part, 'shard', scatter_dimension=shard_axis, tiled=True)  109 us
    all_gather x2, waiting for transfers between devices, rows_to_slots(): everything = lax.all_gather(block, 'ctx', axis=0, tiled=True)  97.7 us
    psum x1, waiting for transfers between devices, owned(): return lax.psum(part, 'ctx').astype(F32)  86.8 us
    pallas_call x3, Pallas kernels, vmem_call(): pl.pallas_call(kernel, out_shape=outs, in_specs=[pl.BlockSpec(memory_spac...  73.1 us
    reduce_scatter x3, waiting for transfers between devices, owned(): lax.psum_scatter(full.astype(BF), 'tp', scatter_dimension=1 - shard_axis,...  60.1 us
    psum x1, blocking collectives, per_device(): lax.psum(jnp.concatenate([query_bias_grad, value_bias_grad, up_bias_grad,...  55.4 us
    all_gather x1, waiting for transfers between devices, slots_to_rows(): everything = lax.all_gather(block, 'ctx', axis=0, tiled=True)  51.9 us
  transfers between devices with their start and end apart: 34, of which 20 were waited for; matrix products, arithmetic and copies ran while one was open for 15% of the time, Pallas kernels for 7%

profile of v1, /device:TPU:0, one launch (start us, length us, event | category | flops | bytes accessed | tf_op | source)
XLA Modules:
  0.0 1088.6 jit_solution(9458325013343135257)
XLA Ops:
  30.0 11.6 %all_gather.55 = bf16[768,384]{1,0:T(8,128)(2,1)} all-gather(bf16[192,384]{1,0:T(8,128)(2,1)S(1)} %copy-done.29), channel_id=1, replica_groups=mesh['shard'=4,'ctx'=4,'tp'=2] {'shard'}, dimensions={0}, use_global_device_ids=true | all-gather | bytes 737280 | tf_op jit(solution)/shard_map/all_gather | solution.py:362
  79.7 11.9 %all-gather.15.cloned.1.call-done = bf16[768,768]{1,0:T(8,128)(2,1)} async-done(((bf16[768,384]{1,0:T(8,128)(2,1)}), bf16[768,768]{1,0:T(8,128)(2,1)}) %all-gather.15.cloned.1.call-update) | async-done | bytes 1179664 | tf_op jit(solution)/shard_map/all_gather | solution.py:363
  94.1 21.7 %all-gather.17.cloned.1.call-done = bf16[768,768]{1,0:T(8,128)(2,1)} async-done(((bf16[768,384]{1,0:T(8,128)(2,1)}), bf16[768,768]{1,0:T(8,128)(2,1)}) %all-gather.17.cloned.1.call-update) | async-done | bytes 1179664 | tf_op jit(solution)/shard_map/all_gather | solution.py:363
  150.3 32.4 %shard_map.314 = (bf16[576,768]{1,0:T(8,128)(2,1)}, f32[576,128]{1,0:T(8,128)}) custom-call(s32[3,2]{1,0:T(4,128)} %pad_add_fusion.bounds, bf16[1792,2304]{1,0:T(8,128)(2,1)} %pad_maximum_fusion.qkv, s32[1792,1]{1,0:T(8,128)} %reshape_select_fusion.seg_col, s32[1,1792]{1,0:T(1,128)} %and_select_fusion.seg_row), custom_call_target="tpu_custom_call" | custom-call | flops 10000000000 | bytes 12000000 | tf_op jit(solution)/shard_map/pallas_call | solution.py:202
  185.8 51.9 %all-gather.31.cloned.1.call-done = bf16[4608,384]{1,0:T(8,128)(2,1)} async-done(((bf16[1152,384]{1,0:T(8,128)(2,1)}), bf16[4608,384]{1,0:T(8,128)(2,1)}) %all-gather.31.cloned.1.call-update) | async-done | bytes 3538960 | tf_op jit(solution)/shard_map/all_gather | solution.py:300
  247.5 19.0 %collective-permute-done.3 = bf16[576,384]{1,0:T(8,128)(2,1)S(1)} collective-permute-done((bf16[576,384]{1,0:T(8,128)(2,1)S(1)}, bf16[576,384]{1,0:T(8,128)(2,1)S(1)}, u32[]{:S(2)}, u32[]{:S(2)}) %collective-permute-start.3) | collective-permute-done | bytes 442400 | tf_op jit(solution)/shard_map/ppermute | solution.py:306
  267.5 40.8 %all-gather.23.cloned.1.call-done = bf16[768,3072]{1,0:T(8,128)(2,1)} async-done(((bf16[768,1536]{1,0:T(8,128)(2,1)}), bf16[768,3072]{1,0:T(8,128)(2,1)}) %all-gather.23.cloned.1.call-update) | async-done | bytes 4718608 | tf_op jit(solution)/shard_map/all_gather | solution.py:363
  316.0 55.2 %all-gather.27.cloned.1.call-done = bf16[3072,768]{0,1:T(8,128)(2,1)} async-done(((bf16[1536,768]{0,1:T(8,128)(2,1)}), bf16[3072,768]{0,1:T(8,128)(2,1)}) %all-gather.27.cloned.1.call-update) | async-done | bytes 4718608 | tf_op jit(solution)/shard_map/all_gather | solution.py:363
  423.1 19.5 %shard_map.315 = f32[576,768]{1,0:T(8,128)} custom-call(s32[3,2]{1,0:T(4,128)} %pad_add_fusion.bounds, bf16[1792,2304]{1,0:T(8,128)(2,1)} %pad_maximum_fusion.qkv, s32[1792,1]{1,0:T(8,128)} %reshape_select_fusion.seg_col, s32[1,1792]{1,0:T(1,128)} %and_select_fusion.seg_row, bf16[576,768]{1,0:T(8,128)(2,1)} %copy-done.3, ...), custom_call_target="tpu_custom_call" | custom-call | flops 15000000512 | bytes 12000000 | tf_op jit(solution)/shard_map/pallas_call | solution.py:202
  455.1 16.6 %collective-permute-done.6 = f32[32,512]{1,0:T(8,128)S(1)} collective-permute-done((f32[32,512]{1,0:T(8,128)S(1)}, f32[32,512]{1,0:T(8,128)S(1)}, u32[]{:S(2)}, u32[]{:S(2)}) %collective-permute-start.6) | collective-permute-done | bytes 65568 | tf_op jit(solution)/shard_map/ppermute | solution.py:447
  476.9 21.3 %shard_map.316 = f32[576,1536]{1,0:T(8,128)} custom-call(s32[3,2]{1,0:T(4,128)} %pad_add_fusion.bounds, bf16[1792,2304]{1,0:T(8,128)(2,1)} %pad_maximum_fusion.qkv, s32[1792,1]{1,0:T(8,128)} %reshape_select_fusion.seg_col, s32[1,1792]{1,0:T(1,128)} %and_select_fusion.seg_row, bf16[1792,768]{1,0:T(8,128)(2,1)} %maximum_maximum_fusion.grad, ...), custom_call_target="tpu_custom_call" | custom-call | flops 20000000000 | bytes 12000000 | tf_op jit(solution)/shard_map/pallas_call | solution.py:202
  527.3 20.0 %collective-permute-done.1 = bf16[576,384]{1,0:T(8,128)(2,1)S(1)} collective-permute-done((bf16[576,384]{1,0:T(8,128)(2,1)S(1)}, bf16[576,384]{1,0:T(8,128)(2,1)S(1)}, u32[]{:S(2)}, u32[]{:S(2)}) %collective-permute-start.1) | collective-permute-done | bytes 442400 | tf_op jit(solution)/shard_map/ppermute | solution.py:282
  557.9 18.1 %collective-permute-done.8 = bf16[576,384]{1,0:T(8,128)(2,1)S(1)} collective-permute-done((bf16[576,384]{1,0:T(8,128)(2,1)S(1)}, bf16[576,384]{1,0:T(8,128)(2,1)S(1)}, u32[]{:S(2)}, u32[]{:S(2)}) %collective-permute-start.8) | collective-permute-done | bytes 442400 | tf_op jit(solution)/shard_map/ppermute | solution.py:282
  586.1 23.0 %reduce-scatter.41.cloned.1.call-done = bf16[384,768]{1,0:T(8,128)(2,1)} async-done(((bf16[768,768]{1,0:T(8,128)(2,1)}), bf16[384,768]{1,0:T(8,128)(2,1)}) %reduce-scatter.41.cloned.1.call-update) | async-done | bytes 589840
  611.3 60.1 %reduce-scatter.31.cloned.1.call-done = bf16[768,1536]{1,0:T(8,128)(2,1)} async-done(((bf16[768,3072]{1,0:T(8,128)(2,1)}), bf16[768,1536]{1,0:T(8,128)(2,1)}) %reduce-scatter.31.cloned.1.call-update) | async-done | bytes 2359312 | tf_op jit(solution)/shard_map/reduce_scatter | solution.py:465
  673.9 69.5 %all-gather.29.cloned.1.call-done = bf16[4608,384]{1,0:T(8,128)(2,1)} async-done(((bf16[1152,384]{1,0:T(8,128)(2,1)}), bf16[4608,384]{1,0:T(8,128)(2,1)}) %all-gather.29.cloned.1.call-update) | async-done | bytes 3538960 | tf_op jit(solution)/shard_map/all_gather | solution.py:286
  751.5 55.4 %psum.50 = f32[9216]{0:T(1024)S(1)} all-reduce(f32[9216]{0:T(1024)S(1)} %constant_dynamic-update-slice_fusion.6), channel_id=1, replica_groups=mesh['shard'=4,'ctx'=4,'tp'=2] {'shard','ctx','tp'}, use_global_device_ids=true, to_apply=%region_25.26 | all-reduce | flops 9216 | bytes 73728 | tf_op jit(solution)/shard_map/psum | solution.py:473
  811.2 28.2 %all-gather.33.cloned.1.call-done = bf16[4608,384]{1,0:T(8,128)(2,1)} async-done(((bf16[1152,384]{1,0:T(8,128)(2,1)}), bf16[4608,384]{1,0:T(8,128)(2,1)}) %all-gather.33.cloned.1.call-update) | async-done | bytes 3538960 | tf_op jit(solution)/shard_map/all_gather | solution.py:286
  847.2 26.3 %reduce-scatter.45.cloned.1.call-done = bf16[192,1536]{1,0:T(8,128)(2,1)} async-done(((bf16[768,1536]{1,0:T(8,128)(2,1)}), bf16[192,1536]{1,0:T(8,128)(2,1)}) %reduce-scatter.45.cloned.1.call-update) | async-done | bytes 589840
  875.7 23.0 %reduce-scatter.23.cloned.1.call-done = bf16[192,384]{1,0:T(8,128)(2,1)} async-done(((bf16[768,384]{1,0:T(8,128)(2,1)}), bf16[192,384]{1,0:T(8,128)(2,1)}) %reduce-scatter.23.cloned.1.call-update) | async-done | bytes 147472 | tf_op jit(solution)/shard_map/reduce_scatter | solution.py:466
  898.7 25.4 %reduce-scatter.25.cloned.1.call-done = bf16[192,384]{1,0:T(8,128)(2,1)} async-done(((bf16[768,384]{1,0:T(8,128)(2,1)}), bf16[192,384]{1,0:T(8,128)(2,1)}) %reduce-scatter.25.cloned.1.call-update) | async-done | bytes 147472 | tf_op jit(solution)/shard_map/reduce_scatter | solution.py:466
  924.0 24.8 %reduce-scatter.27.cloned.1.call-done = bf16[192,384]{1,0:T(8,128)(2,1)} async-done(((bf16[768,384]{1,0:T(8,128)(2,1)}), bf16[192,384]{1,0:T(8,128)(2,1)}) %reduce-scatter.27.cloned.1.call-update) | async-done | bytes 147472 | tf_op jit(solution)/shard_map/reduce_scatter | solution.py:466
  948.8 35.8 %reduce-scatter.33.cloned.1.call-done = bf16[192,1536]{1,0:T(8,128)(2,1)} async-done(((bf16[768,1536]{1,0:T(8,128)(2,1)}), bf16[192,1536]{1,0:T(8,128)(2,1)}) %reduce-scatter.33.cloned.1.call-update) | async-done | bytes 589840 | tf_op jit(solution)/shard_map/reduce_scatter | solution.py:466
  987.8 86.8 %all-reduce.5.cloned.1.call-done = (bf16[384,192]{1,0:T(8,128)(2,1)}, bf16[1536,192]{1,0:T(8,128)(2,1)}, bf16[192,384]{1,0:T(8,128)(2,1)}, bf16[192,384]{1,0:T(8...) async-done(((bf16[384,192]{1,0:T(8,128)(2,1)}, bf16[1536,192]{1,0:T(8,128)(2,1)}, bf16[192,384]{1,0:T(8,128)(2,1)}, bf16[192,384]{1,0:T(8,128)(2,1)}, ...) | async-done | bytes 1769488 | tf_op jit(solution)/shard_map/psum | solution.py:467
  (337 shorter events, 274.4 us)
Async XLA Ops:
  18.6 73.1 %all-gather.15.cloned.1.call-start = ((), (), s32[]{:S(2)}) async-start(), calls=%async_computation.13 | async-start | bytes 1769472 | tf_op jit(solution)/shard_map/all_gather | solution.py:363
  29.9 85.9 %all-gather.17.cloned.1.call-start = ((), (), s32[]{:S(2)}) async-start(), calls=%async_computation.14 | async-start | bytes 1769472 | tf_op jit(solution)/shard_map/all_gather | solution.py:363
  41.6 101.1 %all-gather.25.cloned.1.call-start = ((), (), s32[]{:S(2)}) async-start(), calls=%async_computation.18 | async-start | bytes 2949120 | tf_op jit(solution)/shard_map/all_gather | solution.py:362
  42.2 140.4 %all-gather.19.cloned.1.call-start = ((), (), s32[]{:S(2)}) async-start(), calls=%async_computation.15 | async-start | bytes 1769472 | tf_op jit(solution)/shard_map/all_gather | solution.py:363
  50.9 186.8 %all-gather.31.cloned.1.call-start = ((), (), s32[]{:S(2)}) async-start(), calls=%async_computation.21 | async-start | bytes 4423680 | tf_op jit(solution)/shard_map/all_gather | solution.py:300
  52.1 256.2 %all-gather.23.cloned.1.call-start = ((), (), s32[]{:S(2)}) async-start(), calls=%async_computation.17 | async-start | bytes 7077888 | tf_op jit(solution)/shard_map/all_gather | solution.py:363
  72.9 298.3 %all-gather.27.cloned.1.call-start = ((), (), s32[]{:S(2)}) async-start(), calls=%async_computation.19 | async-start | bytes 7077888 | tf_op jit(solution)/shard_map/all_gather | solution.py:363
  142.8 405.9 %reduce-scatter.29.cloned.1.call-start = ((), (), s32[]{:S(2)}) async-start(), calls=%async_computation.26 | async-start | bytes 1769472 | tf_op jit(solution)/shard_map/reduce_scatter | solution.py:465
  398.0 179.3 %reduce-scatter.35.cloned.1.call-start = ((), (), s32[]{:S(2)}) async-start(), calls=%async_computation.29 | async-start | bytes 7077888 | tf_op jit(solution)/shard_map/reduce_scatter | solution.py:465
  406.0 175.7 %reduce-scatter.37.cloned.1.call-start = ((), (), s32[]{:S(2)}) async-start(), calls=%async_computation.30 | async-start | bytes 1769472
  508.6 75.3 %reduce-scatter.39.cloned.1.call-start = ((), (), s32[]{:S(2)}) async-start(), calls=%async_computation.31 | async-start | bytes 1769472
  510.2 99.0 %reduce-scatter.41.cloned.1.call-start = ((), (), s32[]{:S(2)}) async-start(), calls=%async_computation.32 | async-start | bytes 1769472
  511.7 159.7 %reduce-scatter.31.cloned.1.call-start = ((), (), s32[]{:S(2)}) async-start(), calls=%async_computation.27 | async-start | bytes 7077888 | tf_op jit(solution)/shard_map/reduce_scatter | solution.py:465
  519.9 223.5 %all-gather.29.cloned.1.call-start = ((), (), s32[]{:S(2)}) async-start(), calls=%async_computation.20 | async-start | bytes 4423680 | tf_op jit(solution)/shard_map/all_gather | solution.py:286
  548.6 260.9 %reduce-scatter.43.cloned.1.call-start = ((), (), s32[]{:S(2)}) async-start(), calls=%async_computation.33 | async-start | bytes 737280
  551.1 288.3 %all-gather.33.cloned.1.call-start = ((), (), s32[]{:S(2)}) async-start(), calls=%async_computation.22 | async-start | bytes 4423680 | tf_op jit(solution)/shard_map/all_gather | solution.py:286
  577.2 296.3 %reduce-scatter.45.cloned.1.call-start = ((), (), s32[]{:S(2)}) async-start(), calls=%async_computation.34 | async-start | bytes 2949120
  581.6 317.1 %reduce-scatter.23.cloned.1.call-start = ((), (), s32[]{:S(2)}) async-start(), calls=%async_computation.23 | async-start | bytes 737280 | tf_op jit(solution)/shard_map/reduce_scatter | solution.py:466
  583.8 340.2 %reduce-scatter.25.cloned.1.call-start = ((), (), s32[]{:S(2)}) async-start(), calls=%async_computation.24 | async-start | bytes 737280 | tf_op jit(solution)/shard_map/reduce_scatter | solution.py:466
  586.0 362.8 %reduce-scatter.27.cloned.1.call-start = ((), (), s32[]{:S(2)}) async-start(), calls=%async_computation.25 | async-start | bytes 737280 | tf_op jit(solution)/shard_map/reduce_scatter | solution.py:466
  611.3 373.4 %reduce-scatter.33.cloned.1.call-start = ((), (), s32[]{:S(2)}) async-start(), calls=%async_computation.28 | async-start | bytes 2949120 | tf_op jit(solution)/shard_map/reduce_scatter | solution.py:466
  671.4 403.2 %all-reduce.5.cloned.1.call-start = ((), (), s32[]{:S(2)}) async-start(), calls=%async_computation.35 | async-start | bytes 4030464 | tf_op jit(solution)/shard_map/psum | solution.py:467
  749.9 234.8 %collective-permute-start.2 = (bf16[1152,384]{1,0:T(8,128)(2,1)S(1)}, bf16[1152,384]{1,0:T(8,128)(2,1)S(1)}, u32[]{:S(2)}, u32[]{:S(2)}) collective-permute-start(bf16[1152,384]{1,0:T(8,128)(2,1)S(1)} %gather_fusion), channel_id=1, source_target_pairs={{0,1},{1,0},{2,3},{3,2},{4,5},{5,4},{6,7},{7,6},{8,9},{9,8},{10,11... | collective-permute-start | bytes 2654216 | tf_op jit(solution)/shard_map/ppermute | solution.py:290
  845.9 140.3 %collective-permute-start.9 = (bf16[1152,384]{1,0:T(8,128)(2,1)S(1)}, bf16[1152,384]{1,0:T(8,128)(2,1)S(1)}, u32[]{:S(2)}, u32[]{:S(2)}) collective-permute-start(bf16[1152,384]{1,0:T(8,128)(2,1)S(1)} %gather_fusion.1), channel_id=1, source_target_pairs={{0,1},{1,0},{2,3},{3,2},{4,5},{5,4},{6,7},{7,6},{8,9},{9,8},{10,11... | collective-permute-start | bytes 2654216 | tf_op jit(solution)/shard_map/ppermute | solution.py:290
  (72 other events, 1727.9 us)
Sparse Core Ops, SparseCore 0:
  9.6 33.0 all-gather.20
  44.3 22.8 all-gather.12
  68.8 22.8 all-gather.14
  93.0 22.7 all-gather.16
  117.3 24.0 all-gather.24
  142.8 22.7 all-gather.18
  167.7 69.9 all-gather.30
  239.3 68.9 all-gather.22
  309.9 61.3 all-gather.26
  398.1 21.7 reduce-scatter.28
  422.3 86.0 reduce-scatter.34
  510.5 41.4 reduce-scatter.36
  554.9 26.8 reduce-scatter.38
  583.9 25.2 reduce-scatter.40
  611.4 59.9 reduce-scatter.30
  673.4 69.9 all-gather.28
  745.8 20.6 reduce-scatter.42
  768.5 70.9 all-gather.32
  842.0 31.4 reduce-scatter.44
  876.6 22.0 reduce-scatter.22
  901.9 22.0 reduce-scatter.24
  926.7 22.0 reduce-scatter.26
  951.5 33.0 reduce-scatter.32
  988.5 86.0 all-reduce.4

commit v2 on v1

--- a/solution.py
+++ b/solution.py
@@ -48,6 +48,17 @@
     return inverse * bracket
 
 
+def places(pair, dim):
+    half, inner = divmod(pair, dim // 256)
+    base = half * (3 * dim // 2) + inner * 128
+    return base, base + dim // 2, base + dim
+
+
+def take(qkv, rows, pair, dim, which):
+    first = places(pair, dim)[which]
+    return qkv[rows, first : first + 128]
+
+
 def low_lanes(rows):
     return lax.broadcasted_iota(jnp.int32, (rows, 128), 1) < HEAD
 
@@ -80,7 +91,7 @@
         rows = pl.ds(pl.multiple_of(HALO + first, 64), tile)
         seg_here = seg_col[rows, :]
         for p in range(pairs):
-            query_st[p] = stacked(qkv[rows, p * 128 : p * 128 + 128])
+            query_st[p] = stacked(take(qkv, rows, p, dim, 0))
         acc[...] = jnp.zeros_like(acc)
         total[...] = jnp.zeros_like(total)
         top[...] = jnp.full_like(top, 2 * NEG_FILL)
@@ -90,8 +101,8 @@
             bias = bias_of(seg_here, seg_row[:, pl.ds(start, BLOCK)])
             bias_ref[...] = jnp.concatenate([bias, bias], axis=0)
             for p in range(pairs):
-                key = qkv[pl.ds(start, BLOCK), dim + p * 128 : dim + p * 128 + 128]
-                value = qkv[pl.ds(start, BLOCK), 2 * dim + p * 128 : 2 * dim + p * 128 + 128]
+                key = take(qkv, pl.ds(start, BLOCK), p, dim, 1)
+                value = take(qkv, pl.ds(start, BLOCK), p, dim, 2)
                 scores = matmul_second(query_st[p], key) + bias_ref[...]
                 old = top[p]
                 new = jnp.maximum(old, jnp.max(scores, axis=1, keepdims=True))
@@ -117,7 +128,7 @@
     lax.fori_loop(0, own // tile, one_tile, 0)
 
 
-def query_kernel(dim, tile, bounds, qkv, seg_col, seg_row, grad, logsum, delta, out, query_st, grad_st, bias_ref, acc):
+def query_kernel(dim, tile, bounds, qkv, seg_col, seg_row, grad, logsum, delta, out, sums, query_st, grad_st, bias_ref, acc):
     pairs = dim // 128
     own = out.shape[0]
 
@@ -127,7 +138,7 @@
         rows = pl.ds(pl.multiple_of(HALO + first, 64), tile)
         seg_here = seg_col[rows, :]
         for p in range(pairs):
-            query_st[p] = stacked(qkv[rows, p * 128 : p * 128 + 128])
+            query_st[p] = stacked(take(qkv, rows, p, dim, 0))
             grad_st[p] = stacked(grad[own_rows, p * 128 : p * 128 + 128])
         acc[...] = jnp.zeros_like(acc)
 
@@ -136,8 +147,8 @@
             bias = bias_of(seg_here, seg_row[:, pl.ds(start, BLOCK)])
             bias_ref[...] = jnp.concatenate([bias, bias], axis=0)
             for p in range(pairs):
-                key = qkv[pl.ds(start, BLOCK), dim + p * 128 : dim + p * 128 + 128]
-                value = qkv[pl.ds(start, BLOCK), 2 * dim + p * 128 : 2 * dim + p * 128 + 128]
+                key = take(qkv, pl.ds(start, BLOCK), p, dim, 1)
+                value = take(qkv, pl.ds(start, BLOCK), p, dim, 2)
                 scores = matmul_second(query_st[p], key) + bias_ref[...]
                 probs = jnp.exp(scores - columns(logsum[own_rows, :], p, tile))
                 grad_probs = matmul_second(grad_st[p], value)
@@ -147,13 +158,16 @@
 
         lax.fori_loop(bounds[i, 0], bounds[i, 1], one_block, 0)
         for p in range(pairs):
-            out[own_rows, p * 128 : p * 128 + 128] = 0.125 * unstacked(acc[p])
+            part = 0.125 * unstacked(acc[p])
+            out[own_rows, p * 128 : p * 128 + 128] = part.astype(BF)
+            sums[:, p * 128 : p * 128 + 128] += jnp.sum(part, axis=0, keepdims=True)
         return carry
 
+    sums[...] = jnp.zeros_like(sums)
     lax.fori_loop(0, own // tile, one_tile, 0)
 
 
-def key_kernel(dim, tile, bounds, qkv, seg_col, seg_row, grad, logsum, delta, out, key_st, value_st, bias_ref, key_acc, value_acc):
+def key_kernel(dim, tile, bounds, qkv, seg_col, seg_row, grad, logsum, delta, query_low, out, sums, key_st, value_st, bias_ref, key_acc, value_acc):
     pairs = dim // 128
     own = out.shape[0]
 
@@ -163,8 +177,8 @@
         rows = pl.ds(pl.multiple_of(HALO + first, 64), tile)
         seg_here = seg_col[rows, :]
         for p in range(pairs):
-            key_st[p] = stacked(qkv[rows, dim + p * 128 : dim + p * 128 + 128])
-            value_st[p] = stacked(qkv[rows, 2 * dim + p * 128 : 2 * dim + p * 128 + 128])
+            key_st[p] = stacked(take(qkv, rows, p, dim, 1))
+            value_st[p] = stacked(take(qkv, rows, p, dim, 2))
         key_acc[...] = jnp.zeros_like(key_acc)
         value_acc[...] = jnp.zeros_like(value_acc)
 
@@ -173,7 +187,7 @@
             there = pl.ds(start, BLOCK)
             bias_ref[...] = bias_of(seg_here, seg_row[:, there])
             for p in range(pairs):
-                query = qkv[there, p * 128 : p * 128 + 128]
+                query = take(qkv, there, p, dim, 0)
                 grad_pair = grad[there, p * 128 : p * 128 + 128]
                 scores = matmul_second(key_st[p], query)
                 grad_probs = matmul_second(value_st[p], grad_pair)
@@ -190,10 +204,15 @@
 
         lax.fori_loop(bounds[i, 0], bounds[i, 1], one_block, 0)
         for p in range(pairs):
-            out[own_rows, p * 128 : p * 128 + 128] = unstacked(key_acc[p])
-            out[own_rows, dim + p * 128 : dim + p * 128 + 128] = unstacked(value_acc[p])
+            at_query, at_key, at_value = places(p, dim)
+            out[own_rows, at_query : at_query + 128] = query_low[own_rows, p * 128 : p * 128 + 128]
+            out[own_rows, at_key : at_key + 128] = unstacked(key_acc[p]).astype(BF)
+            part = unstacked(value_acc[p])
+            out[own_rows, at_value : at_value + 128] = part.astype(BF)
+            sums[:, p * 128 : p * 128 + 128] += jnp.sum(part, axis=0, keepdims=True)
         return carry
 
+    sums[...] = jnp.zeros_like(sums)
     lax.fori_loop(0, own // tile, one_tile, 0)
 
 
@@ -244,7 +263,7 @@
         functools.partial(query_kernel, dim, tile),
         (qkv, seg_col, seg_row, grad, logsum, delta),
         bounds,
-        jax.ShapeDtypeStruct((own, dim), F32),
+        (jax.ShapeDtypeStruct((own, dim), BF), jax.ShapeDtypeStruct((1, dim), F32)),
         [
             pltpu.VMEM((pairs, 2 * tile, 128), BF),
             pltpu.VMEM((pairs, 2 * tile, 128), BF),
@@ -255,14 +274,14 @@
     )
 
 
-def attention_key(qkv, seg_col, seg_row, bounds, grad_win, logsum_rows, delta_rows, own, dim):
+def attention_key(qkv, seg_col, seg_row, bounds, grad_win, logsum_rows, delta_rows, query_low, own, dim):
     tile = attention_tile(own)
     pairs = dim // 128
     return vmem_call(
         functools.partial(key_kernel, dim, tile),
-        (qkv, seg_col, seg_row, grad_win, logsum_rows, delta_rows),
+        (qkv, seg_col, seg_row, grad_win, logsum_rows, delta_rows, query_low),
         bounds,
-        jax.ShapeDtypeStruct((own, 2 * dim), F32),
+        (jax.ShapeDtypeStruct((own, 3 * dim), BF), jax.ShapeDtypeStruct((1, dim), F32)),
         [
             pltpu.VMEM((pairs, 2 * tile, 128), BF),
             pltpu.VMEM((pairs, 2 * tile, 128), BF),
@@ -272,6 +291,432 @@
         ],
         20_000_000_000,
     )
+
+
+def remote(src, dst, send_sem, recv_sem, where):
+    return pltpu.make_async_remote_copy(
+        src_ref=src,
+        dst_ref=dst,
+        send_sem=send_sem,
+        recv_sem=recv_sem,
+        device_id=where,
+        device_id_type=pl.DeviceIdType.MESH,
+    )
+
+
+def greet(peers):
+    barrier = pltpu.get_barrier_semaphore()
+    for peer in peers:
+        pl.semaphore_signal(barrier, inc=1, device_id=peer, device_id_type=pl.DeviceIdType.MESH)
+    pl.semaphore_wait(barrier, len(peers))
+
+
+def here():
+    shard, z, y = lax.axis_index("shard"), lax.axis_index("ctx"), lax.axis_index("tp")
+    return shard // 2, shard % 2, y, z
+
+
+def gather_kernel(widths, *refs):
+    count = len(widths)
+    pieces, wholes = refs[:count], refs[count : 2 * count]
+    small, small_whole = refs[2 * count], refs[2 * count + 1]
+    send, recv, own_sem, small_sem = refs[2 * count + 2 :]
+    x, c, y, z = here()
+    at_x, at_y, at_c = {"shard": 2 * (1 - x) + c}, {"tp": 1 - y}, {"shard": 2 * x + 1 - c}
+    greet((at_x, at_y, at_c))
+
+    def slot(a, of_y, of_x, of_c, lines=None):
+        cols = pl.ds(pl.multiple_of(of_y * widths[a], 128), widths[a])
+        rows = wholes[a].shape[2]
+        lines = slice(0, rows) if lines is None else slice(lines * rows // 2, (lines + 1) * rows // 2)
+        return wholes[a].at[of_x, of_c, lines, cols]
+
+    def copy(a, kind, src, dst, where):
+        return remote(src, dst, send.at[a, kind], recv.at[a, kind], where)
+
+    def moves(a):
+        mine, from_x, from_y = slot(a, y, x, c), slot(a, y, 1 - x, c), slot(a, 1 - y, x, c)
+        table = [
+            (pieces[a], mine, at_x),
+            (pieces[a], mine, at_y),
+            (pieces[a], mine, at_c),
+            (slot(a, y, 1 - x, c, 0), slot(a, y, 1 - x, c, 0), at_y),
+            (slot(a, 1 - y, x, c, 1), slot(a, 1 - y, x, c, 1), at_x),
+            (from_x, from_x, at_c),
+            (from_y, from_y, at_c),
+            (slot(a, 1 - y, 1 - x, c, 0), slot(a, 1 - y, 1 - x, c, 0), at_c),
+            (slot(a, 1 - y, 1 - x, c, 1), slot(a, 1 - y, 1 - x, c, 1), at_c),
+        ]
+        return [copy(a, kind, *row) for kind, row in enumerate(table)]
+
+    tables = [moves(a) for a in range(count)]
+    lines = small_whole.shape[0] // 2
+    small_at = small_whole.at[pl.ds(pl.multiple_of(y * lines, 16), lines)]
+    small_copy = remote(small, small_at, small_sem.at[0], small_sem.at[1], at_y)
+    small_copy.start()
+    locals_ = [pltpu.make_async_copy(small, small_at, small_sem.at[2])]
+    for a in range(count):
+        for kind in range(3):
+            tables[a][kind].start()
+        locals_.append(pltpu.make_async_copy(pieces[a], slot(a, y, x, c), own_sem.at[a]))
+    for item in locals_:
+        item.start()
+    for a in range(count):
+        tables[a][0].wait_recv()
+        tables[a][3].start()
+        tables[a][5].start()
+        tables[a][1].wait_recv()
+        tables[a][4].start()
+        tables[a][6].start()
+    for a in range(count):
+        tables[a][3].wait_recv()
+        tables[a][7].start()
+        tables[a][4].wait_recv()
+        tables[a][8].start()
+    for a in range(count):
+        for kind in (2, 5, 6, 7, 8):
+            tables[a][kind].wait_recv()
+        for kind in range(9):
+            tables[a][kind].wait_send()
+    small_copy.wait()
+    for item in locals_:
+        item.wait()
+
+
+def gather_weights(pieces, small):
+    rows = pieces[0].shape[0]
+    widths = tuple(piece.shape[1] for piece in pieces)
+    outs = [jax.ShapeDtypeStruct((2, 2, rows, 2 * width), BF) for width in widths]
+    outs.append(jax.ShapeDtypeStruct((2 * small.shape[0], small.shape[1]), BF))
+    spec = pl.BlockSpec(memory_space=pl.ANY)
+    count = len(pieces)
+
+    def kernel(*refs):
+        ins, rest = refs[: count + 1], refs[count + 1 :]
+        gather_kernel(widths, *ins[:count], *rest[:count], ins[count], *rest[count:])
+
+    gathered = pl.pallas_call(
+        kernel,
+        out_shape=outs,
+        in_specs=[spec] * (count + 1),
+        out_specs=[spec] * (count + 1),
+        scratch_shapes=[
+            pltpu.SemaphoreType.DMA((count, 9)),
+            pltpu.SemaphoreType.DMA((count, 9)),
+            pltpu.SemaphoreType.DMA((count,)),
+            pltpu.SemaphoreType.DMA((3,)),
+        ],
+        compiler_params=pltpu.CompilerParams(collective_id=0, has_side_effects=True),
+        cost_estimate=pl.CostEstimate(flops=0, bytes_accessed=100000000, transcendentals=0),
+    )(*pieces, small)
+    return [full.reshape(4 * rows, full.shape[3]) for full in gathered[:count]], gathered[count]
+
+
+def add_lines(dst, first, second):
+    rows = dst.shape[0]
+    step = 48 if rows % 48 == 0 else 16
+
+    def body(i, carry):
+        lines = pl.ds(pl.multiple_of(i * step, 16), step)
+        dst[lines, :] = (first[lines, :].astype(F32) + second[lines, :].astype(F32)).astype(dst.dtype)
+        return carry
+
+    lax.fori_loop(0, rows // step, body, 0)
+
+
+def reduce_kernel(widths, chunks, *refs):
+    count, number = len(widths), len(chunks)
+    fulls, vector, outs, vector_out = refs[:count], refs[count], refs[count + 1 : 2 * count + 1], refs[2 * count + 1]
+    rest = refs[2 * count + 2 :]
+    by_core, by_x, by_y, plane, half_z, quarter_z, final = (rest[i * number : (i + 1) * number] for i in range(7))
+    vector_in, vector_sum, send, recv, vector_send, vector_recv = rest[7 * number :]
+    x, c, y, z = here()
+    low_z, high_z = z % 2, z // 2
+    at_x, at_y, at_c = {"shard": 2 * (1 - x) + c}, {"tp": 1 - y}, {"shard": 2 * x + 1 - c}
+    at_one, at_two = {"ctx": 2 * high_z + 1 - low_z}, {"ctx": 2 * (1 - high_z) + low_z}
+    greet((at_x, at_y, at_c, at_one, at_two))
+    half = fulls[0].shape[2] // 2
+    quarter = half // 2
+
+    def part(k, of_core, of_y):
+        a, first, width = chunks[k]
+        cols = pl.ds(pl.multiple_of(of_y * widths[a] + first, 128), width)
+        return fulls[a].at[:, of_core, :, cols]
+
+    def copies(k, stage):
+        if stage == 0:
+            table = [(part(k, 1 - c, of_y), by_core[k].at[of_y], at_c) for of_y in range(2)]
+        elif stage == 1:
+            table = [
+                (by_core[k].at[:, 1 - x, :half], by_x[k], at_x),
+                (by_core[k].at[1 - y, :, half:], by_y[k], at_y),
+            ]
+        elif stage == 2:
+            table = [(by_x[k].at[1 - y], plane[k].at[0], at_y), (by_y[k].at[1 - x], plane[k].at[1], at_x)]
+        elif stage == 3:
+            table = [(plane[k].at[1 - low_z], half_z[k], at_one)]
+        elif stage == 4:
+            lines = pl.ds(pl.multiple_of((1 - high_z) * quarter, 16), quarter)
+            table = [(half_z[k].at[lines], quarter_z[k], at_two)]
+        elif stage == 5:
+            mine = final[k].at[2 * low_z + high_z]
+            table = [(mine, mine, at_two)]
+        else:
+            mine = final[k].at[pl.ds(2 * low_z, 2)]
+            table = [(mine, mine, at_one)]
+        return [remote(s, d, send.at[k, stage, i], recv.at[k, stage, i], w) for i, (s, d, w) in enumerate(table)]
+
+    def absorb(k, stage):
+        if stage == 0:
+            for of_y in range(2):
+                mine = part(k, c, of_y)
+                for of_x in range(2):
+                    there = by_core[k].at[of_y, of_x]
+                    add_lines(there, there, mine.at[of_x])
+        elif stage == 1:
+            for i in range(2):
+                add_lines(by_x[k].at[i], by_x[k].at[i], by_core[k].at[i, x, pl.ds(0, half)])
+                add_lines(by_y[k].at[i], by_y[k].at[i], by_core[k].at[y, i, pl.ds(half, half)])
+        elif stage == 2:
+            add_lines(plane[k].at[0], plane[k].at[0], by_x[k].at[y])
+            add_lines(plane[k].at[1], plane[k].at[1], by_y[k].at[x])
+        elif stage == 3:
+            add_lines(half_z[k], half_z[k], plane[k].at[low_z])
+        elif stage == 4:
+            lines = pl.ds(pl.multiple_of(high_z * quarter, 16), quarter)
+            add_lines(final[k].at[2 * low_z + high_z], quarter_z[k], half_z[k].at[lines])
+        elif stage == 6:
+            a, first, width = chunks[k]
+            for i in range(4):
+                outs[a][i * quarter : (i + 1) * quarter, first : first + width] = final[k][i].astype(F32)
+
+    def vector_copy(stage):
+        where = (at_c, at_x, at_y, at_one, at_two)[stage]
+        return remote(vector_sum.at[stage], vector_in.at[stage], vector_send.at[stage], vector_recv.at[stage], where)
+
+    stages = 7
+    for k in range(number):
+        for item in copies(k, 0):
+            item.start()
+    vector_sum[0] = vector[...]
+    vector_copy(0).start()
+    for step in range(number + stages - 1):
+        for stage in reversed(range(stages)):
+            k = step - stage
+            if 0 <= k < number:
+                for item in copies(k, stage):
+                    item.wait_recv()
+                absorb(k, stage)
+                if stage + 1 < stages:
+                    for item in copies(k, stage + 1):
+                        item.start()
+        if step < 5:
+            vector_copy(step).wait_recv()
+            total = vector_sum[step] + vector_in[step]
+            if step < 4:
+                vector_sum[step + 1] = total
+                vector_copy(step + 1).start()
+            else:
+                vector_out[...] = total
+    for k in range(number):
+        for stage in range(stages):
+            for item in copies(k, stage):
+                item.wait_send()
+    for stage in range(5):
+        vector_copy(stage).wait_send()
+
+
+def reduce_grads(fulls, vector):
+    rows = fulls[0].shape[0] // 4
+    widths = tuple(full.shape[1] // 2 for full in fulls)
+    chunks = []
+    for a, width in enumerate(widths):
+        step = 768 if width % 768 == 0 else 384
+        chunks += [(a, first, step) for first in range(0, width, step)]
+    number = len(chunks)
+    spec = pl.BlockSpec(memory_space=pltpu.VMEM)
+    scratch = [pltpu.VMEM((2, 2, rows, width), BF) for _, _, width in chunks]
+    scratch += [pltpu.VMEM((2, rows // 2, width), BF) for _ in range(3) for _, _, width in chunks]
+    scratch += [pltpu.VMEM((rows // 2, width), BF) for _, _, width in chunks]
+    scratch += [pltpu.VMEM((rows // 4, width), BF) for _, _, width in chunks]
+    scratch += [pltpu.VMEM((4, rows // 4, width), BF) for _, _, width in chunks]
+    scratch += [pltpu.VMEM((5,) + vector.shape, F32), pltpu.VMEM((5,) + vector.shape, F32)]
+    scratch += [pltpu.SemaphoreType.DMA((number, 7, 2)), pltpu.SemaphoreType.DMA((number, 7, 2))]
+    scratch += [pltpu.SemaphoreType.DMA((5,)), pltpu.SemaphoreType.DMA((5,))]
+    outs = [jax.ShapeDtypeStruct((rows, width), F32) for width in widths]
+    outs.append(jax.ShapeDtypeStruct(vector.shape, F32))
+    result = pl.pallas_call(
+        functools.partial(reduce_kernel, widths, tuple(chunks)),
+        out_shape=outs,
+        in_specs=[spec] * (len(fulls) + 1),
+        out_specs=[spec] * len(outs),
+        scratch_shapes=scratch,
+        compiler_params=pltpu.CompilerParams(
+            collective_id=1, has_side_effects=True, vmem_limit_bytes=VMEM_LIMIT
+        ),
+        cost_estimate=pl.CostEstimate(flops=0, bytes_accessed=200000000, transcendentals=0),
+    )(*[full.reshape(2, 2, rows, full.shape[1]) for full in fulls], vector)
+    return result[:-1], result[-1]
+
+
+def slots_kernel(values, dealt_col, out, outgoing, blocks, acc, picked, sems, line_send, line_recv):
+    own, dim = values.shape
+    half, slots = dim // 2, 2 * own
+    x, c, y, z = here()
+    last = blocks.shape[0] - 1
+    at_y, at_left, at_right = {"tp": 1 - y}, {"ctx": jnp.maximum(z - 1, 0)}, {"ctx": jnp.minimum(z + 1, last)}
+    barrier = pltpu.get_barrier_semaphore()
+    pl.semaphore_signal(barrier, inc=1, device_id=at_y, device_id_type=pl.DeviceIdType.MESH)
+
+    @pl.when(z > 0)
+    def _():
+        pl.semaphore_signal(barrier, inc=1, device_id=at_left, device_id_type=pl.DeviceIdType.MESH)
+
+    @pl.when(z < last)
+    def _():
+        pl.semaphore_signal(barrier, inc=1, device_id=at_right, device_id_type=pl.DeviceIdType.MESH)
+
+    greetings = 1 + (z > 0).astype(jnp.int32) + (z < last).astype(jnp.int32)
+    pl.semaphore_wait(barrier, greetings)
+    mine_cols = pl.ds(pl.multiple_of(y * half, 128), half)
+    other_cols = pl.ds(pl.multiple_of((1 - y) * half, 128), half)
+    mine_rows = pl.ds(pl.multiple_of(y * own, 64), own)
+    outgoing[...] = values[:, other_cols]
+    first = remote(outgoing, blocks.at[z, mine_rows], sems.at[0], sems.at[1], at_y)
+    first.start()
+    blocks[z, mine_rows, :] = values[:, mine_cols]
+    first.wait_recv()
+
+    def to_right(block):
+        return remote(blocks.at[block], blocks.at[block], line_send.at[0, block], line_recv.at[block], at_right)
+
+    def to_left(block):
+        return remote(blocks.at[block], blocks.at[block], line_send.at[1, block], line_recv.at[block], at_left)
+
+    def select(block, start):
+        wide = 384 if slots % 384 == 0 else 128
+
+        def body(i, carry):
+            lines = pl.ds(pl.multiple_of(i * wide, 128), wide)
+            token = block * slots + lax.broadcasted_iota(jnp.int32, (wide, slots), 1)
+            chosen = jnp.where(dealt_col[lines, :] == token, 1.0, 0.0).astype(BF)
+            part = matmul(chosen, blocks[block])
+            acc[lines, :] = part if start else acc[lines, :] + part
+            return carry
+
+        lax.fori_loop(0, slots // wide, body, 0)
+
+    @pl.when(z < last)
+    def _():
+        to_right(z).start()
+
+    @pl.when(z > 0)
+    def _():
+        to_left(z).start()
+
+    select(z, True)
+    for distance in range(1, last + 1):
+        from_left, from_right = z - distance, z + distance
+
+        @pl.when(from_left >= 0)
+        def _():
+            to_right(from_left).wait_recv()
+
+            @pl.when(z < last)
+            def _():
+                to_right(from_left).start()
+
+        @pl.when(from_right <= last)
+        def _():
+            to_left(from_right).wait_recv()
+
+            @pl.when(z > 0)
+            def _():
+                to_left(from_right).start()
+
+        @pl.when(from_left >= 0)
+        def _():
+            select(from_left, False)
+
+        @pl.when(from_right <= last)
+        def _():
+            select(from_right, False)
+
+    picked[...] = acc[...].astype(BF)
+    back = remote(picked, out.at[:, mine_cols], sems.at[2], sems.at[3], at_y)
+    back.start()
+    out[:, mine_cols] = picked[...]
+    first.wait_send()
+    for block in range(last + 1):
+
+        @pl.when((z < last) & (block <= z))
+        def _():
+            to_right(block).wait_send()
+
+        @pl.when((z > 0) & (block >= z))
+        def _():
+            to_left(block).wait_send()
+
+    back.wait()
+
+
+def rows_to_slots_kernel(values, dealt, place_z):
+    own, dim = values.shape
+    slots = 2 * own
+    ctx_size = lax.axis_size("ctx")
+    mine = lax.dynamic_slice_in_dim(dealt, place_z * slots, slots)[:, None]
+    spec = pl.BlockSpec(memory_space=pltpu.VMEM)
+    return pl.pallas_call(
+        slots_kernel,
+        out_shape=jax.ShapeDtypeStruct((slots, dim), BF),
+        in_specs=[spec, spec],
+        out_specs=spec,
+        scratch_shapes=[
+            pltpu.VMEM((own, dim // 2), BF),
+            pltpu.VMEM((ctx_size, slots, dim // 2), BF),
+            pltpu.VMEM((slots, dim // 2), F32),
+            pltpu.VMEM((slots, dim // 2), BF),
+            pltpu.SemaphoreType.DMA((4,)),
+            pltpu.SemaphoreType.DMA((2, ctx_size)),
+            pltpu.SemaphoreType.DMA((ctx_size,)),
+        ],
+        compiler_params=pltpu.CompilerParams(
+            collective_id=2, has_side_effects=True, vmem_limit_bytes=VMEM_LIMIT
+        ),
+        cost_estimate=pl.CostEstimate(flops=4000000000, bytes_accessed=150000000, transcendentals=0),
+    )(values, mine)
+
+
+def project_kernel(dim, x_ref, weight, bias, out):
+    step = 256
+    third = weight.shape[1] // 3
+
+    def body(i, carry):
+        lines = pl.ds(pl.multiple_of(i * step, step), step)
+        value = (matmul(x_ref[lines, :], weight[...]) + bias[0]).astype(BF)
+        scale = jnp.where(lax.broadcasted_iota(jnp.int32, (1, 3 * third), 1) < third, 0.125, 1.0).astype(BF)
+        out[lines, :] = value * scale
+        return carry
+
+    lax.fori_loop(0, x_ref.shape[0] // step, body, 0)
+
+
+def project(x_window, weight, bias):
+    rows, dim = x_window.shape
+    width = 3 * dim // 2
+    return pl.pallas_call(
+        functools.partial(project_kernel, dim),
+        grid=(2,),
+        out_shape=jax.ShapeDtypeStruct((rows, 2 * width), BF),
+        in_specs=[
+            pl.BlockSpec((rows, dim), lambda i: (0, 0)),
+            pl.BlockSpec((dim, width), lambda i: (0, i)),
+            pl.BlockSpec((1, 1, width), lambda i: (i, 0, 0)),
+        ],
+        out_specs=pl.BlockSpec((rows, width), lambda i: (0, i)),
+        compiler_params=pltpu.CompilerParams(vmem_limit_bytes=VMEM_LIMIT),
+        cost_estimate=pl.CostEstimate(flops=6000000000, bytes_accessed=14000000, transcendentals=0),
+    )(x_window, weight, bias)
 
 
 def rows_to_slots(values, dealt, place_z, place_y):
@@ -335,7 +780,6 @@
     place_z, place_y = lax.axis_index("ctx"), lax.axis_index("tp")
     window = HALO + own + HALO
     padded = -(-window // BLOCK) * BLOCK
-    heads = dim // HEAD
     dealt = dealing[0]
 
     lengths = seq_lengths[0]
@@ -358,9 +802,30 @@
     shift = HALO - first_row
     bounds = jnp.stack([(begin + shift) // BLOCK, (finish + shift + BLOCK - 1) // BLOCK], axis=1).astype(jnp.int32)
 
-    def whole(weight, shard_axis):
-        once = lax.all_gather(weight, "shard", axis=shard_axis, tiled=True)
-        return lax.all_gather(once, "tp", axis=1 - shard_axis, tiled=True)
+    special = lax.axis_size("shard") == 4 and tp_size == 2 and ctx_size == 4
+    half_dim = dim // tp_size
+    pieces = [
+        jnp.concatenate([query_weight, key_weight, value_weight], axis=1),
+        output_weight.T,
+        up_weight,
+        down_weight.T,
+    ]
+    flat = jnp.concatenate([query_bias, value_bias, up_bias])
+    small = jnp.broadcast_to(flat[None, :], (16, flat.shape[0]))
+    if special:
+        whole, biases = gather_weights(pieces, small)
+    else:
+        whole = [
+            lax.all_gather(lax.all_gather(piece, "shard", axis=0, tiled=True), "tp", axis=1, tiled=True)
+            for piece in pieces
+        ]
+        biases = lax.all_gather(small, "tp", axis=0, tiled=True)
+    wide_qkv, wide_output, wide_up, wide_down = whole
+    biases = biases[::16].astype(F32)
+    qkv_bias = jnp.concatenate(
+        [biases[:, :half_dim], jnp.zeros((tp_size, half_dim), F32), biases[:, half_dim:dim]], axis=1
+    )[:, None, :]
+    whole_up_bias = biases[:, dim:].reshape(-1)
 
     edge = jnp.where(place_y == 0, tokens[rows - HALO :], tokens[:HALO])
     hops = [(2 * z, 2 * z + 2) for z in range(ctx_size - 1)] + [(2 * z + 1, 2 * z - 1) for z in range(1, ctx_size)]
@@ -373,12 +838,6 @@
     x_window = jnp.pad(x_window, ((0, padded - window), (0, 0)))
     inputs = lax.dynamic_slice_in_dim(tokens, place_y * own, own, axis=0)
 
-    wide_qkv = jnp.concatenate([whole(query_weight, 0), whole(key_weight, 0), whole(value_weight, 0)], axis=1)
-    wide_output = whole(output_weight, 1)
-    wide_up = whole(up_weight, 0)
-    wide_down = whole(down_weight, 1)
-    whole_bias = lax.all_gather(jnp.stack([query_bias, value_bias]), "tp", axis=1, tiled=True).astype(F32)
-    whole_up_bias = lax.all_gather(up_bias, "tp", axis=0, tiled=True).astype(F32)
     output_bias = output_bias.astype(F32)
     first_gain = first_gain.astype(F32)
     first_shift = first_shift.astype(F32)
@@ -386,26 +845,18 @@
     second_gain = second_gain.astype(F32)
     second_shift = second_shift.astype(F32)
 
-    raw = matmul(x_window, wide_qkv)
-    qkv = jnp.concatenate(
-        [
-            ((raw[:, :dim] + whole_bias[0]).astype(BF) * BF(0.125)),
-            raw[:, dim : 2 * dim].astype(BF),
-            (raw[:, 2 * dim :] + whole_bias[1]).astype(BF),
-        ],
-        axis=1,
-    )
+    qkv = project(x_window, wide_qkv, qkv_bias)
     attended, logsum = attention_forward(qkv, seg_col, seg_row, bounds, own, dim)
     grad_out = slots_to_rows(cotangent, dealt, place_z, place_y).astype(F32)
     hidden_one, normed_one, inverse_one = norm_forward(
-        inputs.astype(F32) + matmul(attended, wide_output) + output_bias, first_gain, first_shift
+        inputs.astype(F32) + matmul_second(attended, wide_output) + output_bias, first_gain, first_shift
     )
     hidden_low = hidden_one.astype(BF)
     pre_act = matmul(hidden_low, wide_up) + whole_up_bias
     erf_part = 0.5 * (1.0 + jax.scipy.special.erf(pre_act * HALF_ROOT))
     act_low = (pre_act * erf_part).astype(BF)
     layer_value, normed_two, inverse_two = norm_forward(
-        hidden_one + matmul(act_low, wide_down) + down_bias, second_gain, second_shift
+        hidden_one + matmul_second(act_low, wide_down) + down_bias, second_gain, second_shift
     )
     layer_out = rows_to_slots(layer_value.astype(BF), dealt, place_z, place_y)
 
@@ -415,7 +866,7 @@
     down_bias_grad = jnp.sum(grad_second, axis=0)
     second_low = grad_second.astype(BF)
     slope = erf_part + pre_act * DENSITY * jnp.exp(-0.5 * pre_act * pre_act)
-    grad_pre = matmul_second(second_low, wide_down) * slope
+    grad_pre = matmul(second_low, wide_down) * slope
     up_bias_grad = jnp.sum(grad_pre, axis=0)
     pre_low = grad_pre.astype(BF)
     grad_hidden = grad_second + matmul_second(pre_low, wide_up)
@@ -424,11 +875,11 @@
     grad_first = norm_backward(grad_hidden, normed_one, inverse_one, first_gain)
     output_bias_grad = jnp.sum(grad_first, axis=0)
     first_low = grad_first.astype(BF)
-    attended_grad = matmul_second(first_low, wide_output).astype(BF)
+    attended_grad = matmul(first_low, wide_output).astype(BF)
     delta = jnp.sum(
-        (attended_grad.astype(F32) * attended.astype(F32)).reshape(own, heads, HEAD), axis=2
-    )
-    delta = jnp.pad(delta, ((0, 0), (0, 128 - heads)))
+        (attended_grad.astype(F32) * attended.astype(F32)).reshape(own, dim // HEAD, HEAD), axis=2
+    )
+    delta = jnp.pad(delta, ((0, 0), (0, 128 - dim // HEAD)))
     up_hops = [(i, i + 1) for i in range(ctx_size * tp_size - 1)]
     down_hops = [(i + 1, i) for i in range(ctx_size * tp_size - 1)]
     both = ("ctx", "tp")
@@ -451,45 +902,46 @@
         ],
         axis=1,
     )
-    query_grad = attention_query(qkv, seg_col, seg_row, bounds, attended_grad, logsum, delta, dim)
-    pair_grad = attention_key(
-        qkv, seg_col, seg_row, bounds, grad_win, stats_win[:16], stats_win[16:], own, dim
-    )
-    query_bias_grad = jnp.sum(query_grad, axis=0)
-    value_bias_grad = jnp.sum(pair_grad[:, dim:], axis=0)
-    qkv_low = jnp.concatenate([query_grad.astype(BF), pair_grad.astype(BF)], axis=1)
+    query_low, query_bias_grad = attention_query(qkv, seg_col, seg_row, bounds, attended_grad, logsum, delta, dim)
+    qkv_low, value_bias_grad = attention_key(
+        qkv, seg_col, seg_row, bounds, grad_win, stats_win[:16], stats_win[16:], query_low, own, dim
+    )
     tokens_grad = (grad_first + matmul_second(qkv_low, wide_qkv)).astype(BF)
-    tokens_grad = rows_to_slots(tokens_grad, dealt, place_z, place_y)
-
-    def owned(full, shard_axis):
-        part = lax.psum_scatter(full.astype(BF), "tp", scatter_dimension=1 - shard_axis, tiled=True)
-        part = lax.psum_scatter(part, "shard", scatter_dimension=shard_axis, tiled=True)
-        return lax.psum(part, "ctx").astype(F32)
-
-    down_full = matmul_first(act_low, second_low)
-    up_full = matmul_first(hidden_low, pre_low)
-    output_full = matmul_first(attended, first_low)
-    qkv_full = matmul_first(inputs, qkv_low)
-    small = lax.psum(
-        jnp.concatenate(
-            [
-                query_bias_grad,
-                value_bias_grad,
-                up_bias_grad,
-                output_bias_grad,
-                first_gain_grad,
-                first_shift_grad,
-                down_bias_grad,
-                second_gain_grad,
-                second_shift_grad,
-            ]
-        ),
-        ("shard", "ctx", "tp"),
-    )
+    fulls = [
+        matmul_first(inputs, qkv_low).astype(BF),
+        matmul_first(first_low, attended).astype(BF),
+        matmul_first(hidden_low, pre_low).astype(BF),
+        matmul_first(second_low, act_low).astype(BF),
+    ]
+    vectors = jnp.concatenate(
+        [
+            query_bias_grad[0],
+            value_bias_grad[0],
+            up_bias_grad,
+            output_bias_grad,
+            first_gain_grad,
+            first_shift_grad,
+            down_bias_grad,
+            second_gain_grad,
+            second_shift_grad,
+        ]
+    )
+    if special:
+        owned, small_sum = reduce_grads(fulls, vectors.reshape(-1, 128))
+        small_sum = small_sum.reshape(-1)
+        tokens_grad = rows_to_slots_kernel(tokens_grad, dealt, place_z)
+    else:
+        owned = []
+        for full in fulls:
+            part = lax.psum_scatter(full, "tp", scatter_dimension=1, tiled=True)
+            part = lax.psum_scatter(part, "shard", scatter_dimension=0, tiled=True)
+            owned.append(lax.psum(part, "ctx").astype(F32))
+        small_sum = lax.psum(vectors, ("shard", "ctx", "tp"))
+        tokens_grad = rows_to_slots(tokens_grad, dealt, place_z, place_y)
     hidden = up_bias_grad.shape[0]
     sizes = [dim, dim, hidden] + [dim] * 6
     offsets = [sum(sizes[:i]) for i in range(len(sizes))]
-    parts = [small[o : o + s] for o, s in zip(offsets, sizes)]
+    parts = [small_sum[o : o + s] for o, s in zip(offsets, sizes)]
 
     def by_tp(vector):
         part = vector.shape[0] // tp_size
@@ -498,18 +950,18 @@
     return (
         layer_out,
         tokens_grad,
-        owned(qkv_full[:, :dim], 0),
+        owned[0][:, :half_dim],
         by_tp(parts[0]),
-        owned(qkv_full[:, dim : 2 * dim], 0),
-        owned(qkv_full[:, 2 * dim :], 0),
+        owned[0][:, half_dim : 2 * half_dim],
+        owned[0][:, 2 * half_dim :],
         by_tp(parts[1]),
-        owned(output_full, 1),
+        owned[1].T,
         parts[3],
         parts[4],
         parts[5],
-        owned(up_full, 0),
+        owned[2],
         by_tp(parts[2]),
-        owned(down_full, 1),
+        owned[3].T,
         parts[6],
         parts[7],
         parts[8],

time: 1100 us -> 595 us (0.54)
  waiting for transfers between devices: 660 us -> 30.4 us
  Pallas kernels: 73.1 us -> 373 us
  blocking collectives: 106 us -> 0 us
  local copies, waits for them, and re-layouts: 68.9 us -> 35.6 us
  other arithmetic: 56.2 us -> 28.9 us
    pallas_call x0 -> x4, Pallas kernels: none -> 307 us  [the longest x1 131 us: reduce_grads(): pl.pallas_call(functools.partial(reduce_kernel, widths, tuple(chunks)), o...]
    reduce_scatter x7 -> x0, waiting for transfers between devices: 169 us -> none  [the longest x4 109 us: owned(): lax.psum_scatter(part, 'shard', scatter_dimension=shard_axis, tiled=True)]
    all_gather x8 -> x0, waiting for transfers between devices: 130 us -> none  [the longest x6 130 us: whole(): return lax.all_gather(once, 'tp', axis=1 - shard_axis, tiled=True)]
    all_gather x2 -> x1, waiting for transfers between devices: 97.7 us -> 0.01 us  [rows_to_slots(): everything = lax.all_gather(block, 'ctx', axis=0, tiled=True)]
    psum x1 -> x0, waiting for transfers between devices: 86.8 us -> none  [owned(): return lax.psum(part, 'ctx').astype(F32)]
    psum x1 -> x0, blocking collectives: 55.4 us -> none  [per_device(): lax.psum(jnp.concatenate([query_bias_grad, value_bias_grad, up_bias_grad,...]
    all_gather x1, waiting for transfers between devices: 51.9 us -> 0.01 us  [slots_to_rows(): everything = lax.all_gather(block, 'ctx', axis=0, tiled=True)]
    unnamed x29 -> x2, waiting for transfers between devices: 50.9 us -> 0.03 us
  transfers between devices with their start and end apart: 34 -> 10, of which waited for: 20 -> 2; matrix products, arithmetic and copies ran while one was open for 15% -> 12% of each run, Pallas kernels for 7% -> 60%
where the time goes in v2:
time: 595 us; the launch traced here: 592 us
  Pallas kernels  373 us (63%)
  matrix products  65.7 us (11%)
  starting transfers between devices  42.4 us (7%)
  local copies, waits for them, and re-layouts  35.6 us (6%)
  waiting for transfers between devices  30.4 us (5%)
  other arithmetic  28.9 us (5%)
  between operations  15.5 us (3%)
    pallas_call x1, Pallas kernels, reduce_grads(): pl.pallas_call(functools.partial(reduce_kernel, widths, tuple(chunks)), o...  131 us
    pallas_call x1, Pallas kernels, rows_to_slots_kernel(): pl.pallas_call(slots_kernel, out_shape=jax.ShapeDtypeStruct((slots, dim),...  97.5 us
    pallas_call x3, Pallas kernels, vmem_call(): pl.pallas_call(kernel, out_shape=outs, in_specs=[pl.BlockSpec(memory_spac...  66.8 us
    pallas_call x1, Pallas kernels, gather_weights(): pl.pallas_call(kernel, out_shape=outs, in_specs=[spec] * (count + 1), out...  63.6 us
    dot_general x4, matrix products, matmul_first(): lax.dot_general(former, latter, (((0,), (0,)), ((), ())), preferred_eleme...  27.6 us
    ppermute x1, waiting for transfers between devices, rows_to_slots(): other = lax.ppermute(send, 'tp', [(0, 1), (1, 0)])  24.8 us
    dot_general x4, matrix products, matmul(): return jnp.dot(former, latter, preferred_element_type=F32)  23.9 us
    dot_general x4, matrix products, matmul_second(): lax.dot_general(former, latter, (((1,), (1,)), ((), ())), preferred_eleme...  14.3 us
  transfers between devices with their start and end apart: 10, of which 2 were waited for; matrix products, arithmetic and copies ran while one was open for 12% of the time, Pallas kernels for 60%

profile of v2, /device:TPU:0, one launch (start us, length us, event | category | flops | bytes accessed | tf_op | source)
XLA Modules:
  0.0 591.9 jit_solution(11721303660293039060)
XLA Ops:
  8.8 5.0 collective-permute-start
  19.7 63.6 %shard_map.314 = (bf16[2,2,192,2304]{3,2,1,0:T(8,128)(2,1)}, bf16[2,2,192,768]{3,2,1,0:T(8,128)(2,1)}, bf16[2,2,192,3072]{3,2,1,0:T(8,128)(2,1)}, bf16[2,2,192,3072]{3,2,1,0:T(8,128)(2,1)}, bf16[32,2304]{1,0:T(8,128)(2,1)}) custom-call(bf16[192,1152]{1,0:T(8,128)(2,1)} %pad_maximum_fusion.3.refs_0_, bf16[192,384]{1,0:T(8,128)(2,1)} %bitcast.74, ...), custom_call_target="tpu_custom_call" | custom-call | bytes 100000000 | tf_op jit(solution)/shard_map/pallas_call | solution.py:398
  95.8 14.2 %shard_map.315.qkv = bf16[1792,2304]{1,0:T(8,128)(2,1)} custom-call(bf16[1792,768]{1,0:T(8,128)(2,1)} %pad.8.x_ref, bf16[768,2304]{1,0:T(8,128)(2,1)} %bitcast.87, f32[2,1,1152]{2,1,0:T(1,128)} %broadcast_in_dim.94.bias), custom_call_target="tpu_custom_call" | custom-call | flops 6000000000 | bytes 14000000 | tf_op jit(solution)/shard_map/pallas_call | solution.py:707
  110.0 29.2 %shard_map.316 = (bf16[576,768]{1,0:T(8,128)(2,1)}, f32[576,128]{1,0:T(8,128)}) custom-call(s32[3,2]{1,0:T(4,128)} %pad_add_fusion.bounds, bf16[1792,2304]{1,0:T(8,128)(2,1)} %shard_map.315.qkv, s32[1792,1]{1,0:T(8,128)} %reshape_select_fusion.seg_col, s32[1,1792]{1,0:T(1,128)} %and_select_fusion.seg_row), custom_call_target="tpu_custom_call" | custom-call | flops 10000000000 | bytes 12000000 | tf_op jit(solution)/shard_map/pallas_call | solution.py:221
  141.8 6.4 %multiply_convert_fusion = (bf16[576,3072]{1,0:T(8,128)(2,1)S(1)}, f32[576,3072]{1,0:T(8,128)}) fusion(f32[3072]{0:T(1024)S(1)} %add.251, bf16[768,3072]{1,0:T(8,128)(2,1)S(1)} %bitcast.79, f32[576,768]{1,0:T(8,128)S(1)} %get-tuple-element.92, f32[768]{0:T(1024)S(1)} %convert_element_type.86, f32[576]{0:T(1024)S(1)} %add_rsqrt_fusion.1, ...), kind=kOutput, calls=%fused_computation.10 | convolution fusion | flops 2730737664 | bytes 17127936 | tf_op jit(solution)/shard_map/dot_general | solution.py:22
  150.0 3.8 fusion.53
  153.8 7.7 %fusion.8 = bf16[1152,384]{1,0:T(8,128)(2,1)S(1)} fusion(bf16[4608,384]{1,0:T(8,128)(2,1)} %all-gather.5.cloned.1.call-done, s32[4608]{0:T(1024)} %reduce.1, s32[1152]{0:T(1024)} %iota_add_fusion.1), kind=kOutput, calls=%fused_computation.15 | convolution fusion | flops 4082614272 | bytes 4446720 | tf_op jit(solution)/shard_map/dot_general | solution.py:22
  163.2 14.3 %collective-permute-start.3 = (bf16[576,384]{1,0:T(8,128)(2,1)}, bf16[576,384]{1,0:T(8,128)(2,1)}, u32[]{:S(2)}, u32[]{:S(2)}) collective-permute-start(bf16[576,384]{1,0:T(8,128)(2,1)} %constant_dynamic-slice_fusion), channel_id=1, source_target_pairs={{0,1},{1,0},{2,3},{3,2},{4,5},{5,4},{6,7},{7,6},{8,9},{9,8},{10,11... | collective-permute-start | bytes 1327112 | tf_op jit(solution)/shard_map/ppermute | solution.py:751
  179.8 5.6 collective-permute-done.3
  190.3 7.7 %fusion.54 = (f32[3072]{0:T(1024)S(1)}, bf16[576,3072]{1,0:T(8,128)(2,1)S(1)}) fusion(f32[576,3072]{1,0:T(8,128)S(1)} %copy-done.49, f32[3072]{0:T(1024)S(1)} %copy-done.36, bf16[768,3072]{1,0:T(8,128)(2,1)} %bitcast.83, f32[576,768]{1,0:T(8,128)S(1)} %get-tuple-element.58), kind=kOutput, calls=%fused_computation.149 | convolution fusion | flops 2739581952 | bytes 17129472 | tf_op jit(solution)/shard_map/dot_general | solution.py:22
  210.3 8.9 %convolution_convert_fusion.2 = bf16[768,3072]{1,0:T(8,128)(2,1)} fusion(bf16[576,3072]{1,0:T(8,128)(2,1)} %copy-done.51, f32[576,768]{1,0:T(8,128)} %copy-done.7, f32[768]{0:T(1024)S(1)} %copy-done.39, f32[576]{0:T(1024)S(1)} %copy-done.34, f32[576]{0:T(1024)S(1)} %broadcast_multiply_fusion.5, f32[768]{0:T(1024)S(1)} %copy-done.32), kind=kOutput, calls=%fused_computation.14 | convolution fusion | flops 2722480128 | bytes 10037760 | tf_op jit(solution)/shard_map/dot_general | solution.py:26
  221.1 18.0 %shard_map.317 = (bf16[576,768]{1,0:T(8,128)(2,1)}, f32[1,768]{1,0:T(1,128)}) custom-call(s32[3,2]{1,0:T(4,128)} %pad_add_fusion.bounds, bf16[1792,2304]{1,0:T(8,128)(2,1)} %shard_map.315.qkv, s32[1792,1]{1,0:T(8,128)} %reshape_select_fusion.seg_col, s32[1,1792]{1,0:T(1,128)} %and_select_fusion.seg_row, bf16[576,768]{1,0:T(8,128)(2,1)} %copy-done.3, ...), custom_call_target="tpu_custom_call" | custom-call | flops 15000000512 | bytes 12000000 | tf_op jit(solution)/shard_map/pallas_call | solution.py:221
  239.2 10.3 %collective-permute-start.6 = (f32[32,512]{1,0:T(8,128)S(1)}, f32[32,512]{1,0:T(8,128)S(1)}, u32[]{:S(2)}, u32[]{:S(2)}) collective-permute-start(f32[32,512]{1,0:T(8,128)S(1)} %get-tuple-element.78), channel_id=1, source_target_pairs={{0,1},{1,2},{2,3},{3,4},{4,5},{5,6},{6,7},{8,9},{9,10},{10,11},{11... | collective-permute-start | bytes 196616 | tf_op jit(solution)/shard_map/ppermute | solution.py:898
  250.8 5.4 collective-permute-start.4
  261.7 8.5 %convolution_convert_fusion.1 = bf16[768,3072]{1,0:T(8,128)(2,1)} fusion(bf16[576,3072]{1,0:T(8,128)(2,1)} %copy-done.50, f32[576,768]{1,0:T(8,128)} %copy-done.10), kind=kOutput, calls=%fused_computation.13 | convolution fusion | flops 2720710656 | bytes 10027008 | tf_op jit(solution)/shard_map/dot_general | solution.py:26
  270.3 24.8 %collective-permute-done.1 = bf16[576,384]{1,0:T(8,128)(2,1)S(1)} collective-permute-done((bf16[576,384]{1,0:T(8,128)(2,1)}, bf16[576,384]{1,0:T(8,128)(2,1)S(1)}, u32[]{:S(2)}, u32[]{:S(2)}) %collective-permute-start.1) | collective-permute-done | bytes 442400 | tf_op jit(solution)/shard_map/ppermute | solution.py:727
  296.3 3.9 convolution_convert_fusion.3
  301.1 4.6 maximum_maximum_fusion.grad
  305.7 19.6 %shard_map.318 = (bf16[576,2304]{1,0:T(8,128)(2,1)}, f32[1,768]{1,0:T(1,128)}) custom-call(s32[3,2]{1,0:T(4,128)} %pad_add_fusion.bounds, bf16[1792,2304]{1,0:T(8,128)(2,1)} %shard_map.315.qkv, s32[1792,1]{1,0:T(8,128)} %reshape_select_fusion.seg_col, s32[1,1792]{1,0:T(1,128)} %and_select_fusion.seg_row, bf16[1792,768]{1,0:T(8,128)(2,1)} %maximum_maximum_fusion.grad, ...), custom_call_target="tpu_custom_call" | custom-call | flops 20000000000 | bytes 12000000 | tf_op jit(solution)/shard_map/pallas_call | solution.py:221
  326.1 6.2 %convolution_convert_fusion = bf16[768,2304]{1,0:T(8,128)(2,1)} fusion(bf16[576,2304]{1,0:T(8,128)(2,1)} %get-tuple-element.41, bf16[1152,768]{1,0:T(8,128)(2,1)S(1)} %copy-done.2, s32[]{:T(128)S(6)} %select_n.126), kind=kOutput, calls=%fused_computation.12 | convolution fusion | flops 2040201216 | bytes 7077892 | tf_op jit(solution)/shard_map/dot_general | solution.py:26
  332.4 131.3 %shard_map.320 = (f32[192,1152]{1,0:T(8,128)}, f32[192,384]{1,0:T(8,128)}, f32[192,1536]{1,0:T(8,128)}, f32[192,1536]{1,0:T(8,128)}, f32[72,128]{1,0:T(8,128)}) custom-call(bf16[2,2,192,2304]{3,2,1,0:T(8,128)(2,1)} %bitcast.67, bf16[2,2,192,768]{3,2,1,0:T(8,128)(2,1)} %bitcast.71, bf16[2,2,192,3072]{3,2,1,0:T(8,128)(2,1)} %bitcast.65, ...), custom_call_target="tpu_custom_call" | custom-call | bytes 200000000 | tf_op jit(solution)/shard_map/pallas_call | solution.py:548
  463.8 4.9 add_convert_fusion.values
  468.7 6.4 %gather_fusion = bf16[1152,384]{1,0:T(8,128)(2,1)S(1)} fusion(bf16[4608,384]{1,0:T(8,128)(2,1)} %all-gather.3.cloned.1.call-done, s32[2048]{0:T(1024)S(1)} %copy-done.25), kind=kCustom, calls=%fused_computation | custom fusion | bytes 1774080 | tf_op jit(solution)/shard_map/jit(_take)/gather | solution.py:734
  479.1 97.5 %shard_map.319 = bf16[1152,768]{1,0:T(8,128)(2,1)} custom-call(bf16[576,768]{1,0:T(8,128)(2,1)} %add_convert_fusion.values, s32[1152,1]{1,0:T(8,128)} %copy.71.dealt_col), custom_call_target="tpu_custom_call" | custom-call | flops 4000000000 | bytes 150000000 | tf_op jit(solution)/shard_map/pallas_call | solution.py:669
  (239 shorter events, 68.6 us)
Async XLA Ops:
  7.2 146.6 %all-gather.5.cloned.1.call-start = ((), (), s32[]{:S(2)}) async-start(), calls=%async_computation.1 | async-start | bytes 4423680 | tf_op jit(solution)/shard_map/all_gather | solution.py:745
  8.8 84.5 %collective-permute-start = (bf16[512,768]{1,0:T(8,128)(2,1)S(1)}, bf16[512,768]{1,0:T(8,128)(2,1)S(1)}, u32[]{:S(2)}, u32[]{:S(2)}) collective-permute-start(bf16[512,768]{1,0:T(8,128)(2,1)S(1)} %slice_select_fusion), channel_id=1, source_target_pairs={{0,2},{2,4},{4,6},{3,1},{5,3},{7,5},{8,10},{10,12},{12,14},{11,9},... | collective-permute-start | bytes 2359304 | tf_op jit(solution)/shard_map/ppermute | solution.py:832
  14.9 453.8 %all-gather.3.cloned.1.call-start = ((), (), s32[]{:S(2)}) async-start(), calls=%async_computation | async-start | bytes 4423680 | tf_op jit(solution)/shard_map/all_gather | solution.py:731
  15.2 70.9 %copy-start.42 = (bf16[768]{0:T(1024)(128)(2,1)S(1)}, bf16[768]{0:T(1024)(128)(2,1)}, u32[]{:S(2)}) copy-start(bf16[768]{0:T(1024)(128)(2,1)} %param.29) | copy-start | bytes 4612
  15.2 70.9 %copy-start.43 = (bf16[768]{0:T(1024)(128)(2,1)S(1)}, bf16[768]{0:T(1024)(128)(2,1)}, u32[]{:S(2)}) copy-start(bf16[768]{0:T(1024)(128)(2,1)} %param.30) | copy-start | bytes 4612
  15.2 70.9 %copy-start.44 = (bf16[768]{0:T(1024)(128)(2,1)S(1)}, bf16[768]{0:T(1024)(128)(2,1)}, u32[]{:S(2)}) copy-start(bf16[768]{0:T(1024)(128)(2,1)} %param.31) | copy-start | bytes 4612
  15.3 72.3 %copy-start.26 = (s32[1,4608]{1,0:T(1,128)S(1)}, s32[1,4608]{1,0:T(1,128)}, u32[]{:S(2)}) copy-start(s32[1,4608]{1,0:T(1,128)} %param.22) | copy-start | bytes 55300
  17.1 76.0 %copy-start.2 = (bf16[1152,768]{1,0:T(8,128)(2,1)S(1)}, bf16[1152,768]{1,0:T(8,128)(2,1)}, u32[]{:S(2)}) copy-start(bf16[1152,768]{1,0:T(8,128)(2,1)} %param.19) | copy-start | bytes 5308420
  86.2 55.6 %copy-start.35 = (f32[3072]{0:T(1024)}, f32[3072]{0:T(1024)S(1)}, u32[]{:S(2)}) copy-start(f32[3072]{0:T(1024)S(1)} %add.251) | copy-start | bytes 36868
  86.2 62.0 %copy-start.31 = (f32[768]{0:T(1024)}, f32[768]{0:T(1024)S(1)}, u32[]{:S(2)}) copy-start(f32[768]{0:T(1024)S(1)} %convert_element_type.81) | copy-start | bytes 9220
  86.2 62.0 %copy-start.38 = (f32[768]{0:T(1024)}, f32[768]{0:T(1024)S(1)}, u32[]{:S(2)}) copy-start(f32[768]{0:T(1024)S(1)} %convert_element_type.86) | copy-start | bytes 9220
  95.8 45.9 %slice-start.1 = ((s8[4718592]{0:T(1024)(128)(4,1)}), s8[4194304]{0:T(1024)(128)(4,1)S(1)}, s32[]{:S(2)}) async-start(s8[4718592]{0:T(1024)(128)(4,1)} %bitcast.77), calls=%async_computation.3 | async-start | bytes 8388608
  110.0 31.7 %slice-start.2 = ((s8[4718592]{0:T(1024)(128)(4,1)}), s8[524288]{0:T(1024)(128)(4,1)S(1)}, s32[]{:S(2)}) async-start(s8[4718592]{0:T(1024)(128)(4,1)} %bitcast.77), calls=%async_computation.4 | async-start | bytes 1048576
  163.2 22.1 %collective-permute-start.3 = (bf16[576,384]{1,0:T(8,128)(2,1)}, bf16[576,384]{1,0:T(8,128)(2,1)}, u32[]{:S(2)}, u32[]{:S(2)}) collective-permute-start(bf16[576,384]{1,0:T(8,128)(2,1)} %constant_dynamic-slice_fusion), channel_id=1, source_target_pairs={{0,1},{1,0},{2,3},{3,2},{4,5},{5,4},{6,7},{7,6},{8,9},{9,8},{10,11... | collective-permute-start | bytes 1327112 | tf_op jit(solution)/shard_map/ppermute | solution.py:751
  221.1 36.4 %copy-start.9 = (bf16[576,768]{1,0:T(8,128)(2,1)S(1)}, bf16[576,768]{1,0:T(8,128)(2,1)}, u32[]{:S(2)}) copy-start(bf16[576,768]{1,0:T(8,128)(2,1)} %get-tuple-element.61) | copy-start | bytes 2654212
  239.2 61.0 %collective-permute-start.6 = (f32[32,512]{1,0:T(8,128)S(1)}, f32[32,512]{1,0:T(8,128)S(1)}, u32[]{:S(2)}, u32[]{:S(2)}) collective-permute-start(f32[32,512]{1,0:T(8,128)S(1)} %get-tuple-element.78), channel_id=1, source_target_pairs={{0,1},{1,2},{2,3},{3,4},{4,5},{5,6},{6,7},{8,9},{9,10},{10,11},{11... | collective-permute-start | bytes 196616 | tf_op jit(solution)/shard_map/ppermute | solution.py:898
  249.5 50.7 %collective-permute-start.7 = (f32[32,512]{1,0:T(8,128)S(1)}, f32[32,512]{1,0:T(8,128)S(1)}, u32[]{:S(2)}, u32[]{:S(2)}) collective-permute-start(f32[32,512]{1,0:T(8,128)S(1)} %get-tuple-element.77), channel_id=1, source_target_pairs={{1,0},{2,1},{3,2},{4,3},{5,4},{6,5},{7,6},{9,8},{10,9},{11,10},{12... | collective-permute-start | bytes 196616 | tf_op jit(solution)/shard_map/ppermute | solution.py:900
  250.8 50.2 %collective-permute-start.4 = (bf16[512,768]{1,0:T(8,128)(2,1)}, bf16[512,768]{1,0:T(8,128)(2,1)}, u32[]{:S(2)}, u32[]{:S(2)}) collective-permute-start(bf16[512,768]{1,0:T(8,128)(2,1)} %get-tuple-element.73), channel_id=1, source_target_pairs={{0,1},{1,2},{2,3},{3,4},{4,5},{5,6},{6,7},{8,9},{9,10},{10,11},{11... | collective-permute-start | bytes 2359304 | tf_op jit(solution)/shard_map/ppermute | solution.py:889
  256.3 44.8 %collective-permute-start.5 = (bf16[512,768]{1,0:T(8,128)(2,1)}, bf16[512,768]{1,0:T(8,128)(2,1)}, u32[]{:S(2)}, u32[]{:S(2)}) collective-permute-start(bf16[512,768]{1,0:T(8,128)(2,1)} %get-tuple-element.74), channel_id=1, source_target_pairs={{1,0},{2,1},{3,2},{4,3},{5,4},{6,5},{7,6},{9,8},{10,9},{11,10},{12... | collective-permute-start | bytes 2359304 | tf_op jit(solution)/shard_map/ppermute | solution.py:891
  258.4 36.7 %collective-permute-start.1 = (bf16[576,384]{1,0:T(8,128)(2,1)}, bf16[576,384]{1,0:T(8,128)(2,1)S(1)}, u32[]{:S(2)}, u32[]{:S(2)}) collective-permute-start(bf16[576,384]{1,0:T(8,128)(2,1)} %constant_dynamic-slice_fusion.2), channel_id=1, source_target_pairs={{0,1},{1,0},{2,3},{3,2},{4,5},{5,4},{6,7},{7,6},{8,9},{9,8},{10,11... | collective-permute-start | bytes 1327112 | tf_op jit(solution)/shard_map/ppermute | solution.py:727
  332.4 131.4 %copy-start.6 = (f32[576,768]{1,0:T(8,128)S(1)}, f32[576,768]{1,0:T(8,128)}, u32[]{:S(2)}) copy-start(f32[576,768]{1,0:T(8,128)} %copy-done.5) | copy-start | bytes 5308420
  332.4 131.4 %copy-start.47 = (bf16[2,2,192,2304]{3,2,1,0:T(8,128)(2,1)S(1)}, bf16[2,2,192,2304]{3,2,1,0:T(8,128)(2,1)}, u32[]{:S(2)}) copy-start(bf16[2,2,192,2304]{3,2,1,0:T(8,128)(2,1)} %get-tuple-element.33) | copy-start | bytes 10616836
  475.1 103.1 %collective-permute-start.2 = (bf16[1152,384]{1,0:T(8,128)(2,1)S(1)}, bf16[1152,384]{1,0:T(8,128)(2,1)S(1)}, u32[]{:S(2)}, u32[]{:S(2)}) collective-permute-start(bf16[1152,384]{1,0:T(8,128)(2,1)S(1)} %gather_fusion), channel_id=1, source_target_pairs={{0,1},{1,0},{2,3},{3,2},{4,5},{5,4},{6,7},{7,6},{8,9},{9,8},{10,11... | collective-permute-start | bytes 2654216 | tf_op jit(solution)/shard_map/ppermute | solution.py:735
  479.1 98.2 %copy-start.17 = (f32[192,1152]{1,0:T(8,128)S(1)}, f32[192,1152]{1,0:T(8,128)}, u32[]{:S(2)}) copy-start(f32[192,1152]{1,0:T(8,128)} %get-tuple-element.44) | copy-start | bytes 2654212
  (45 other events, 312.0 us)
Sparse Core Ops, SparseCore 0:
  15.0 72.9 all-gather.4
  296.4 81.7 all-gather.2

commit v3 on v2

v3 whole, which is shorter than its diff:
```python
import functools

import jax
import jax.numpy as jnp
from jax import lax
from jax.experimental import pallas as pl
from jax.experimental.pallas import tpu as pltpu
from jax.sharding import PartitionSpec as P

HEAD = 64
HALO = 512
HALF_ROOT = 0.7071067811865476
DENSITY = 0.3989422804014327
NEG_FILL = -1000000000.0
BF = jnp.bfloat16
F32 = jnp.float32
BLOCK = 256
VMEM_LIMIT = 56 * 1024 * 1024


def matmul(former, latter):
    return jnp.dot(former, latter, preferred_element_type=F32)


def matmul_first(former, latter):
    return lax.dot_general(former, latter, (((0,), (0,)), ((), ())), preferred_element_type=F32)


def matmul_second(former, latter):
    return lax.dot_general(former, latter, (((1,), (1,)), ((), ())), preferred_element_type=F32)


def norm_forward(values, norm_gain, norm_shift):
    centre = values - jnp.mean(values, axis=1, keepdims=True)
    spread = jnp.mean(centre * centre, axis=1, keepdims=True)
    inverse = lax.rsqrt(spread + 1e-06)
    normed = centre * inverse
    return (norm_gain * normed + norm_shift, normed, inverse)


def norm_backward(gradient, normed, inverse, norm_gain):
    scaled = gradient * norm_gain
    bracket = (
        scaled
        - jnp.mean(scaled, axis=1, keepdims=True)
        - normed * jnp.mean(scaled * normed, axis=1, keepdims=True)
    )
    return inverse * bracket


def places(pair, dim):
    half, inner = divmod(pair, dim // 256)
    base = half * (3 * dim // 2) + inner * 128
    return base, base + dim // 2, base + dim


def take(qkv, rows, pair, dim, which):
    first = places(pair, dim)[which]
    return qkv[rows, first : first + 128]


def low_lanes(rows):
    return lax.broadcasted_iota(jnp.int32, (rows, 128), 1) < HEAD


def stacked(pair):
    low = low_lanes(pair.shape[0])
    zero = jnp.zeros_like(pair)
    return jnp.concatenate([jnp.where(low, pair, zero), jnp.where(low, zero, pair)], axis=0)


def unstacked(both):
    rows = both.shape[0] // 2
    return jnp.where(low_lanes(rows), both[:rows], both[rows:])


def columns(ref_value, head, rows):
    return jnp.concatenate([ref_value[:, 2 * head : 2 * head + 1], ref_value[:, 2 * head + 1 : 2 * head + 2]], axis=0)


def bias_of(own_seg, other_seg):
    return jnp.where(own_seg == other_seg, 0.0, NEG_FILL)


def forward_kernel(dim, tile, bounds, qkv, seg_col, seg_row, out, logsum, query_st, bias_ref, acc, top, total):
    pairs = dim // 128
    own = out.shape[0]

    def one_tile(i, carry):
        first = pl.multiple_of(i * tile, tile)
        rows = pl.ds(pl.multiple_of(HALO + first, 64), tile)
        seg_here = seg_col[rows, :]
        for p in range(pairs):
            query_st[p] = stacked(take(qkv, rows, p, dim, 0))
        acc[...] = jnp.zeros_like(acc)
        total[...] = jnp.zeros_like(total)
        top[...] = jnp.full_like(top, 2 * NEG_FILL)

        def one_block(j, inner):
            start = pl.multiple_of(j * BLOCK, BLOCK)
            bias = bias_of(seg_here, seg_row[:, pl.ds(start, BLOCK)])
            bias_ref[...] = jnp.concatenate([bias, bias], axis=0)
            for p in range(pairs):
                key = take(qkv, pl.ds(start, BLOCK), p, dim, 1)
                value = take(qkv, pl.ds(start, BLOCK), p, dim, 2)
                scores = matmul_second(query_st[p], key) + bias_ref[...]
                old = top[p]
                new = jnp.maximum(old, jnp.max(scores, axis=1, keepdims=True))
                keep = jnp.exp(old - new)
                raised = jnp.exp(scores - new[:, :1])
                total[p] = keep * total[p] + jnp.sum(raised, axis=1, keepdims=True)
                acc[p] = keep * acc[p] + matmul(raised.astype(BF), value)
                top[p] = new
            return inner

        lax.fori_loop(bounds[i, 0], bounds[i, 1], one_block, 0)
        lane = lax.broadcasted_iota(jnp.int32, (tile, 128), 1)
        sums = jnp.zeros((tile, 128), F32)
        for p in range(pairs):
            whole = total[p]
            out[pl.ds(first, tile), p * 128 : p * 128 + 128] = unstacked(acc[p] / whole).astype(BF)
            lse = top[p] + jnp.log(whole)
            sums = jnp.where(lane == 2 * p, lse[:tile], sums)
            sums = jnp.where(lane == 2 * p + 1, lse[tile:], sums)
        logsum[pl.ds(first, tile), :] = sums
        return carry

    lax.fori_loop(0, own // tile, one_tile, 0)


def query_kernel(dim, tile, bounds, qkv, seg_col, seg_row, grad, stats, out, sums, query_st, grad_st, bias_ref, acc):
    pairs = dim // 128
    own = out.shape[0]

    def one_tile(i, carry):
        first = pl.multiple_of(i * tile, tile)
        own_rows = pl.ds(first, tile)
        rows = pl.ds(pl.multiple_of(HALO + first, 64), tile)
        seg_here = seg_col[rows, :]
        for p in range(pairs):
            query_st[p] = stacked(take(qkv, rows, p, dim, 0))
            grad_st[p] = stacked(grad[own_rows, p * 128 : p * 128 + 128])
        acc[...] = jnp.zeros_like(acc)

        def one_block(j, inner):
            start = pl.multiple_of(j * BLOCK, BLOCK)
            bias = bias_of(seg_here, seg_row[:, pl.ds(start, BLOCK)])
            bias_ref[...] = jnp.concatenate([bias, bias], axis=0)
            for p in range(pairs):
                key = take(qkv, pl.ds(start, BLOCK), p, dim, 1)
                value = take(qkv, pl.ds(start, BLOCK), p, dim, 2)
                scores = matmul_second(query_st[p], key) + bias_ref[...]
                probs = jnp.exp(scores - columns(stats[own_rows, :], p, tile))
                grad_probs = matmul_second(grad_st[p], value)
                grad_scores = (probs * (grad_probs - columns(stats[own_rows, :], p + 8, tile))).astype(BF)
                acc[p] += matmul(grad_scores, key)
            return inner

        lax.fori_loop(bounds[i, 0], bounds[i, 1], one_block, 0)
        for p in range(pairs):
            part = 0.125 * unstacked(acc[p])
            out[own_rows, p * 128 : p * 128 + 128] = part.astype(BF)
            sums[:, p * 128 : p * 128 + 128] += jnp.sum(part, axis=0, keepdims=True)
        return carry

    sums[...] = jnp.zeros_like(sums)
    lax.fori_loop(0, own // tile, one_tile, 0)


def key_kernel(dim, tile, bounds, qkv, seg_col, seg_row, grad, stats, query_low, out, sums, key_st, value_st, bias_ref, key_acc, value_acc, stats_t):
    pairs = dim // 128
    own = out.shape[0]

    def one_tile(i, carry):
        first = pl.multiple_of(i * tile, tile)
        own_rows = pl.ds(first, tile)
        rows = pl.ds(pl.multiple_of(HALO + first, 64), tile)
        seg_here = seg_col[rows, :]
        for p in range(pairs):
            key_st[p] = stacked(take(qkv, rows, p, dim, 1))
            value_st[p] = stacked(take(qkv, rows, p, dim, 2))
        key_acc[...] = jnp.zeros_like(key_acc)
        value_acc[...] = jnp.zeros_like(value_acc)

        def one_block(j, inner):
            start = pl.multiple_of(j * BLOCK, BLOCK)
            there = pl.ds(start, BLOCK)
            bias_ref[...] = bias_of(seg_here, seg_row[:, there])
            for p in range(pairs):
                query = take(qkv, there, p, dim, 0)
                grad_pair = grad[there, p * 128 : p * 128 + 128]
                scores = matmul_second(key_st[p], query)
                grad_probs = matmul_second(value_st[p], grad_pair)
                probs_all, grads_all = [], []
                for half in range(2):
                    head = 2 * p + half
                    lines = slice(half * tile, half * tile + tile)
                    probs = jnp.exp(scores[lines] + bias_ref[...] - stats_t[head : head + 1, there])
                    grads_all.append((probs * (grad_probs[lines] - stats_t[16 + head : 17 + head, there])).astype(BF))
                    probs_all.append(probs.astype(BF))
                key_acc[p] += matmul(jnp.concatenate(grads_all, axis=0), query)
                value_acc[p] += matmul(jnp.concatenate(probs_all, axis=0), grad_pair)
            return inner

        lax.fori_loop(bounds[i, 0], bounds[i, 1], one_block, 0)
        for p in range(pairs):
            at_query, at_key, at_value = places(p, dim)
            out[own_rows, at_query : at_query + 128] = query_low[own_rows, p * 128 : p * 128 + 128]
            out[own_rows, at_key : at_key + 128] = unstacked(key_acc[p]).astype(BF)
            part = unstacked(value_acc[p])
            out[own_rows, at_value : at_value + 128] = part.astype(BF)
            sums[:, p * 128 : p * 128 + 128] += jnp.sum(part, axis=0, keepdims=True)
        return carry

    stats_t[...] = stats[...].T
    sums[...] = jnp.zeros_like(sums)
    lax.fori_loop(0, own // tile, one_tile, 0)


def vmem_call(kernel, arrays, bounds, outs, scratch, flops):
    spec = pl.BlockSpec(memory_space=pltpu.VMEM)
    return pl.pallas_call(
        kernel,
        out_shape=outs,
        in_specs=[pl.BlockSpec(memory_space=pltpu.SMEM)] + [spec] * len(arrays),
        out_specs=jax.tree.map(lambda leaf: spec, outs),
        scratch_shapes=scratch,
        compiler_params=pltpu.CompilerParams(vmem_limit_bytes=VMEM_LIMIT),
        cost_estimate=pl.CostEstimate(flops=flops, bytes_accessed=12000000, transcendentals=6000000),
    )(bounds, *arrays)


def attention_tile(own):
    for tile in (192, 128, 64, 32, 16):
        if own % tile == 0:
            return tile
    raise ValueError("rows")


def attention_forward(qkv, seg_col, seg_row, bounds, own, dim):
    tile = attention_tile(own)
    pairs = dim // 128
    return vmem_call(
        functools.partial(forward_kernel, dim, tile),
        (qkv, seg_col, seg_row),
        bounds,
        (jax.ShapeDtypeStruct((own, dim), BF), jax.ShapeDtypeStruct((own, 128), F32)),
        [
            pltpu.VMEM((pairs, 2 * tile, 128), BF),
            pltpu.VMEM((2 * tile, BLOCK), F32),
            pltpu.VMEM((pairs, 2 * tile, 128), F32),
            pltpu.VMEM((pairs, 2 * tile, 128), F32),
            pltpu.VMEM((pairs, 2 * tile, 128), F32),
        ],
        10_000_000_000,
    )


def attention_query(qkv, seg_col, seg_row, bounds, grad, stats, dim):
    own = grad.shape[0]
    tile = attention_tile(own)
    pairs = dim // 128
    return vmem_call(
        functools.partial(query_kernel, dim, tile),
        (qkv, seg_col, seg_row, grad, stats),
        bounds,
        (jax.ShapeDtypeStruct((own, dim), BF), jax.ShapeDtypeStruct((1, dim), F32)),
        [
            pltpu.VMEM((pairs, 2 * tile, 128), BF),
            pltpu.VMEM((pairs, 2 * tile, 128), BF),
            pltpu.VMEM((2 * tile, BLOCK), F32),
            pltpu.VMEM((pairs, 2 * tile, 128), F32),
        ],
        15_000_000_000,
    )


def attention_key(qkv, seg_col, seg_row, bounds, grad_win, stats_win, query_low, own, dim):
    tile = attention_tile(own)
    pairs = dim // 128
    return vmem_call(
        functools.partial(key_kernel, dim, tile),
        (qkv, seg_col, seg_row, grad_win, stats_win, query_low),
        bounds,
        (jax.ShapeDtypeStruct((own, 3 * dim), BF), jax.ShapeDtypeStruct((1, dim), F32)),
        [
            pltpu.VMEM((pairs, 2 * tile, 128), BF),
            pltpu.VMEM((pairs, 2 * tile, 128), BF),
            pltpu.VMEM((tile, BLOCK), F32),
            pltpu.VMEM((pairs, 2 * tile, 128), F32),
            pltpu.VMEM((pairs, 2 * tile, 128), F32),
            pltpu.VMEM((128, qkv.shape[0]), F32),
        ],
        20_000_000_000,
    )


def remote(src, dst, send_sem, recv_sem, where):
    return pltpu.make_async_remote_copy(
        src_ref=src,
        dst_ref=dst,
        send_sem=send_sem,
        recv_sem=recv_sem,
        device_id=where,
        device_id_type=pl.DeviceIdType.MESH,
    )


def here():
    shard, z, y = lax.axis_index("shard"), lax.axis_index("ctx"), lax.axis_index("tp")
    return shard // 2, shard % 2, y, z


def interleave(tasks):
    running, turn = [], 0
    while tasks or running:
        running += [task for first, task in tasks if first <= turn]
        tasks = [item for item in tasks if item[0] > turn]
        alive = []
        for task in running:
            try:
                next(task)
                alive.append(task)
            except StopIteration:
                pass
        running, turn = alive, turn + 1


def greet_all(always, sometimes):
    barrier = pltpu.get_barrier_semaphore()
    number = jnp.int32(len(always))
    for peer in always:
        pl.semaphore_signal(barrier, inc=1, device_id=peer, device_id_type=pl.DeviceIdType.MESH)
    for condition, peer in sometimes:

        @pl.when(condition)
        def _():
            pl.semaphore_signal(barrier, inc=1, device_id=peer, device_id_type=pl.DeviceIdType.MESH)

        number = number + condition.astype(jnp.int32)
    pl.semaphore_wait(barrier, number)


class Line:
    SCRATCH = 4

    def __init__(self, z, dealt, to_slots, refs, sems):
        self.z, self.dealt, self.to_slots = z, dealt, to_slots
        self.blocks, self.picked, self.away, self.arrived = refs
        self.send, self.block_recv, self.away_recv = sems
        self.inner = (z == 1) | (z == 2)
        self.outer = (z == 0) | (z == 3)
        self.near = 1 + z // 3
        self.end = jnp.maximum(3 * (z - 1), 0) % 6
        self.middle = 3 - z
        self.far = 3 - self.end
        self.slots = refs[0].shape[1]

    def copy(self, what):
        if what == "own_near":
            block, where, sem = self.z, self.near, 0
        elif what == "own_middle":
            block, where, sem = self.z, self.middle, 0
        elif what == "forward":
            block, where, sem = self.end, self.middle, 1
        else:
            where = self.end
            return remote(self.away, self.arrived, self.send.at[2], self.away_recv, {"ctx": where})
        there = self.blocks.at[block]
        return remote(there, there, self.send.at[sem], self.block_recv.at[block], {"ctx": where})

    def wait_block(self, block):
        there = self.blocks.at[block]
        remote(there, there, self.send.at[0], self.block_recv.at[block], {"ctx": self.middle}).wait_recv()

    def select(self, target, wanted_by, block, start):
        slots = self.slots
        wide = 384 if slots % 384 == 0 else 128

        def body(i, carry):
            lines = pl.ds(pl.multiple_of(i * wide, 128), wide)
            if self.to_slots:
                wanted = self.dealt[pl.ds(pl.multiple_of(wanted_by * slots + i * wide, 128), wide), :]
                offered = block * slots + lax.broadcasted_iota(jnp.int32, (wide, slots), 1)
            else:
                wanted = wanted_by * slots + i * wide + lax.broadcasted_iota(jnp.int32, (wide, slots), 0)
                offered = self.dealt[:, pl.ds(pl.multiple_of(block * slots, 128), slots)]
            chosen = jnp.where(wanted == offered, 1.0, 0.0).astype(BF)
            part = matmul(chosen, self.blocks[block]).astype(BF)
            target[lines, :] = part if start else target[lines, :] + part
            return carry

        lax.fori_loop(0, slots // wide, body, 0)

    def run(self):
        @pl.when(self.outer)
        def _():
            self.copy("own_near").start()

        @pl.when(self.inner)
        def _():
            self.copy("own_middle").start()

        self.select(self.picked, self.z, self.z, True)
        yield

        @pl.when(self.inner)
        def _():
            self.wait_block(self.end)
            self.copy("forward").start()
            self.select(self.picked, self.z, self.end, False)
            self.select(self.away, self.end, self.z, True)

        yield

        @pl.when(self.inner)
        def _():
            self.wait_block(self.middle)
            self.select(self.away, self.end, self.middle, False)
            self.select(self.picked, self.z, self.middle, False)

        yield

        @pl.when(self.inner)
        def _():
            self.wait_block(self.far)
            self.select(self.away, self.end, self.far, False)
            self.copy("away").start()
            self.select(self.picked, self.z, self.far, False)

        yield

        @pl.when(self.outer)
        def _():
            self.copy("away").wait_recv()
            self.picked[...] = self.picked[...] + self.arrived[...]

    def settle(self):
        @pl.when(self.outer)
        def _():
            self.copy("own_near").wait_send()

        @pl.when(self.inner)
        def _():
            self.copy("own_middle").wait_send()
            self.copy("forward").wait_send()
            self.copy("away").wait_send()


def line_scratch(ctx_size, slots, chunks, columns):
    blocks = [pltpu.VMEM((ctx_size, slots, columns), BF) for _ in range(chunks)]
    others = [pltpu.VMEM((slots, columns), BF) for _ in range(3 * chunks)]
    sems = [pltpu.SemaphoreType.DMA((chunks, 3)), pltpu.SemaphoreType.DMA((chunks, ctx_size)), pltpu.SemaphoreType.DMA((chunks,))]
    return blocks + others + sems


def line_of(j, chunks, z, dealt, to_slots, refs):
    blocks, others, sems = refs[:chunks], refs[chunks : 4 * chunks], refs[4 * chunks :]
    return Line(
        z,
        dealt,
        to_slots,
        (blocks[j], others[3 * j], others[3 * j + 1], others[3 * j + 2]),
        (sems[0].at[j], sems[1].at[j], sems[2].at[j]),
    )


PERM = 3


def first_kernel(widths, padded, *refs):
    count = len(widths)
    pieces, (small, tokens, cotangent, dealt_row) = refs[:count], refs[count : count + 4]
    wholes, (small_whole, qkv, cot_rows) = refs[count + 4 : 2 * count + 4], refs[2 * count + 4 : 2 * count + 7]
    rest = refs[2 * count + 7 :]
    weight, window, send, recv, own_sem, small_sem, halo_sem, post_send, post_recv, bring = rest[:10]
    line_refs = rest[10:]
    x, c, y, z = here()
    rows, dim = tokens.shape
    own = rows // 2
    half = dim // 2
    last = 3
    at_x, at_y, at_c = {"shard": 2 * (1 - x) + c}, {"tp": 1 - y}, {"shard": 2 * x + 1 - c}
    left, right = {"ctx": jnp.maximum(z - 1, 0)}, {"ctx": jnp.minimum(z + 1, last)}
    greet_all((at_x, at_y, at_c), ((z > 0, left), (z < last, right)))

    def slot(a, of_y, of_x, of_c, lines=None):
        cols = pl.ds(pl.multiple_of(of_y * widths[a], 128), widths[a])
        depth = wholes[a].shape[2]
        lines = slice(0, depth) if lines is None else slice(lines * depth // 2, (lines + 1) * depth // 2)
        return (weight if a == 0 else wholes[a]).at[of_x, of_c, lines, cols]

    def moves(a):
        table = [
            (pieces[a], slot(a, y, x, c), at_x),
            (pieces[a], slot(a, y, x, c), at_y),
            (pieces[a], slot(a, y, x, c), at_c),
            (slot(a, y, 1 - x, c, 0), slot(a, y, 1 - x, c, 0), at_y),
            (slot(a, 1 - y, x, c, 1), slot(a, 1 - y, x, c, 1), at_x),
            (slot(a, y, 1 - x, c), slot(a, y, 1 - x, c), at_c),
            (slot(a, 1 - y, x, c), slot(a, 1 - y, x, c), at_c),
            (slot(a, 1 - y, 1 - x, c, 0), slot(a, 1 - y, 1 - x, c, 0), at_c),
            (slot(a, 1 - y, 1 - x, c, 1), slot(a, 1 - y, 1 - x, c, 1), at_c),
        ]
        return [remote(s, d, send.at[a, kind], recv.at[a, kind], w) for kind, (s, d, w) in enumerate(table)]

    tables = [moves(a) for a in range(count)]
    depth = small_whole.shape[0] // 2
    small_at = small_whole.at[pl.ds(pl.multiple_of(y * depth, 16), depth)]
    small_copy = remote(small, small_at, small_sem.at[0], small_sem.at[1], at_y)
    sends_right, sends_left = (y == 0) & (z < last), (y == 1) & (z > 0)
    gets_left, gets_right = (y == 0) & (z > 0), (y == 1) & (z < last)

    def halo(where):
        src = tokens.at[pl.ds(pl.multiple_of((1 - y) * (rows - HALO), 64), HALO)]
        dst = window.at[pl.ds(pl.multiple_of(y * (HALO + own), 64), HALO)]
        return remote(src, dst, halo_sem.at[0], halo_sem.at[1], where)

    inside = pltpu.make_async_copy(
        tokens.at[pl.ds(pl.multiple_of(y * (own - HALO), 64), own + HALO)],
        window.at[pl.ds(pl.multiple_of((1 - y) * HALO, 64), own + HALO)],
        halo_sem.at[2],
    )
    small_local = pltpu.make_async_copy(small, small_at, small_sem.at[2])
    piece_local = [pltpu.make_async_copy(pieces[a], slot(a, y, x, c), own_sem.at[a]) for a in range(count)]
    lines = [line_of(j, PERM, z, dealt_row, False, line_refs) for j in range(PERM)]

    def columns_of(j):
        return pl.ds(pl.multiple_of(y * half + j * (half // PERM), 128), half // PERM)

    bring_cot = [
        pltpu.make_async_copy(cotangent.at[:, columns_of(j)], lines[j].blocks.at[z], bring.at[j]) for j in range(PERM)
    ]
    for kind in range(3):
        tables[0][kind].start()
    small_copy.start()

    @pl.when(sends_right)
    def _():
        halo(right).start()

    @pl.when(sends_left)
    def _():
        halo(left).start()

    for item in (small_local, *piece_local, inside, *bring_cot):
        item.start()
    window[padded - (padded - 2 * HALO - own) :, :] = jnp.zeros((padded - 2 * HALO - own, dim), BF)

    @pl.when((y == 0) & (z == 0))
    def _():
        window[:HALO, :] = jnp.zeros((HALO, dim), BF)

    @pl.when((y == 1) & (z == last))
    def _():
        window[HALO + own : 2 * HALO + own, :] = jnp.zeros((HALO, dim), BF)

    def weights_task(a):
        if a:
            for kind in range(3):
                tables[a][kind].start()
            yield
        tables[a][0].wait_recv()
        tables[a][3].start()
        tables[a][5].start()
        tables[a][1].wait_recv()
        tables[a][4].start()
        tables[a][6].start()
        yield
        tables[a][3].wait_recv()
        tables[a][7].start()
        tables[a][4].wait_recv()
        tables[a][8].start()
        yield
        for kind in (2, 5, 6, 7, 8):
            tables[a][kind].wait_recv()
        if a == 0:
            yield from project_task()

    def project_task():
        piece_local[0].wait()
        pltpu.make_async_copy(weight, wholes[0], own_sem.at[0]).start()
        inside.wait()
        small_copy.wait()
        small_local.wait()

        @pl.when(gets_left | gets_right)
        def _():
            halo(left).wait_recv()

        depth_w, width = weight.shape[2], widths[0]
        third = width // 3
        step = 256
        for of_y in range(2):
            bias = small_whole[of_y * depth : of_y * depth + 1, :].astype(F32)
            bias = jnp.concatenate([bias[:, :third], jnp.zeros((1, third), F32), bias[:, third : 2 * third]], axis=1)
            scale = jnp.where(lax.broadcasted_iota(jnp.int32, (1, width), 1) < third, 0.125, 1.0).astype(BF)
            full = jnp.concatenate(
                [weight[i // 2, i % 2, :, of_y * width : (of_y + 1) * width] for i in range(4)], axis=0
            )

            def body(i, carry):
                there = pl.ds(pl.multiple_of(i * step, step), step)
                value = (matmul(window[there, :], full) + bias).astype(BF)
                qkv[there, of_y * width : (of_y + 1) * width] = value * scale
                return carry

            lax.fori_loop(0, padded // step, body, 0)
            yield

    def post(j):
        there = lines[j].picked.at[pl.ds(pl.multiple_of((1 - y) * own, 64), own)]
        return remote(there, cot_rows.at[:, columns_of(j)], post_send.at[j], post_recv.at[j], at_y)

    def cotangent_task(j):
        bring_cot[j].wait()
        yield from lines[j].run()
        post(j).start()
        cot_rows[:, columns_of(j)] = lines[j].picked[pl.ds(pl.multiple_of(y * own, 64), own), :]
        yield
        post(j).wait_recv()

    tasks = [(a, weights_task(a)) for a in range(count)] + [(1 + j, cotangent_task(j)) for j in range(PERM)]
    interleave(sorted(tasks, key=lambda item: item[0]))
    for a in range(count):
        for kind in range(9):
            tables[a][kind].wait_send()
        if a:
            piece_local[a].wait()
    pltpu.make_async_copy(weight, wholes[0], own_sem.at[0]).wait()

    @pl.when(sends_right | sends_left)
    def _():
        halo(left).wait_send()

    for j in range(PERM):
        lines[j].settle()
        post(j).wait_send()


def first_stage(pieces, small, tokens, cotangent, dealt, padded):
    rows, dim = tokens.shape
    depth = pieces[0].shape[0]
    own = rows // 2
    widths = tuple(piece.shape[1] for piece in pieces)
    count = len(pieces)
    ctx_size = lax.axis_size("ctx")
    outs = [jax.ShapeDtypeStruct((2, 2, depth, 2 * width), BF) for width in widths]
    outs += [
        jax.ShapeDtypeStruct((2 * small.shape[0], small.shape[1]), BF),
        jax.ShapeDtypeStruct((padded, 3 * dim), BF),
        jax.ShapeDtypeStruct((own, dim), BF),
    ]
    anywhere, vmem = pl.BlockSpec(memory_space=pl.ANY), pl.BlockSpec(memory_space=pltpu.VMEM)
    result = pl.pallas_call(
        functools.partial(first_kernel, widths, padded),
        out_shape=outs,
        in_specs=[anywhere] * (count + 3) + [vmem],
        out_specs=[anywhere] * count + [vmem] * 3,
        scratch_shapes=[
            pltpu.VMEM((2, 2, depth, 2 * widths[0]), BF),
            pltpu.VMEM((padded, dim), BF),
            pltpu.SemaphoreType.DMA((count, 9)),
            pltpu.SemaphoreType.DMA((count, 9)),
            pltpu.SemaphoreType.DMA((count,)),
            pltpu.SemaphoreType.DMA((3,)),
            pltpu.SemaphoreType.DMA((3,)),
            pltpu.SemaphoreType.DMA((PERM,)),
            pltpu.SemaphoreType.DMA((PERM,)),
            pltpu.SemaphoreType.DMA((PERM,)),
        ]
        + line_scratch(ctx_size, rows, PERM, dim // 2 // PERM),
        compiler_params=pltpu.CompilerParams(
            collective_id=0, has_side_effects=True, vmem_limit_bytes=VMEM_LIMIT
        ),
        cost_estimate=pl.CostEstimate(flops=10000000000, bytes_accessed=100000000, transcendentals=0),
    )(*pieces, small, tokens, cotangent, dealt[None, :])
    whole = [full.reshape(4 * depth, full.shape[3]) for full in result[:count]]
    return whole, result[count], result[count + 1], result[count + 2]


def add_lines(dst, first, second):
    rows = dst.shape[0]
    step = 48 if rows % 48 == 0 else 16

    def body(i, carry):
        lines = pl.ds(pl.multiple_of(i * step, 16), step)
        dst[lines, :] = (first[lines, :].astype(F32) + second[lines, :].astype(F32)).astype(dst.dtype)
        return carry

    lax.fori_loop(0, rows // step, body, 0)


class Reduction:
    def __init__(self, chunks, outs, refs):
        number = len(chunks)
        self.chunks, self.outs = chunks, outs
        self.full, self.by_core, self.by_x, self.by_y, self.plane, self.half_z, self.quarter_z, self.final = (
            refs[i * number : (i + 1) * number] for i in range(8)
        )
        self.send, self.recv = refs[8 * number :]
        self.place = here()
        self.rows = self.full[0].shape[3]

    def peers(self):
        x, c, y, z = self.place
        low, high = z % 2, z // 2
        return (
            {"shard": 2 * x + 1 - c},
            {"shard": 2 * (1 - x) + c},
            {"tp": 1 - y},
            {"ctx": 2 * high + 1 - low},
            {"ctx": 2 * (1 - high) + low},
        )

    def copies(self, k, stage):
        x, c, y, z = self.place
        low, high = z % 2, z // 2
        at_c, at_x, at_y, at_one, at_two = self.peers()
        half, quarter = self.rows // 2, self.rows // 4
        if stage == 0:
            table = [(self.full[k].at[:, :, 1 - c], self.by_core[k], at_c)]
        elif stage == 1:
            table = [
                (self.by_core[k].at[:, 1 - x, :half], self.by_x[k], at_x),
                (self.by_core[k].at[1 - y, :, half:], self.by_y[k], at_y),
            ]
        elif stage == 2:
            table = [
                (self.by_x[k].at[1 - y], self.plane[k].at[0], at_y),
                (self.by_y[k].at[1 - x], self.plane[k].at[1], at_x),
            ]
        elif stage == 3:
            table = [(self.plane[k].at[1 - low], self.half_z[k], at_one)]
        elif stage == 4:
            lines = pl.ds(pl.multiple_of((1 - high) * quarter, 16), quarter)
            table = [(self.half_z[k].at[lines], self.quarter_z[k], at_two)]
        elif stage == 5:
            mine = self.final[k].at[2 * low + high]
            table = [(mine, mine, at_two)]
        else:
            mine = self.final[k].at[pl.ds(2 * low, 2)]
            table = [(mine, mine, at_one)]
        return [
            remote(s, d, self.send.at[k, stage, i], self.recv.at[k, stage, i], w) for i, (s, d, w) in enumerate(table)
        ]

    def absorb(self, k, stage):
        x, c, y, z = self.place
        low, high = z % 2, z // 2
        half, quarter = self.rows // 2, self.rows // 4
        if stage == 0:
            for of_y in range(2):
                for of_x in range(2):
                    there = self.by_core[k].at[of_y, of_x]
                    add_lines(there, there, self.full[k].at[of_y, of_x, c])
        elif stage == 1:
            for i in range(2):
                add_lines(self.by_x[k].at[i], self.by_x[k].at[i], self.by_core[k].at[i, x, pl.ds(0, half)])
                add_lines(self.by_y[k].at[i], self.by_y[k].at[i], self.by_core[k].at[y, i, pl.ds(half, half)])
        elif stage == 2:
            add_lines(self.plane[k].at[0], self.plane[k].at[0], self.by_x[k].at[y])
            add_lines(self.plane[k].at[1], self.plane[k].at[1], self.by_y[k].at[x])
        elif stage == 3:
            add_lines(self.half_z[k], self.half_z[k], self.plane[k].at[low])
        elif stage == 4:
            lines = pl.ds(pl.multiple_of(high * quarter, 16), quarter)
            add_lines(self.final[k].at[2 * low + high], self.quarter_z[k], self.half_z[k].at[lines])
        elif stage == 6:
            a, first, width = self.chunks[k]
            for i in range(4):
                self.outs[a][i * quarter : (i + 1) * quarter, first : first + width] = self.final[k][i].astype(F32)

    def task(self, k, produce):
        produce(k)
        for stage in range(7):
            for item in self.copies(k, stage):
                item.start()
            yield
            for item in self.copies(k, stage):
                item.wait_recv()
            self.absorb(k, stage)

    def settle(self):
        for k in range(len(self.chunks)):
            for stage in range(7):
                for item in self.copies(k, stage):
                    item.wait_send()

    def product(self, k, turned, other, half_columns):
        _, first, width = self.chunks[k]
        for of_y in range(2):
            right = other[:, of_y * half_columns + first : of_y * half_columns + first + width]
            for i in range(4):
                value = matmul(turned[i * self.rows : (i + 1) * self.rows, :], right)
                self.full[k][of_y, i // 2, i % 2] = value.astype(BF)


def reduction_scratch(rows, chunks):
    shapes = [
        lambda w: (2, 2, 2, rows, w),
        lambda w: (2, 2, rows, w),
        lambda w: (2, rows // 2, w),
        lambda w: (2, rows // 2, w),
        lambda w: (2, rows // 2, w),
        lambda w: (rows // 2, w),
        lambda w: (rows // 4, w),
        lambda w: (4, rows // 4, w),
    ]
    scratch = [pltpu.VMEM(shape(width), BF) for shape in shapes for _, _, width in chunks]
    return scratch + [pltpu.SemaphoreType.DMA((len(chunks), 7, 2)), pltpu.SemaphoreType.DMA((len(chunks), 7, 2))]


CHUNK = 384


def chunks_of(widths):
    return tuple((a, first, CHUNK) for a, width in enumerate(widths) for first in range(0, width, CHUNK))


def slots_task(line, j, y, values, out, pre, post_sem, at_y):
    slots = line.slots
    own = slots // 2
    outgoing, pre_send, pre_recv = pre
    post_send, post_recv = post_sem
    width = line.picked.shape[1]
    mine_rows = pl.ds(pl.multiple_of(y * own, 64), own)
    half = out.shape[1] // 2
    outgoing[...] = values(j, 1 - y)
    before = remote(outgoing, line.blocks.at[line.z, mine_rows], pre_send, pre_recv, at_y)
    before.start()
    line.blocks[line.z, mine_rows, :] = values(j, y)
    yield
    before.wait_recv()
    yield from line.run()
    cols = pl.ds(pl.multiple_of(y * half + j * width, 128), width)
    after = remote(line.picked, out.at[:, cols], post_send, post_recv, at_y)
    after.start()
    out[:, cols] = line.picked[...]
    yield
    after.wait_recv()
    before.wait_send()
    after.wait_send()
    line.settle()


def middle_kernel(chunks, padded, *refs):
    first_low, attended, hidden_low, pre_low, second_low, act_low, layer_low, grad, stats, dealt_col = refs[:10]
    outs, layer_out, grad_win, stats_win = refs[10:13], refs[13], refs[14], refs[15]
    rest = refs[16:]
    turned, halo_sem, outgoing, pre_send, pre_recv, post_send, post_recv = (
        rest[0:3],
        rest[3],
        rest[4 : 4 + PERM],
        rest[4 + PERM],
        rest[5 + PERM],
        rest[6 + PERM],
        rest[7 + PERM],
    )
    rest = rest[8 + PERM :]
    line_number = 4 * PERM + 3
    line_refs, reduction_refs = rest[:line_number], rest[line_number:]
    reduction = Reduction(chunks, outs, reduction_refs)
    x, c, y, z = reduction.place
    own, dim = grad.shape
    at_y = {"tp": 1 - y}
    last = 3
    inner = (z == 1) | (z == 2)
    diagonal = {"ctx": jnp.clip(z - 1 + 2 * y, 0, last), "tp": 1 - y}
    has_diagonal = ((y == 0) & (z > 0)) | ((y == 1) & (z < last))
    greet_all(reduction.peers(), ((inner, {"ctx": 3 - z}), (has_diagonal, diagonal)))
    halos = []
    for i, (src, dst) in enumerate(((grad, grad_win), (stats, stats_win))):
        to_y = remote(
            src.at[pl.ds(pl.multiple_of((1 - y) * (own - HALO), 64), HALO)],
            dst.at[pl.ds(pl.multiple_of(y * (HALO + own), 64), HALO)],
            halo_sem.at[i, 0],
            halo_sem.at[i, 1],
            at_y,
        )
        to_diagonal = remote(
            src.at[pl.ds(pl.multiple_of(y * (own - HALO), 64), HALO)],
            dst.at[pl.ds(pl.multiple_of((1 - y) * (HALO + own), 64), HALO)],
            halo_sem.at[i, 2],
            halo_sem.at[i, 3],
            diagonal,
        )
        to_y.start()

        @pl.when(has_diagonal)
        def _():
            to_diagonal.start()

        halos.append((to_y, to_diagonal))
    lines = [line_of(j, PERM, z, dealt_col, True, line_refs) for j in range(PERM)]
    width = dim // 2 // PERM

    def layer_values(j, half):
        return layer_low[:, pl.ds(pl.multiple_of(half * (dim // 2) + j * width, 128), width)]

    factors = ((first_low, attended), (hidden_low, pre_low), (second_low, act_low))

    def produce(k):
        a, first, _ = chunks[k]
        if first == 0:
            turned[a][...] = factors[a][0][...].T
        reduction.product(k, turned[a], factors[a][1], factors[a][1].shape[1] // 2)

    tasks = [(k, reduction.task(k, produce)) for k in range(len(chunks))]
    tasks += [
        (
            2 * j,
            slots_task(
                lines[j],
                j,
                y,
                layer_values,
                layer_out,
                (outgoing[j], pre_send.at[j], pre_recv.at[j]),
                (post_send.at[j], post_recv.at[j]),
                at_y,
            ),
        )
        for j in range(PERM)
    ]
    for src, dst in ((grad, grad_win), (stats, stats_win)):
        dst[HALO : HALO + own, :] = src[...]
        rest_rows = padded - 2 * HALO - own
        dst[2 * HALO + own :, :] = jnp.zeros((rest_rows, dst.shape[1]), dst.dtype)

        @pl.when((y == 0) & (z == 0))
        def _():
            dst[:HALO, :] = jnp.zeros((HALO, dst.shape[1]), dst.dtype)

        @pl.when((y == 1) & (z == last))
        def _():
            dst[HALO + own : 2 * HALO + own, :] = jnp.zeros((HALO, dst.shape[1]), dst.dtype)

    interleave(sorted(tasks, key=lambda item: item[0]))
    for to_y, to_diagonal in halos:
        to_y.wait()

        @pl.when(has_diagonal)
        def _():
            to_diagonal.wait()

    reduction.settle()


def middle_stage(first_low, attended, hidden_low, pre_low, second_low, act_low, layer_low, grad, stats, dealt, padded):
    own, dim = grad.shape
    ctx_size = lax.axis_size("ctx")
    rows = dim // 4
    widths = (attended.shape[1] // 2, pre_low.shape[1] // 2, act_low.shape[1] // 2)
    chunks = chunks_of(widths)
    spec = pl.BlockSpec(memory_space=pltpu.VMEM)
    outs = [jax.ShapeDtypeStruct((rows, width), F32) for width in widths]
    outs += [
        jax.ShapeDtypeStruct((2 * own, dim), BF),
        jax.ShapeDtypeStruct((padded, dim), BF),
        jax.ShapeDtypeStruct((padded, 128), F32),
    ]
    scratch = [pltpu.VMEM((dim, own), BF) for _ in range(3)]
    scratch += [pltpu.SemaphoreType.DMA((2, 4))]
    scratch += [pltpu.VMEM((own, dim // 2 // PERM), BF) for _ in range(PERM)]
    scratch += [pltpu.SemaphoreType.DMA((PERM,)) for _ in range(4)]
    scratch += line_scratch(ctx_size, 2 * own, PERM, dim // 2 // PERM)
    scratch += reduction_scratch(rows, chunks)
    return pl.pallas_call(
        functools.partial(middle_kernel, chunks, padded),
        out_shape=outs,
        in_specs=[spec] * 10,
        out_specs=[spec] * len(outs),
        scratch_shapes=scratch,
        compiler_params=pltpu.CompilerParams(
            collective_id=1, has_side_effects=True, vmem_limit_bytes=VMEM_LIMIT
        ),
        cost_estimate=pl.CostEstimate(flops=20000000000, bytes_accessed=100000000, transcendentals=0),
    )(first_low, attended, hidden_low, pre_low, second_low, act_low, layer_low, grad, stats, dealt[:, None])


def last_kernel(chunks, *refs):
    inputs, qkv_low, weight, grad_first, dealt_col, vector = refs[:6]
    out, tokens_grad, vector_out = refs[6:9]
    rest = refs[9:]
    turned, outgoing, pre_send, pre_recv, post_send, post_recv = (
        rest[0],
        rest[1 : 1 + PERM],
        rest[1 + PERM],
        rest[2 + PERM],
        rest[3 + PERM],
        rest[4 + PERM],
    )
    vector_in, vector_sum, vector_send, vector_recv = rest[5 + PERM : 9 + PERM]
    rest = rest[9 + PERM :]
    line_number = 4 * PERM + 3
    line_refs, reduction_refs = rest[:line_number], rest[line_number:]
    reduction = Reduction(chunks, (out,), reduction_refs)
    x, c, y, z = reduction.place
    own, dim = inputs.shape
    at_y = {"tp": 1 - y}
    inner = (z == 1) | (z == 2)
    peers = reduction.peers()
    greet_all(peers, ((inner, {"ctx": 3 - z}),))
    lines = [line_of(j, PERM, z, dealt_col, True, line_refs) for j in range(PERM)]
    width = dim // 2 // PERM

    def vector_copy(stage):
        return remote(
            vector_sum.at[stage], vector_in.at[stage], vector_send.at[stage], vector_recv.at[stage], peers[stage]
        )

    def vector_task():
        vector_sum[0] = vector[...]
        for stage in range(5):
            vector_copy(stage).start()
            yield
            vector_copy(stage).wait_recv()
            total = vector_sum[stage] + vector_in[stage]
            if stage < 4:
                vector_sum[stage + 1] = total
            else:
                vector_out[...] = total

    def grad_values(j, half):
        first = pl.ds(pl.multiple_of(half * (dim // 2) + j * width, 128), width)
        return (grad_first[:, first] + matmul_second(qkv_low[...], weight[first, :])).astype(BF)

    def produce(k):
        if k == 0:
            turned[...] = inputs[...].T
        reduction.product(k, turned, qkv_low, qkv_low.shape[1] // 2)

    tasks = [
        (
            j,
            slots_task(
                lines[j],
                j,
                y,
                grad_values,
                tokens_grad,
                (outgoing[j], pre_send.at[j], pre_recv.at[j]),
                (post_send.at[j], post_recv.at[j]),
                at_y,
            ),
        )
        for j in range(PERM)
    ]
    tasks += [(k, reduction.task(k, produce)) for k in range(len(chunks))]
    tasks += [(1, vector_task())]
    interleave(sorted(tasks, key=lambda item: item[0]))
    reduction.settle()
    for stage in range(5):
        vector_copy(stage).wait_send()


def last_stage(inputs, qkv_low, weight, grad_first, dealt, vector):
    own, dim = inputs.shape
    ctx_size = lax.axis_size("ctx")
    rows = dim // 4
    width = qkv_low.shape[1] // 2
    chunks = chunks_of((width,))
    spec = pl.BlockSpec(memory_space=pltpu.VMEM)
    outs = [
        jax.ShapeDtypeStruct((rows, width), F32),
        jax.ShapeDtypeStruct((2 * own, dim), BF),
        jax.ShapeDtypeStruct(vector.shape, F32),
    ]
    scratch = [pltpu.VMEM((dim, own), BF)]
    scratch += [pltpu.VMEM((own, dim // 2 // PERM), BF) for _ in range(PERM)]
    scratch += [pltpu.SemaphoreType.DMA((PERM,)) for _ in range(4)]
    scratch += [pltpu.VMEM((5,) + vector.shape, F32), pltpu.VMEM((5,) + vector.shape, F32)]
    scratch += [pltpu.SemaphoreType.DMA((5,)), pltpu.SemaphoreType.DMA((5,))]
    scratch += line_scratch(ctx_size, 2 * own, PERM, dim // 2 // PERM)
    scratch += reduction_scratch(rows, chunks)
    return pl.pallas_call(
        functools.partial(last_kernel, chunks),
        out_shape=outs,
        in_specs=[spec] * 6,
        out_specs=[spec] * len(outs),
        scratch_shapes=scratch,
        compiler_params=pltpu.CompilerParams(
            collective_id=2, has_side_effects=True, vmem_limit_bytes=VMEM_LIMIT
        ),
        cost_estimate=pl.CostEstimate(flops=10000000000, bytes_accessed=100000000, transcendentals=0),
    )(inputs, qkv_low, weight, grad_first, dealt[:, None], vector)


def project_kernel(dim, x_ref, weight, bias, out):
    step = 256
    third = weight.shape[1] // 3

    def body(i, carry):
        lines = pl.ds(pl.multiple_of(i * step, step), step)
        value = (matmul(x_ref[lines, :], weight[...]) + bias[0]).astype(BF)
        scale = jnp.where(lax.broadcasted_iota(jnp.int32, (1, 3 * third), 1) < third, 0.125, 1.0).astype(BF)
        out[lines, :] = value * scale
        return carry

    lax.fori_loop(0, x_ref.shape[0] // step, body, 0)


def project(x_window, weight, bias):
    rows, dim = x_window.shape
    width = 3 * dim // 2
    return pl.pallas_call(
        functools.partial(project_kernel, dim),
        grid=(2,),
        out_shape=jax.ShapeDtypeStruct((rows, 2 * width), BF),
        in_specs=[
            pl.BlockSpec((rows, dim), lambda i: (0, 0)),
            pl.BlockSpec((dim, width), lambda i: (0, i)),
            pl.BlockSpec((1, 1, width), lambda i: (i, 0, 0)),
        ],
        out_specs=pl.BlockSpec((rows, width), lambda i: (0, i)),
        compiler_params=pltpu.CompilerParams(vmem_limit_bytes=VMEM_LIMIT),
        cost_estimate=pl.CostEstimate(flops=6000000000, bytes_accessed=14000000, transcendentals=0),
    )(x_window, weight, bias)


def rows_to_slots(values, dealt, place_z, place_y):
    own, dim = values.shape
    half = dim // 2
    keep = lax.dynamic_slice_in_dim(values, place_y * half, half, axis=1)
    send = lax.dynamic_slice_in_dim(values, (1 - place_y) * half, half, axis=1)
    other = lax.ppermute(send, "tp", [(0, 1), (1, 0)])
    first = jnp.where(place_y == 0, keep, other)
    second = jnp.where(place_y == 0, other, keep)
    block = jnp.concatenate([first, second], axis=0)
    everything = lax.all_gather(block, "ctx", axis=0, tiled=True)
    slots = 2 * own
    mine = lax.dynamic_slice_in_dim(dealt, place_z * slots, slots)
    picked = jnp.take(everything, mine, axis=0, mode="clip")
    other_columns = lax.ppermute(picked, "tp", [(0, 1), (1, 0)])
    return jnp.concatenate(
        [jnp.where(place_y == 0, picked, other_columns), jnp.where(place_y == 0, other_columns, picked)], axis=1
    )


def slots_to_rows(values, dealt, place_z, place_y):
    slots, dim = values.shape
    half, own = dim // 2, slots // 2
    block = lax.dynamic_slice_in_dim(values, place_y * half, half, axis=1)
    everything = lax.all_gather(block, "ctx", axis=0, tiled=True)
    wanted = place_z * slots + lax.broadcasted_iota(jnp.int32, (slots, 1), 0)
    chosen = (wanted == dealt[None, :]).astype(BF)
    picked = matmul(chosen, everything).astype(BF)
    keep = lax.dynamic_slice_in_dim(picked, place_y * own, own, axis=0)
    send = lax.dynamic_slice_in_dim(picked, (1 - place_y) * own, own, axis=0)
    other = lax.ppermute(send, "tp", [(0, 1), (1, 0)])
    return jnp.concatenate([jnp.where(place_y == 0, keep, other), jnp.where(place_y == 0, other, keep)], axis=1)


def per_device(
    tokens,
    cotangent,
    seq_lengths,
    dealing,
    query_weight,
    query_bias,
    key_weight,
    value_weight,
    value_bias,
    output_weight,
    output_bias,
    first_gain,
    first_shift,
    up_weight,
    up_bias,
    down_weight,
    down_bias,
    second_gain,
    second_shift,
):
    rows, dim = tokens.shape
    ctx_size, tp_size = lax.axis_size("ctx"), lax.axis_size("tp")
    group_rows = rows * ctx_size
    own = rows // tp_size
    place_z, place_y = lax.axis_index("ctx"), lax.axis_index("tp")
    window = HALO + own + HALO
    padded = -(-window // BLOCK) * BLOCK
    dealt = dealing[0]

    lengths = seq_lengths[0]
    number = lengths.shape[0]
    upto = jnp.arange(number)[:, None] >= jnp.arange(number)[None, :]
    ends = jnp.sum(jnp.where(upto, lengths[None, :], 0), axis=1)
    starts = ends - lengths
    first_row = place_z * rows + place_y * own
    index = jnp.arange(padded, dtype=jnp.int32)
    position = first_row - HALO + index
    valid = (position >= 0) & (position < group_rows) & (index < window)
    segment = jnp.sum((position[:, None] >= ends[None, :-1]).astype(jnp.int32), axis=1)
    segment = jnp.where(valid, segment, -1)
    seg_row, seg_col = segment[None, :], segment[:, None]
    tile = attention_tile(own)
    tile_first = first_row + tile * jnp.arange(own // tile, dtype=jnp.int32)
    tile_last = tile_first + tile - 1
    begin = jnp.max(jnp.where(starts[None, :] <= tile_first[:, None], starts[None, :], 0), axis=1)
    finish = jnp.min(jnp.where(ends[None, :] > tile_last[:, None], ends[None, :], group_rows), axis=1)
    shift = HALO - first_row
    bounds = jnp.stack([(begin + shift) // BLOCK, (finish + shift + BLOCK - 1) // BLOCK], axis=1).astype(jnp.int32)

    special = lax.axis_size("shard") == 4 and tp_size == 2 and ctx_size == 4
    half_dim = dim // tp_size
    pieces = [
        jnp.concatenate([query_weight, key_weight, value_weight], axis=1),
        output_weight.T,
        up_weight,
        down_weight.T,
    ]
    flat = jnp.concatenate([query_bias, value_bias, up_bias])
    small = jnp.broadcast_to(flat[None, :], (16, flat.shape[0]))
    inputs = lax.dynamic_slice_in_dim(tokens, place_y * own, own, axis=0)
    if special:
        whole, biases, qkv, cot_rows = first_stage(pieces, small, tokens, cotangent, dealt, padded)
        whole_up_bias = biases[::16, dim:].reshape(-1).astype(F32)
    else:
        whole = [
            lax.all_gather(lax.all_gather(piece, "shard", axis=0, tiled=True), "tp", axis=1, tiled=True)
            for piece in pieces
        ]
        biases = lax.all_gather(small, "tp", axis=0, tiled=True)[::16].astype(F32)
        qkv_bias = jnp.concatenate(
            [biases[:, :half_dim], jnp.zeros((tp_size, half_dim), F32), biases[:, half_dim:dim]], axis=1
        )[:, None, :]
        whole_up_bias = biases[:, dim:].reshape(-1)
        edge = jnp.where(place_y == 0, tokens[rows - HALO :], tokens[:HALO])
        hops = [(2 * z, 2 * z + 2) for z in range(ctx_size - 1)] + [(2 * z + 1, 2 * z - 1) for z in range(1, ctx_size)]
        arrived = lax.ppermute(edge, ("ctx", "tp"), hops)
        x_window = jnp.where(
            place_y == 0,
            jnp.concatenate([arrived, tokens[: own + HALO]], axis=0),
            jnp.concatenate([tokens[own - HALO :], arrived], axis=0),
        )
        x_window = jnp.pad(x_window, ((0, padded - window), (0, 0)))
        qkv = project(x_window, whole[0], qkv_bias)
        cot_rows = slots_to_rows(cotangent, dealt, place_z, place_y)
    wide_qkv, wide_output, wide_up, wide_down = whole
    output_bias = output_bias.astype(F32)
    first_gain = first_gain.astype(F32)
    first_shift = first_shift.astype(F32)
    down_bias = down_bias.astype(F32)
    second_gain = second_gain.astype(F32)
    second_shift = second_shift.astype(F32)

    attended, logsum = attention_forward(qkv, seg_col, seg_row, bounds, own, dim)
    grad_out = cot_rows.astype(F32)
    hidden_one, normed_one, inverse_one = norm_forward(
        inputs.astype(F32) + matmul_second(attended, wide_output) + output_bias, first_gain, first_shift
    )
    hidden_low = hidden_one.astype(BF)
    pre_act = matmul(hidden_low, wide_up) + whole_up_bias
    erf_part = 0.5 * (1.0 + jax.scipy.special.erf(pre_act * HALF_ROOT))
    act_low = (pre_act * erf_part).astype(BF)
    layer_value, normed_two, inverse_two = norm_forward(
        hidden_one + matmul_second(act_low, wide_down) + down_bias, second_gain, second_shift
    )
    layer_low = layer_value.astype(BF)

    second_shift_grad = jnp.sum(grad_out, axis=0)
    second_gain_grad = jnp.sum(grad_out * normed_two, axis=0)
    grad_second = norm_backward(grad_out, normed_two, inverse_two, second_gain)
    down_bias_grad = jnp.sum(grad_second, axis=0)
    second_low = grad_second.astype(BF)
    slope = erf_part + pre_act * DENSITY * jnp.exp(-0.5 * pre_act * pre_act)
    grad_pre = matmul(second_low, wide_down) * slope
    up_bias_grad = jnp.sum(grad_pre, axis=0)
    pre_low = grad_pre.astype(BF)
    grad_hidden = grad_second + matmul_second(pre_low, wide_up)
    first_shift_grad = jnp.sum(grad_hidden, axis=0)
    first_gain_grad = jnp.sum(grad_hidden * normed_one, axis=0)
    grad_first = norm_backward(grad_hidden, normed_one, inverse_one, first_gain)
    output_bias_grad = jnp.sum(grad_first, axis=0)
    first_low = grad_first.astype(BF)
    attended_grad = matmul(first_low, wide_output).astype(BF)
    delta = jnp.sum(
        (attended_grad.astype(F32) * attended.astype(F32)).reshape(own, dim // HEAD, HEAD), axis=2
    )
    stats = logsum + jnp.pad(delta, ((0, 0), (16, 112 - dim // HEAD)))
    if special:
        output_own, up_own, down_own, layer_out, grad_win, stats_win = middle_stage(
            first_low, attended, hidden_low, pre_low, second_low, act_low, layer_low, attended_grad, stats, dealt, padded
        )
    else:
        layer_out = rows_to_slots(layer_low, dealt, place_z, place_y)
        up_hops = [(i, i + 1) for i in range(ctx_size * tp_size - 1)]
        down_hops = [(i + 1, i) for i in range(ctx_size * tp_size - 1)]
        grad_win, stats_win = [
            jnp.concatenate(
                [
                    lax.ppermute(array[own - HALO :], ("ctx", "tp"), up_hops),
                    array,
                    lax.ppermute(array[:HALO], ("ctx", "tp"), down_hops),
                    jnp.zeros((padded - window, array.shape[1]), array.dtype),
                ],
                axis=0,
            )
            for array in (attended_grad, stats)
        ]
    query_low, query_bias_grad = attention_query(qkv, seg_col, seg_row, bounds, attended_grad, stats, dim)
    qkv_low, value_bias_grad = attention_key(
        qkv, seg_col, seg_row, bounds, grad_win, stats_win, query_low, own, dim
    )
    vectors = jnp.concatenate(
        [
            query_bias_grad[0],
            value_bias_grad[0],
            up_bias_grad,
            output_bias_grad,
            first_gain_grad,
            first_shift_grad,
            down_bias_grad,
            second_gain_grad,
            second_shift_grad,
        ]
    )
    if special:
        qkv_own, tokens_grad, small_sum = last_stage(
            inputs, qkv_low, wide_qkv, grad_first, dealt, vectors.reshape(-1, 128)
        )
        small_sum = small_sum.reshape(-1)
        owned = [qkv_own, output_own, up_own, down_own]
    else:
        owned = []
        for full in (
            matmul_first(inputs, qkv_low),
            matmul_first(first_low, attended),
            matmul_first(hidden_low, pre_low),
            matmul_first(second_low, act_low),
        ):
            part = lax.psum_scatter(full.astype(BF), "tp", scatter_dimension=1, tiled=True)
            part = lax.psum_scatter(part, "shard", scatter_dimension=0, tiled=True)
            owned.append(lax.psum(part, "ctx").astype(F32))
        small_sum = lax.psum(vectors, ("shard", "ctx", "tp"))
        tokens_grad = (grad_first + matmul_second(qkv_low, wide_qkv)).astype(BF)
        tokens_grad = rows_to_slots(tokens_grad, dealt, place_z, place_y)
    hidden = up_bias_grad.shape[0]
    sizes = [dim, dim, hidden] + [dim] * 6
    offsets = [sum(sizes[:i]) for i in range(len(sizes))]
    parts = [small_sum[o : o + s] for o, s in zip(offsets, sizes)]

    def by_tp(vector):
        part = vector.shape[0] // tp_size
        return lax.dynamic_slice_in_dim(vector, place_y * part, part)

    return (
        layer_out,
        tokens_grad,
        owned[0][:, :half_dim],
        by_tp(parts[0]),
        owned[0][:, half_dim : 2 * half_dim],
        owned[0][:, 2 * half_dim :],
        by_tp(parts[1]),
        owned[1].T,
        parts[3],
        parts[4],
        parts[5],
        owned[2],
        by_tp(parts[2]),
        owned[3].T,
        parts[6],
        parts[7],
        parts[8],
    )


def solution(mesh):
    return jax.shard_map(
        per_device,
        mesh=mesh,
        in_specs=(
            P(("shard", "ctx"), None),
            P(("shard", "ctx"), None),
            P("shard", None),
            P("shard", None),
            P("shard", "tp"),
            P("tp"),
            P("shard", "tp"),
            P("shard", "tp"),
            P("tp"),
            P("tp", "shard"),
            P(),
            P(),
            P(),
            P("shard", "tp"),
            P("tp"),
            P("tp", "shard"),
            P(),
            P(),
            P(),
        ),
        out_specs=(
            P(("shard", "ctx"), None),
            P(("shard", "ctx"), None),
            P("shard", "tp"),
            P("tp"),
            P("shard", "tp"),
            P("shard", "tp"),
            P("tp"),
            P("tp", "shard"),
            P(),
            P(),
            P(),
            P("shard", "tp"),
            P("tp"),
            P("tp", "shard"),
            P(),
            P(),
            P(),
        ),
        check_vma=False,
    )
```

time: 595 us -> 506 us (0.85); the launches traced: 592 us -> 496 us
  Pallas kernels: 373 us -> 431 us
  starting transfers between devices: 42.4 us -> 0 us
  matrix products: 65.7 us -> 26.2 us
  waiting for transfers between devices: 30.4 us -> 0 us
  other arithmetic: 28.9 us -> 13.8 us
  between operations: 15.5 us -> 1.71 us
  local copies, waits for them, and re-layouts: 35.6 us -> 23.8 us
    pallas_call x4 -> x3, Pallas kernels: 307 us -> 358 us  [the longest x1 175 us: middle_stage(): pl.pallas_call(functools.partial(middle_kernel, chunks, padded), out_shap...]
    ppermute x8 -> x0, starting transfers between devices: 42.3 us -> none  [the longest x1 14.3 us: slots_to_rows(): other = lax.ppermute(send, 'tp', [(0, 1), (1, 0)])]
    ppermute x8 -> x0, waiting for transfers between devices: 30.4 us -> none  [the longest x1 24.8 us: rows_to_slots(): other = lax.ppermute(send, 'tp', [(0, 1), (1, 0)])]
    dot_general x4 -> x0, matrix products: 27.6 us -> none  [matmul_first(): lax.dot_general(former, latter, (((0,), (0,)), ((), ())), preferred_eleme...]
    dot_general x4 -> x3, matrix products: 23.9 us -> 13.7 us  [matmul(): return jnp.dot(former, latter, preferred_element_type=F32)]
    concatenate x4 -> x0, other arithmetic: 6.97 us -> none  [the longest x1 4.58 us: per_device(): jnp.concatenate([lax.ppermute(attended_grad[own - HALO:], both, up_hops),...]
    pallas_call x3, Pallas kernels: 66.8 us -> 73.2 us  [vmem_call(): pl.pallas_call(kernel, out_shape=outs, in_specs=[pl.BlockSpec(memory_spac...]
    gather x1 -> x0, local copies, waits for them, and re-layouts: 6.44 us -> none  [rows_to_slots(): picked = jnp.take(everything, mine, axis=0, mode='clip')]
  transfers between devices with their start and end apart: 10 -> 0, of which waited for: 2 -> 0; matrix products, arithmetic and copies ran while one was open for 12% -> 0% of each run, Pallas kernels for 60% -> 0%
where the time goes in v3:
time: 506 us; the launch traced here: 496 us
  Pallas kernels  431 us (85%)
  matrix products  26.2 us (5%)
  local copies, waits for them, and re-layouts  23.8 us (5%)
  other arithmetic  13.8 us (3%)
    pallas_call x1, Pallas kernels, middle_stage(): pl.pallas_call(functools.partial(middle_kernel, chunks, padded), out_shap...  175 us
    pallas_call x1, Pallas kernels, first_stage(): pl.pallas_call(functools.partial(first_kernel, widths, padded), out_shape...  97.8 us
    pallas_call x1, Pallas kernels, last_stage(): pl.pallas_call(functools.partial(last_kernel, chunks), out_shape=outs, in...  84.5 us
    pallas_call x3, Pallas kernels, vmem_call(): pl.pallas_call(kernel, out_shape=outs, in_specs=[pl.BlockSpec(memory_spac...  73.2 us
    dot_general x3, matrix products, matmul(): return jnp.dot(former, latter, preferred_element_type=F32)  13.7 us
    dot_general x3, matrix products, matmul_second(): lax.dot_general(former, latter, (((1,), (1,)), ((), ())), preferred_eleme...  12.5 us
    unnamed x81, local copies, waits for them, and re-layouts  11.5 us

profile of v3, /device:TPU:0, one launch (start us, length us, event | category | flops | bytes accessed | tf_op | source)
XLA Modules:
  0.0 496.4 jit_solution(8516110774697101559)
XLA Ops:
  3.5 1.2 reshape_select_fusion.seg_col
  5.3 1.9 pad_maximum_fusion.refs_0_
  7.8 97.8 %shard_map.314 = (bf16[2,2,192,2304]{3,2,1,0:T(8,128)(2,1)}, bf16[2,2,192,768]{3,2,1,0:T(8,128)(2,1)}, bf16[2,2,192,3072]{3,2,1,0:T(8,128)(2,1)}, bf16[2,2,192,3...) custom-call(bf16[192,1152]{1,0:T(8,128)(2,1)} %pad_maximum_fusion.refs_0_, ...), custom_call_target="tpu_custom_call" | custom-call | flops 10000000000 | bytes 100000000 | tf_op jit(solution)/shard_map/pallas_call | solution.py:655
  105.7 32.4 %shard_map.315 = (bf16[576,768]{1,0:T(8,128)(2,1)}, f32[576,128]{1,0:T(8,128)}) custom-call(s32[3,2]{1,0:T(4,128)} %pad_add_fusion.1.bounds, bf16[1792,2304]{1,0:T(8,128)(2,1)} %get-tuple-element.39.qkv, s32[1792,1]{1,0:T(8,128)} %reshape_select_fusion.seg_col, s32[1,1792]{1,0:T(1,128)} %and_select_fusion.seg_row), custom_call_target="tpu_custom_call" | custom-call | flops 10000000000 | bytes 12000000 | tf_op jit(solution)/shard_map/pallas_call | solution.py:222
  139.5 2.3 fusion.26
  142.9 1.0 slice.70
  143.9 5.7 %multiply_convert_fusion = (bf16[576,3072]{1,0:T(8,128)(2,1)S(1)}, f32[576,3072]{1,0:T(8,128)S(1)}) fusion(f32[3072]{0:T(1024)S(1)} %reshape.313, bf16[576,768]{1,0:T(8,128)(2,1)S(1)} %fusion.11.refs_2_, bf16[768,3072]{1,0:T(8,128)(2,1)} %bitcast.64), kind=kOutput, calls=%fused_computation.5 | convolution fusion | flops 2728525824 | bytes 16232448 | tf_op jit(solution)/shard_map/dot_general | solution.py:22
  149.7 6.8 %fusion.27 = (f32[576]{0:T(1024)S(1)}, f32[576,768]{1,0:T(8,128)S(1)}) fusion(f32[768]{0:T(1024)S(1)} %convert_element_type.75, bf16[576,3072]{1,0:T(8,128)(2,1)S(1)} %get-tuple-element.89.refs_5_, bf16[768,3072]{1,0:T(8,128)(2,1)} %bitcast.68, f32[768]{0:T(1024)S(1)} %convert_element_type.70, f32[576]{0:T(1024)S(1)} %add_rsqrt_fusion.1, ...), kind=kOutput, calls=%fused_computation.103 | convolution fusion | flops 2721005056 | bytes 11812608 | tf_op jit(solution)/shard_map/dot_general | solution.py:30
  157.7 1.8 fusion.10
  160.3 6.1 %fusion.24 = (f32[3072]{0:T(1024)S(1)}, bf16[576,3072]{1,0:T(8,128)(2,1)S(1)}) fusion(f32[576,3072]{1,0:T(8,128)S(1)} %get-tuple-element.90, f32[3072]{0:T(1024)S(1)} %reshape.313, bf16[576,768]{1,0:T(8,128)(2,1)S(1)} %convert_element_type.78.refs_4_, bf16[768,3072]{1,0:T(8,128)(2,1)S(1)} %bitcast.71), kind=kOutput, calls=%fused_computation.100 | convolution fusion | flops 2739139584 | bytes 16244736 | tf_op jit(solution)/shard_map/dot_general | solution.py:22
  166.5 3.5 multiply_reduce_fusion
  170.7 1.7 copy-done.4
  172.8 1.8 convert_multiply_fusion.2
  174.6 1.8 copy.78
  176.4 1.7 reduce_sum.181
  179.1 19.2 %shard_map.317 = (bf16[576,768]{1,0:T(8,128)(2,1)}, f32[1,768]{1,0:T(1,128)}) custom-call(s32[3,2]{1,0:T(4,128)} %pad_add_fusion.1.bounds, bf16[1792,2304]{1,0:T(8,128)(2,1)} %get-tuple-element.39.qkv, s32[1792,1]{1,0:T(8,128)} %reshape_select_fusion.seg_col, s32[1,1792]{1,0:T(1,128)} %and_select_fusion.seg_row, ...), custom_call_target="tpu_custom_call" | custom-call | flops 15000000512 | bytes 12000000 | tf_op jit(solution)/shard_map/pallas_call | solution.py:222
  198.3 2.1 copy.80.refs_9_.refs_4_
  200.5 175.3 %shard_map.316 = (f32[192,384]{1,0:T(8,128)}, f32[192,1536]{1,0:T(8,128)}, f32[192,1536]{1,0:T(8,128)}, bf16[1152,768]{1,0:T(8,128)(2,1)}, bf16[1792,768]{1,0:T(8,128)(2,1)}, /*index=5*/f32[1792,128]{1,0:T(8,128)}) custom-call(bf16[576,768]{1,0:T(8,128)(2,1)} %copy-done.1, bf16[576,768]{1,0:T(8,128)(2,1)} %get-tuple-element.40.refs_1_, ...), custom_call_target="tpu_custom_call" | custom-call | flops 20000000000 | bytes 100000000 | tf_op jit(solution)/shard_map/pallas_call | solution.py:969
  375.8 21.7 %shard_map.318 = (bf16[576,2304]{1,0:T(8,128)(2,1)}, f32[1,768]{1,0:T(1,128)}) custom-call(s32[3,2]{1,0:T(4,128)} %pad_add_fusion.1.bounds, bf16[1792,2304]{1,0:T(8,128)(2,1)} %get-tuple-element.39.qkv, s32[1792,1]{1,0:T(8,128)} %reshape_select_fusion.seg_col, s32[1,1792]{1,0:T(1,128)} %and_select_fusion.seg_row, bf16[1792,768]{1,0:T(8,128)(2,1)} %get-tuple-element.48.grad, ...), custom_call_target="tpu_custom_call" | custom-call | flops 20000000000 | bytes 12000000 | tf_op jit(solution)/shard_map/pallas_call | solution.py:222
  399.0 84.5 %shard_map.319 = (f32[192,1152]{1,0:T(8,128)}, bf16[1152,768]{1,0:T(8,128)(2,1)}, f32[72,128]{1,0:T(8,128)}) custom-call(bf16[576,768]{1,0:T(8,128)(2,1)} %copy-done.10, bf16[576,2304]{1,0:T(8,128)(2,1)} %get-tuple-element.51.refs_1_, bf16[768,2304]{1,0:T(8,128)(2,1)} %bitcast.72, f32[576,768]{1,0:T(8,128)} %copy-done, s32[4608,1]{1,0:T(8,128)} %copy.80.refs_9_.refs_4_, ...), custom_call_target="tpu_custom_call" | custom-call | flops 10000000000 | bytes 100000000 | tf_op jit(solution)/shard_map/pallas_call | solution.py:1077
  483.5 2.2 fusion.25
  485.7 1.4 slice_bitcast_fusion.1
  489.8 1.2 copy.96
  491.9 1.2 copy.97
  (130 shorter events, 18.4 us)
Async XLA Ops:
  0.7 6.5 %copy-start.26 = (bf16[384]{0:T(512)(128)(2,1)S(1)}, bf16[384]{0:T(512)(128)(2,1)}, u32[]{:S(2)}) copy-start(bf16[384]{0:T(512)(128)(2,1)} %param.24) | copy-start | bytes 2308
  0.7 6.5 %copy-start.25 = (bf16[384]{0:T(512)(128)(2,1)S(1)}, bf16[384]{0:T(512)(128)(2,1)}, u32[]{:S(2)}) copy-start(bf16[384]{0:T(512)(128)(2,1)} %param.27) | copy-start | bytes 2308
  0.7 6.5 %copy-start.17 = (bf16[1536]{0:T(1024)(128)(2,1)S(1)}, bf16[1536]{0:T(1024)(128)(2,1)}, u32[]{:S(2)}) copy-start(bf16[1536]{0:T(1024)(128)(2,1)} %param.33) | copy-start | bytes 9220
  105.7 32.4 %copy-start.13 = (bf16[1152,768]{1,0:T(8,128)(2,1)S(1)}, bf16[1152,768]{1,0:T(8,128)(2,1)}, u32[]{:S(2)}) copy-start(bf16[1152,768]{1,0:T(8,128)(2,1)} %refs_5_.1) | copy-start | bytes 5308420
  138.1 3.7 copy-start.10
  142.9 6.8 %copy-start.11 = (bf16[576,768]{1,0:T(8,128)(2,1)}, bf16[576,768]{1,0:T(8,128)(2,1)S(1)}, u32[]{:S(2)}) copy-start(bf16[576,768]{1,0:T(8,128)(2,1)S(1)} %fusion.11.refs_2_) | copy-start | bytes 2654212
  143.9 5.8 %copy-start.22 = (bf16[768]{0:T(1024)(128)(2,1)S(1)}, bf16[768]{0:T(1024)(128)(2,1)}, u32[]{:S(2)}) copy-start(bf16[768]{0:T(1024)(128)(2,1)} %param.35) | copy-start | bytes 4612
  143.9 16.3 %slice-start.2 = ((s8[4718592]{0:T(1024)(128)(4,1)}), s8[4194304]{0:T(1024)(128)(4,1)S(1)}, s32[]{:S(2)}) async-start(s8[4718592]{0:T(1024)(128)(4,1)} %bitcast.69), calls=%async_computation.2 | async-start | bytes 8388608
  149.7 6.8 %copy-start.28 = (bf16[576,3072]{1,0:T(8,128)(2,1)}, bf16[576,3072]{1,0:T(8,128)(2,1)S(1)}, u32[]{:S(2)}) copy-start(bf16[576,3072]{1,0:T(8,128)(2,1)S(1)} %get-tuple-element.89.refs_5_) | copy-start | bytes 10616836
  149.7 10.6 %slice-start.3 = ((s8[4718592]{0:T(1024)(128)(4,1)}), s8[524288]{0:T(1024)(128)(4,1)S(1)}, s32[]{:S(2)}) async-start(s8[4718592]{0:T(1024)(128)(4,1)} %bitcast.69), calls=%async_computation.3 | async-start | bytes 1048576
  160.1 6.3 %slice-start = ((s8[4718592]{0:T(1024)(128)(4,1)}), s8[4194304]{0:T(1024)(128)(4,1)S(1)}, s32[]{:S(2)}) async-start(s8[4718592]{0:T(1024)(128)(4,1)} %bitcast.65), calls=%async_computation | async-start | bytes 8388608
  160.2 6.2 %copy-start.12 = (bf16[576,768]{1,0:T(8,128)(2,1)}, bf16[576,768]{1,0:T(8,128)(2,1)S(1)}, u32[]{:S(2)}) copy-start(bf16[576,768]{1,0:T(8,128)(2,1)S(1)} %convert_element_type.78.refs_4_) | copy-start | bytes 2654212
  160.3 6.2 %slice-start.1 = ((s8[4718592]{0:T(1024)(128)(4,1)}), s8[524288]{0:T(1024)(128)(4,1)S(1)}, s32[]{:S(2)}) async-start(s8[4718592]{0:T(1024)(128)(4,1)} %bitcast.65), calls=%async_computation.1 | async-start | bytes 1048576
  166.5 3.5 copy-start.29
  170.6 4.0 copy-start
  170.6 2.2 copy-start.7
  172.8 1.8 copy-start.1
  176.4 1.9 copy-start.14
  179.1 19.2 %copy-start.16 = (s32[1,4608]{1,0:T(1,128)S(1)}, s32[1,4608]{1,0:T(1,128)}, u32[]{:S(2)}) copy-start(s32[1,4608]{1,0:T(1,128)} %refs_7_.1) | copy-start | bytes 55300
  375.8 22.4 %copy-start.18 = (f32[1,768]{1,0:T(1,128)S(1)}, f32[1,768]{1,0:T(1,128)}, u32[]{:S(2)}) copy-start(f32[1,768]{1,0:T(1,128)} %get-tuple-element.53) | copy-start | bytes 9220
  483.5 6.3 %copy-start.5 = (bf16[1152,768]{1,0:T(8,128)(2,1)S(1)}, bf16[1152,768]{1,0:T(8,128)(2,1)}, u32[]{:S(2)}) copy-start(bf16[1152,768]{1,0:T(8,128)(2,1)} %get-tuple-element.116) | copy-start | bytes 5308420
  489.8 2.1 copy-start.6
  491.9 2.0 copy-start.9
  493.1 1.8 copy-start.8
  (10 other events, 9.7 us)
